TPU v7x, 32 devices: a whole 2x2x4 slice. The times are simulated.
32 devices in a mesh: row: 8 (over z, x), col: 4 (over y, core).
Axes of the slice: x: 2, y: 2, z: 4, core: 2. Of those that a mesh axis runs over, the one named last changes fastest.
Arguments:
- sources: float32 [128, 16384], P('col', 'row'), may hold values from -6 to 6
- tiles: bfloat16 [8, 4, 48, 256, 256], P('row', 'col')
- tile_row: int32 [8, 4, 48], P('row', 'col'), may hold values from 0 to 7
- tile_col: int32 [8, 4, 48], P('row', 'col'), may hold values from 0 to 15
- tile_count: int32 [8, 4], P('row', 'col'), may hold values from 1 to 48, as said below
Outputs:
- potential: float32 [128, 16384], P('col', 'row')
Inputs may be any that keep to these rules, and one draw needn't show every extreme that they name: `tile_count`: slots at or past a device's count hold no part of the operator; some device holds exactly 48 live slots; tile pairs may repeat and then add.
All inputs are finite; a program needn't handle non-finite values.
Results may differ from a plain program's by a relative error of at most 0.0029.
Values may be sent and summed in bfloat16 or wider, within the bound.
No kernel may reach another device: no remote copies, remote signals or barrier semaphores. Data moves between devices by JAX's collectives and lax.ppermute only.
A program may use at most 128 MiB of HBM per device.

v0:
```python
import functools
import math

import jax
import jax.numpy as jnp
from jax import lax
from jax.experimental import pallas as pl
from jax.experimental.pallas import tpu as pltpu
from jax.sharding import PartitionSpec as P

ROOT_HALF = 1.0 / math.sqrt(2.0)
SIDE_ROWS = 16
FIRST_ROWS = 16
CHUNKS = 2
UNROLL = 4
FETCHES = 6
MIB = 2**20


def haar_parts(extent, transposed):
    k = lax.broadcasted_iota(jnp.int32, (extent, extent), 1 if transposed else 0)
    n = lax.broadcasted_iota(jnp.int32, (extent, extent), 0 if transposed else 1)
    stride = jnp.where(n == 0, extent, n & -n)
    signs = jnp.where((k ^ n) < 2 * stride, jnp.where((k & stride) == 0, 1.0, -1.0), 0.0)
    n = lax.broadcasted_iota(jnp.int32, (1, extent), 1)
    scale = jnp.full((1, extent), 1.0 / math.sqrt(extent), jnp.float32)
    level = 1
    while level < extent:
        scale = jnp.where((n & -n) == level, 1.0 / math.sqrt(2 * level), scale)
        level *= 2
    return signs.astype(jnp.bfloat16), scale


def three_terms(value):
    high = value.astype(jnp.bfloat16)
    rest = value - high.astype(jnp.float32)
    middle = rest.astype(jnp.bfloat16)
    low = (rest - middle.astype(jnp.float32)).astype(jnp.bfloat16)
    return high, middle, low


def exact_dot(value, signs):
    return sum(jnp.dot(term, signs, preferred_element_type=jnp.float32) for term in three_terms(value))


def block_forward(columns):
    columns = list(columns)
    stride = 1
    while stride < len(columns):
        for p in range(0, len(columns), 2 * stride):
            u, v = columns[p], columns[p + stride]
            columns[p], columns[p + stride] = (u + v) * ROOT_HALF, (u - v) * ROOT_HALF
        stride *= 2
    return columns


def block_inverse(columns):
    columns = list(columns)
    stride = len(columns) // 2
    while stride >= 1:
        for p in range(0, len(columns), 2 * stride):
            u, v = columns[p], columns[p + stride]
            columns[p], columns[p + stride] = (u + v) * ROOT_HALF, (u - v) * ROOT_HALF
        stride //= 2
    return columns


def packed_place(core, span, x, z):
    return (core + 2 * span + 256 * x + 65536 * z).astype(jnp.int32).reshape(1)


def chunk_of(block, blocks):
    lead = blocks - blocks // 4
    return (0, block) if block < lead else (1, block - lead)


def core_of(place_ref):
    return place_ref[0] & 1


def span_of(place_ref):
    return (place_ref[0] >> 1) & 127


def x_of(place_ref):
    return (place_ref[0] >> 8) & 255


def source_span(place_ref, m, spans):
    return lax.rem((place_ref[0] >> 16) - m + spans * 256, spans)


def front_kernel(place_ref, sources_ref, other_ref, lead_ref, body_ref, first_ref, mine_ref, sem, *, blocks, extent):
    copy = pltpu.make_async_copy(sources_ref, mine_ref, sem)
    copy.start()
    height = mine_ref.shape[0]
    pair = 2 * height
    signs, scale = haar_parts(extent, False)
    copy.wait()
    mine, other = mine_ref[...], other_ref[...]
    first_core = core_of(place_ref) == 0
    both = jnp.concatenate([jnp.where(first_core, mine, other), jnp.where(first_core, other, mine)], axis=0)
    parts = [both[:, b * extent : (b + 1) * extent] for b in range(blocks)]
    coef = exact_dot(jnp.concatenate(parts, axis=0), signs) * scale
    columns = block_forward([coef[b * pair : (b + 1) * pair, 0:1] for b in range(blocks)])
    lane = lax.broadcasted_iota(jnp.int32, (pair, extent), 1)
    for b in range(blocks):
        column = jnp.zeros_like(columns[0]) if b == 0 else columns[b]
        block = jnp.where(lane == 0, column, coef[b * pair : (b + 1) * pair, :])
        chunk, at = chunk_of(b, blocks)
        (lead_ref, body_ref)[chunk][at * pair : (at + 1) * pair, :] = block.astype(jnp.bfloat16)
    total = functools.reduce(jnp.add, parts)
    ones = jnp.ones((FIRST_ROWS, extent), jnp.bfloat16)
    first = sum(
        lax.dot_general(ones, term, (((1,), (1,)), ((), ())), preferred_element_type=jnp.float32)
        for term in three_terms(total)
    )
    first_ref[...] = jnp.zeros_like(first_ref)
    first_ref[:, 0:pair] = first * (1.0 / math.sqrt(blocks * extent))


def edge_kernel(
    place_ref,
    rows_ref,
    cols_ref,
    count_ref,
    tiles_ref,
    first_ref,
    _,
    first_cols_ref,
    edge_ref,
    order_ref,
    sizes_ref,
    held_ref,
    sems,
    *,
    blocks,
    owners,
):
    slots, extent = tiles_ref.shape[0], tiles_ref.shape[-1]
    count = count_ref[0]
    x = x_of(place_ref)
    size = slots // FETCHES
    fetches = [
        pltpu.make_async_copy(tiles_ref.at[pl.ds(i * size, size)], held_ref.at[pl.ds(i * size, size)], sems.at[i])
        for i in range(FETCHES)
    ]
    for fetch in fetches:
        fetch.start()
    first_cols_ref[...] = jnp.zeros_like(first_cols_ref)
    edge_ref[...] = jnp.zeros_like(edge_ref)
    edge_ref[owners * blocks : owners * blocks + 8, :] = first_ref[0:8, :]
    pick = (lax.broadcasted_iota(jnp.int32, (SIDE_ROWS, extent), 1) == 0).astype(jnp.bfloat16)

    def visit(slot, sizes):
        row, col = rows_ref[slot], cols_ref[slot]
        owner, block = col // blocks, lax.rem(col, blocks)
        behind = lax.rem(x - owner + owners, owners)
        own = (behind == 0).astype(jnp.int32)
        side = jnp.where(behind == 0, block, (behind - 1) * blocks + block)
        order_ref[1 - own, jnp.where(own == 1, sizes[0], sizes[1])] = (slot << 16) + (side << 8) + row
        return sizes[0] + own, sizes[1] + 1 - own

    sizes = lax.fori_loop(0, count, visit, (jnp.int32(0), jnp.int32(0)))
    for which in range(2):
        sizes_ref[which] = sizes[which]
        for k in range(UNROLL - 1):
            order_ref[which, sizes[which] + k] = blocks

    def add(slot, _):
        row, col = rows_ref[slot], cols_ref[slot]

        @pl.when(lax.rem(col, blocks) == 0)
        def _():
            first_cols_ref[pl.ds(col + row, 1), :] += held_ref[slot, 0:SIDE_ROWS, :].astype(jnp.float32)[0:1, :]

        @pl.when(row == 0)
        def _():
            column = lax.dot_general(
                pick, held_ref[slot], (((1,), (1,)), ((), ())), preferred_element_type=jnp.float32
            )
            edge_ref[pl.ds(col, 1), :] += column[0:1, :]

        return 0

    for i, fetch in enumerate(fetches):
        fetch.wait()
        lax.fori_loop(jnp.minimum(count, i * size), jnp.minimum(count, (i + 1) * size), add, 0)


def seal_kernel(place_ref, body_ref, *refs, blocks, owners):
    edges, (out_ref, line_ref, rest_ref) = refs[:owners], refs[owners:]
    x = x_of(place_ref)
    by_x = []
    for i in range(owners):
        value = edges[0][...]
        for j in range(1, owners):
            value = jnp.where(lax.rem(x - i + owners, owners) == j, edges[j][...], value)
        by_x.append(value)
    length = owners * blocks
    line_ref[...] = by_x[0][0:length, :]
    for i in range(1, owners):
        rest_ref[i - 1] = by_x[i][0:length, :]
    firsts = block_forward([value[length : length + 1, :] for value in by_x])
    row = lax.broadcasted_iota(jnp.int32, (SIDE_ROWS, body_ref.shape[1]), 0)
    side = jnp.zeros(row.shape, jnp.float32)
    for i, first in enumerate(firsts):
        for k, term in enumerate(three_terms(first)):
            side = jnp.where(row == 3 * i + k, term.astype(jnp.float32), side)
    rows = body_ref.shape[0]
    out_ref[0:rows, :] = body_ref[...]
    out_ref[rows:, :] = side.astype(jnp.bfloat16)


def firsts_kernel(place_ref, *refs, owners, spans, pair):
    messages, out_ref = refs[:spans], refs[-1]
    total = jnp.zeros(out_ref.shape, jnp.float32)
    row = lax.broadcasted_iota(jnp.int32, out_ref.shape, 0)
    lane = lax.broadcasted_iota(jnp.int32, out_ref.shape, 1)
    for m, message in enumerate(messages):
        side = message[message.shape[0] - SIDE_ROWS :, :].astype(jnp.float32)
        copies = jnp.concatenate([side[:, 0:pair]] * spans, axis=1)
        at = source_span(place_ref, m, spans) * pair
        for i in range(owners):
            value = copies[3 * i : 3 * i + 1, :] + copies[3 * i + 1 : 3 * i + 2, :] + copies[3 * i + 2 : 3 * i + 3, :]
            total = jnp.where((row == i) & (lane >= at) & (lane < at + pair), value, total)
    out_ref[...] = total


def fill_sides(sides, messages, place_ref, blocks, spans):
    pair = sides.shape[1] // spans
    for index in range(len(messages) // CHUNKS):
        behind, m = index // spans, index % spans
        rows = pl.ds(pl.multiple_of(source_span(place_ref, m, spans) * pair, pair), pair)
        for b in range(blocks):
            chunk, at = chunk_of(b, blocks)
            sides[behind * blocks + b, rows, :] = messages[index * CHUNKS + chunk][at * pair : (at + 1) * pair, :]


def add_products(order_ref, sizes_ref, which, tiles_ref, sides, acc):
    def group(index, _):
        for k in range(UNROLL):
            entry = order_ref[which, index * UNROLL + k]
            slot, side, row = entry >> 16, (entry >> 8) & 255, entry & 255
            acc[row] += jnp.dot(sides[side], tiles_ref[slot], preferred_element_type=jnp.float32)
        return 0

    lax.fori_loop(0, (sizes_ref[which] + UNROLL - 1) // UNROLL, group, 0)


def near_kernel(place_ref, order_ref, sizes_ref, tiles_ref, *refs, blocks, spans):
    *messages, acc_ref, sides = refs
    fill_sides(sides, messages, place_ref, blocks, spans)
    acc_ref[...] = jnp.zeros_like(acc_ref)
    add_products(order_ref, sizes_ref, 0, tiles_ref, sides, acc_ref)


def far_kernel(
    place_ref, order_ref, sizes_ref, tiles_ref, near_ref, firsts_ref, cols_ref, row_ref, *refs, blocks, owners, spans
):
    direct, swapped = refs[: spans * CHUNKS], refs[spans * CHUNKS : owners * spans * CHUNKS]
    keep_ref, send_ref, sides, acc = refs[owners * spans * CHUNKS :]
    extent = tiles_ref.shape[-1]
    pair = sides.shape[1] // spans
    height = pair // 2
    x = x_of(place_ref)
    fill_sides(sides, swapped, place_ref, blocks, spans)
    messages = (*direct, *swapped)
    columns = jnp.transpose(firsts_ref[...])
    for i in range(blocks):
        total = near_ref[i]
        for owner in range(owners):
            total += columns[:, owner : owner + 1] * cols_ref[owner * blocks + i : owner * blocks + i + 1, :]
        acc[i] = total
    add_products(order_ref, sizes_ref, 1, tiles_ref, sides, acc)

    top = jnp.zeros((spans * pair, 1), jnp.float32)
    for owner in range(owners):
        top += columns[:, owner : owner + 1] * row_ref[owner * blocks : owner * blocks + 1, 0:1]
    lane = lax.broadcasted_iota(jnp.int32, (spans * pair, extent), 1)
    acc[0] = jnp.where(lane == 0, top, acc[0])
    lane = lane[0:pair]
    for m in range(spans):
        rows = pl.ds(pl.multiple_of(source_span(place_ref, m, spans) * pair, pair), pair)
        total = jnp.zeros((pair, extent), jnp.float32)
        for behind in range(owners):
            owner = lax.rem(x - behind + owners, owners)
            for b in range(blocks):
                chunk, at = chunk_of(b, blocks)
                message = messages[(behind * spans + m) * CHUNKS + chunk]
                line = row_ref[pl.ds(owner * blocks + b, 1), :]
                total += message[at * pair : (at + 1) * pair, :].astype(jnp.float32) * line
        part = jnp.sum(total, axis=1, keepdims=True)
        acc[0, rows, :] = acc[0, rows, :] + jnp.where(lane == 0, part, 0.0)
    first_core = core_of(place_ref) == 0
    for i in range(blocks):
        value = acc[i]
        for y in range(spans):
            one = value[y * pair : y * pair + height, :]
            two = value[y * pair + height : (y + 1) * pair, :]
            keep_ref[y, i] = jnp.where(first_core, one, two)
            send_ref[y, i] = jnp.where(first_core, two, one)


def combine_kernel(place_ref, keep_ref, arrived_ref, own_ref, *out_refs):
    spans = keep_ref.shape[0]
    span = span_of(place_ref)
    own_ref[...] = keep_ref[span] + arrived_ref[span]
    for j, out_ref in enumerate(out_refs, 1):
        at = lax.rem(span + j, spans)
        out_ref[...] = (keep_ref[at] + arrived_ref[at]).astype(jnp.bfloat16)


def back_kernel(own_ref, *refs):
    *arrived, out_ref = refs
    blocks, height, extent = own_ref.shape
    total = own_ref[...]
    for part in arrived:
        total = total + part[...].astype(jnp.float32)
    columns = block_inverse([total[b][:, 0:1] for b in range(blocks)])
    lane = lax.broadcasted_iota(jnp.int32, (height, extent), 1)
    fixed = jnp.concatenate([jnp.where(lane == 0, columns[b], total[b]) for b in range(blocks)], axis=0)
    signs, scale = haar_parts(extent, True)
    result = exact_dot(fixed * scale, signs)
    for b in range(blocks):
        out_ref[:, b * extent : (b + 1) * extent] = result[b * height : (b + 1) * height, :]


def butterfly(value, partner, index, bit):
    active = index % 2**bit == 0
    upper = index // 2**bit % 2 == 1
    combined = jnp.where(upper, partner - value, partner + value) * ROOT_HALF
    return jnp.where(active, combined, value)


def local(sources, tiles, tile_row, tile_col, tile_count):
    n_row, n_col = lax.axis_size("row"), lax.axis_size("col")
    owners = n_row // n_col
    spans = n_col // 2
    extent = tiles.shape[-1]
    slots = tiles.shape[2]
    height = sources.shape[0]
    blocks = sources.shape[1] // extent
    pair = 2 * height
    last = blocks // 4
    row_index, col_index = lax.axis_index("row"), lax.axis_index("col")
    z, x = row_index // owners, row_index % owners
    span, core = col_index // 2, col_index % 2

    def moved(value, to):
        pairs = []
        for a in range(n_row):
            for b in range(n_col):
                zz, xx, yy, cc = to(a // owners, a % owners, b // 2, b % 2)
                pairs.append((a * n_col + b, (zz * owners + xx) * n_col + yy * 2 + cc))
        return lax.ppermute(value, ("row", "col"), pairs)

    def other_core(value):
        return moved(value, lambda zz, xx, yy, cc: (zz, xx, yy, 1 - cc))

    def along_x(value, j):
        return moved(value, lambda zz, xx, yy, cc: (zz, (xx + j) % owners, yy, cc))

    smem = pl.BlockSpec(memory_space=pltpu.SMEM)
    vmem = pl.BlockSpec(memory_space=pltpu.VMEM)
    hbm = pl.BlockSpec(memory_space=pltpu.HBM)
    unread = pl.BlockSpec(memory_space=pl.ANY)

    def call(kernel, name, out_shape, in_specs, out_specs, limit=16, scratch=(), flops=0, moved_bytes=MIB, **sizes):
        return pl.pallas_call(
            functools.partial(kernel, **sizes) if sizes else kernel,
            out_shape=out_shape,
            in_specs=in_specs,
            out_specs=out_specs,
            scratch_shapes=scratch,
            name=name,
            compiler_params=pltpu.CompilerParams(vmem_limit_bytes=int(limit * MIB)),
            cost_estimate=pl.CostEstimate(flops=flops, bytes_accessed=moved_bytes, transcendentals=0),
        )

    def in_hbm(value):
        return pltpu.with_memory_space_constraint(value, pltpu.HBM)

    def f32(*dims):
        return jax.ShapeDtypeStruct(dims, jnp.float32)

    def bf16(*dims):
        return jax.ShapeDtypeStruct(dims, jnp.bfloat16)

    place = packed_place(core, span, x, z)

    def after(value, *others):
        return lax.optimization_barrier((value, *others))[0]

    length = owners * blocks
    lead, body, first = call(
        front_kernel,
        "front",
        [bf16((blocks - last) * pair, extent), bf16(last * pair, extent), f32(FIRST_ROWS, extent)],
        [smem, hbm, vmem],
        [vmem] * 3,
        scratch=[pltpu.VMEM(sources.shape, jnp.float32), pltpu.SemaphoreType.DMA],
        blocks=blocks,
        extent=extent,
    )(place, in_hbm(sources), other_core(sources))

    def spread(message):
        return [
            moved(message, lambda zz, xx, yy, cc, m=m: (cc * spans + (yy + m) % spans, xx, zz // 2, zz % 2))
            for m in range(spans)
        ]

    direct_lead = spread(lead)
    stack = tiles.reshape(slots, extent, extent)
    first_cols, edge, order, sizes, held = call(
        edge_kernel,
        "edges",
        [
            f32(length, extent),
            f32(length + 8, extent),
            pltpu.SMEM((2, slots + UNROLL), jnp.int32),
            pltpu.SMEM((2,), jnp.int32),
            pltpu.VMEM((slots, extent, extent), jnp.bfloat16),
        ],
        [smem] * 4 + [hbm, vmem, unread],
        [vmem] * 2 + [smem] * 2 + [vmem],
        scratch=[pltpu.SemaphoreType.DMA((FETCHES,))],
        blocks=blocks,
        owners=owners,
    )(
        place,
        in_hbm(tile_row.reshape(-1)),
        in_hbm(tile_col.reshape(-1)),
        tile_count.reshape(1),
        in_hbm(stack),
        first,
        direct_lead[0],
    )
    message, line, rest = call(
        seal_kernel,
        "seal",
        [bf16(last * pair + SIDE_ROWS, extent), f32(length, extent), f32(owners - 1, length, extent)],
        [smem] + [vmem] * (1 + owners),
        [vmem] * 3,
        blocks=blocks,
        owners=owners,
    )(place, body, edge, *[along_x(edge, j) for j in range(1, owners)])
    direct_last = spread(message)
    direct = [piece for m in range(spans) for piece in (direct_lead[m], direct_last[m])]
    swapped = [along_x(piece, j) for j in range(1, owners) for piece in direct]

    firsts = call(
        firsts_kernel,
        "firsts",
        f32(FIRST_ROWS, spans * pair),
        [smem] + [vmem] * spans + [unread] * spans,
        vmem,
        owners=owners,
        spans=spans,
        pair=pair,
    )(place, *direct_last, *swapped[0 : CHUNKS * spans : CHUNKS])
    top_row = (jnp.arange(FIRST_ROWS) == 0)[:, None]
    for bit in range(n_col.bit_length() - 1):
        pairs = [(source, source ^ 2**bit) for source in range(n_col)]
        partner = lax.ppermute(firsts, "col", pairs)
        firsts = jnp.where(top_row, butterfly(firsts, partner, col_index, bit), firsts)

    for bit in reversed(range((n_row // owners).bit_length() - 1)):
        partner = moved(line, lambda zz, xx, yy, cc, bit=bit: (zz ^ 2**bit, xx, yy, cc))
        line = after(butterfly(line, partner, z, bit), *direct_last)
    by_x = block_inverse([line] + [rest[i] for i in range(owners - 1)])
    first_row = by_x[0]
    for i in range(1, owners):
        first_row = jnp.where(x == i, by_x[i], first_row)

    every = (spans * pair, extent)
    near = call(
        near_kernel,
        "near",
        f32(blocks + 1, *every),
        [smem] * 3 + [vmem] * (1 + len(direct)),
        vmem,
        scratch=[pltpu.VMEM((blocks, *every), jnp.bfloat16)],
        blocks=blocks,
        spans=spans,
    )(place, order, sizes, held, *direct)

    shape = (spans, blocks, height, extent)
    keep, send = call(
        far_kernel,
        "far",
        [f32(*shape)] * 2,
        [smem] * 3 + [vmem] * (5 + len(direct) + len(swapped)),
        [vmem] * 2,
        limit=24,
        scratch=[
            pltpu.VMEM(((owners - 1) * blocks, *every), jnp.bfloat16),
            pltpu.VMEM((blocks + 1, *every), jnp.float32),
        ],
        blocks=blocks,
        owners=owners,
        spans=spans,
    )(place, order, sizes, held, near, firsts, first_cols, first_row, *direct, *swapped)

    own, *outgoing = call(
        combine_kernel,
        "combine",
        [f32(*shape[1:])] + [bf16(*shape[1:])] * (spans - 1),
        [smem, vmem, vmem],
        [vmem] * spans,
    )(place, keep, other_core(send))
    arrived = [
        moved(value, lambda zz, xx, yy, cc, j=j: (zz, xx, (yy + j) % spans, cc)) for j, value in enumerate(outgoing, 1)
    ]
    return call(back_kernel, "back", f32(*sources.shape), [vmem] * spans, vmem)(own, *arrived)


def solution(mesh):
    return jax.shard_map(
        local,
        mesh=mesh,
        in_specs=(
            P("col", "row"),
            P("row", "col", None, None, None),
            P("row", "col", None),
            P("row", "col", None),
            P("row", "col"),
        ),
        out_specs=P("col", "row"),
        check_vma=False,
    )
```

profile of v0, /device:TPU:0, one launch (start us, length us, event | category | flops | bytes accessed | tf_op | source)
XLA Modules:
  0.0 60.2 jit_solution(16795624324149921262)
XLA Ops:
  0.5 1.4 %collective-permute-done.other_ref = f32[32,2048]{1,0:T(8,128)S(1)} collective-permute-done((f32[32,2048]{1,0:T(8,128)}, f32[32,2048]{1,0:T(8,128)S(1)}, u32[]{:S(2)}, u32[]{:S(2)}) %collective-permute-start) | collective-permute-done | bytes 262176 | tf_op jit(solution)/shard_map/ppermute | solution.py:356
  1.8 1.4 %front.1 = (bf16[384,256]{1,0:T(8,128)(2,1)S(1)}, bf16[128,256]{1,0:T(8,128)(2,1)S(1)}, f32[16,256]{1,0:T(8,128)S(1)}) custom-call(s32[1]{0:T(128)} %bitcast.place_ref, f32[32,2048]{1,0:T(8,128)} %sources_ref.1, f32[32,2048]{1,0:T(8,128)S(1)} %collective-permute-done.other_ref), custom_call_target="tpu_custom_call" | custom-call | bytes 1048576 | tf_op jit(solution)/shard_map/front/pallas_call | solution.py:396
  3.3 0.7 %collective-permute-start.1 = (bf16[384,256]{1,0:T(8,128)(2,1)S(1)}, bf16[384,256]{1,0:T(8,128)(2,1)S(1)}, u32[]{:S(2)}, u32[]{:S(2)}) collective-permute-start(bf16[384,256]{1,0:T(8,128)(2,1)S(1)} %get-tuple-element.23), channel_id=1, source_target_pairs={{0,0},{1,16},{2,8},{3,24},{4,4},{5,20},{6,12},{7,28},{8,1},{9,17},... | collective-permute-start | bytes 589832 | tf_op jit(solution)/shard_map/ppermute | solution.py:356
  4.0 4.2 %collective-permute-start.4 = (bf16[384,256]{1,0:T(8,128)(2,1)S(1)}, bf16[384,256]{1,0:T(8,128)(2,1)S(1)}, u32[]{:S(2)}, u32[]{:S(2)}) collective-permute-start(bf16[384,256]{1,0:T(8,128)(2,1)S(1)} %get-tuple-element.23), channel_id=1, source_target_pairs={{0,8},{1,24},{2,0},{3,16},{4,12},{5,28},{6,4},{7,20},{8,9},{9,25},... | collective-permute-start | bytes 589832 | tf_op jit(solution)/shard_map/ppermute | solution.py:356
  8.9 3.5 %edges.1 = (f32[16,256]{1,0:T(8,128)S(1)}, f32[24,256]{1,0:T(8,128)S(1)}, s32[2,52]{1,0:T(2,128)S(4)}, s32[2]{0:T(128)S(4)}, bf16[48,256,256]{2,1,0:T(8,128)(2,1)S(1)}) custom-call(s32[1]{0:T(128)} %bitcast.place_ref, s32[48]{0:T(128)} %bitcast.18, s32[48]{0:T(128)} %bitcast.19, s32[1]{0:T(128)} %bitcast.16.count_ref, bf16[48,256,256]{2,1,0:T(8,128)(2,1)} %bitcast.17, ...), custom_call_target="tpu_custom_call" | custom-call | bytes 1048576 | tf_op jit(solution)/shard_map/edges/pallas_call | solution.py:415
  12.4 2.6 %copy-done = bf16[48,256,256]{2,1,0:T(8,128)(2,1)} copy-done((bf16[48,256,256]{2,1,0:T(8,128)(2,1)}, bf16[48,256,256]{2,1,0:T(8,128)(2,1)S(1)}, u32[]{:S(2)}) %copy-start) | copy-done | bytes 6291480
  15.1 1.7 %collective-permute-start.2 = (f32[24,256]{1,0:T(8,128)S(1)}, f32[24,256]{1,0:T(8,128)S(1)}, u32[]{:S(2)}, u32[]{:S(2)}) collective-permute-start(f32[24,256]{1,0:T(8,128)S(1)} %get-tuple-element.28.refs_0_), channel_id=1, source_target_pairs={{0,4},{1,5},{2,6},{3,7},{4,0},{5,1},{6,2},{7,3},{8,12},{9,13},{10,... | collective-permute-start | bytes 73736 | tf_op jit(solution)/shard_map/ppermute | solution.py:356
  16.7 2.2 %collective-permute-done.2.refs_1_ = f32[24,256]{1,0:T(8,128)S(1)} collective-permute-done((f32[24,256]{1,0:T(8,128)S(1)}, f32[24,256]{1,0:T(8,128)S(1)}, u32[]{:S(2)}, u32[]{:S(2)}) %collective-permute-start.2) | collective-permute-done | bytes 24608 | tf_op jit(solution)/shard_map/ppermute | solution.py:356
  18.9 8.3 %collective-permute-start.10 = (f32[16,256]{1,0:T(8,128)S(1)}, f32[16,256]{1,0:T(8,128)S(1)}, u32[]{:S(2)}, u32[]{:S(2)}) collective-permute-start(f32[16,256]{1,0:T(8,128)S(1)} %get-tuple-element.31), channel_id=1, source_target_pairs={{0,16},{1,17},{2,18},{3,19},{4,20},{5,21},{6,22},{7,23},{8,24},{9,... | collective-permute-start | bytes 49160 | tf_op jit(solution)/shard_map/ppermute | solution.py:356
  27.2 1.5 %collective-permute-start.6 = (bf16[384,256]{1,0:T(8,128)(2,1)S(1)}, bf16[384,256]{1,0:T(8,128)(2,1)S(1)}, u32[]{:S(2)}, u32[]{:S(2)}) collective-permute-start(bf16[384,256]{1,0:T(8,128)(2,1)S(1)} %collective-permute-done.1._.refs_0_), channel_id=1, source_target_pairs={{0,4},{1,5},{2,6},{3,7},{4,0},{5,1},{6,2},{7,3},{8,12},{9,13},{10,... | collective-permute-start | bytes 589832 | tf_op jit(solution)/shard_map/ppermute | solution.py:356
  29.3 2.2 %collective-permute-start.5 = (bf16[144,256]{1,0:T(8,128)(2,1)S(1)}, bf16[144,256]{1,0:T(8,128)(2,1)S(1)}, u32[]{:S(2)}, u32[]{:S(2)}) collective-permute-start(bf16[144,256]{1,0:T(8,128)(2,1)S(1)} %get-tuple-element.29), channel_id=1, source_target_pairs={{0,8},{1,24},{2,0},{3,16},{4,12},{5,28},{6,4},{7,20},{8,9},{9,25},... | collective-permute-start | bytes 221192 | tf_op jit(solution)/shard_map/ppermute | solution.py:356
  31.5 0.7 %collective-permute-start.3 = (bf16[144,256]{1,0:T(8,128)(2,1)S(1)}, bf16[144,256]{1,0:T(8,128)(2,1)S(1)}, u32[]{:S(2)}, u32[]{:S(2)}) collective-permute-start(bf16[144,256]{1,0:T(8,128)(2,1)S(1)} %get-tuple-element.29), channel_id=1, source_target_pairs={{0,0},{1,16},{2,8},{3,24},{4,4},{5,20},{6,12},{7,28},{8,1},{9,17},... | collective-permute-start | bytes 221192 | tf_op jit(solution)/shard_map/ppermute | solution.py:356
  32.2 1.4 %collective-permute-done.5.refs_3_.refs_1_ = bf16[144,256]{1,0:T(8,128)(2,1)S(1)} collective-permute-done((bf16[144,256]{1,0:T(8,128)(2,1)S(1)}, bf16[144,256]{1,0:T(8,128)(2,1)S(1)}, u32[]{:S(2)}, u32[]{:S(2)}) %collective-permute-start.5) | collective-permute-done | bytes 73760 | tf_op jit(solution)/shard_map/ppermute | solution.py:356
  33.6 5.1 %collective-permute-start.11 = (f32[16,256]{1,0:T(8,128)S(1)}, f32[16,256]{1,0:T(8,128)S(1)}, u32[]{:S(2)}, u32[]{:S(2)}) collective-permute-start(f32[16,256]{1,0:T(8,128)S(1)} %multiply_select_fusion), channel_id=1, source_target_pairs={{0,8},{1,9},{2,10},{3,11},{4,12},{5,13},{6,14},{7,15},{8,0},{9,1},... | collective-permute-start | bytes 49160 | tf_op jit(solution)/shard_map/ppermute | solution.py:356
  38.8 1.4 %collective-permute-start.13 = (bf16[144,256]{1,0:T(8,128)(2,1)S(1)}, bf16[144,256]{1,0:T(8,128)(2,1)S(1)}, u32[]{:S(2)}, u32[]{:S(2)}) collective-permute-start(bf16[144,256]{1,0:T(8,128)(2,1)S(1)} %collective-permute-done.5.refs_3_.refs_1_), channel_id=1, source_target_pairs={{0,4},{1,5},{2,6},{3,7},{4,0},{5,1},{6,2},{7,3},{8,12},{9,13},{10,... | collective-permute-start | bytes 221192 | tf_op jit(solution)/shard_map/ppermute | solution.py:356
  40.8 2.8 %copy-done.1 = bf16[48,256,256]{2,1,0:T(8,128)(2,1)S(1)} copy-done((bf16[48,256,256]{2,1,0:T(8,128)(2,1)S(1)}, bf16[48,256,256]{2,1,0:T(8,128)(2,1)}, u32[]{:S(2)}) %copy-start.1) | copy-done | bytes 6291480
  44.4 1.1 %collective-permute-done.8 = f32[16,128]{1,0:T(8,128)S(1)} collective-permute-done((f32[16,128]{1,0:T(8,128)S(1)}, f32[16,128]{1,0:T(8,128)S(1)}, u32[]{:S(2)}, u32[]{:S(2)}) %collective-permute-start.8) | collective-permute-done | bytes 8224 | tf_op jit(solution)/shard_map/ppermute | solution.py:465
  45.6 2.4 %collective-permute-start.9 = (f32[16,128]{1,0:T(8,128)S(1)}, f32[16,128]{1,0:T(8,128)S(1)}, u32[]{:S(2)}, u32[]{:S(2)}) collective-permute-start(f32[16,128]{1,0:T(8,128)S(1)} %multiply_select_fusion.1), channel_id=1, source_target_pairs={{0,2},{1,3},{2,0},{3,1},{4,6},{5,7},{6,4},{7,5},{8,10},{9,11},{10,... | collective-permute-start | bytes 24584 | tf_op jit(solution)/shard_map/ppermute | solution.py:465
  48.0 1.6 %collective-permute-done.9 = f32[16,128]{1,0:T(8,128)S(1)} collective-permute-done((f32[16,128]{1,0:T(8,128)S(1)}, f32[16,128]{1,0:T(8,128)S(1)}, u32[]{:S(2)}, u32[]{:S(2)}) %collective-permute-start.9) | collective-permute-done | bytes 8224 | tf_op jit(solution)/shard_map/ppermute | solution.py:465
  49.8 1.2 %far.1 = (f32[2,8,32,256]{3,2,1,0:T(8,128)S(1)}, f32[2,8,32,256]{3,2,1,0:T(8,128)S(1)}) custom-call(s32[1]{0:T(128)} %bitcast.place_ref, s32[2,52]{1,0:T(2,128)S(4)} %get-tuple-element.24.order_ref, s32[2]{0:T(128)S(4)} %get-tuple-element.25.sizes_ref, bf16[48,256,256]{2,1,0:T(8,128)(2,1)S(1)} %copy-done.2, f32[9,128,256]{2,1,0:T(8,128)S(1)} %near.1.near_ref, ...), custom_call_target="tpu_custom_call" | custom-call | bytes 1048576 | tf_op jit(solution)/shard_map/far/pallas_call | solution.py:489
  51.1 1.9 %collective-permute-done.14.arrived_ref = f32[2,8,32,256]{3,2,1,0:T(8,128)S(1)} collective-permute-done((f32[2,8,32,256]{3,2,1,0:T(8,128)S(1)}, f32[2,8,32,256]{3,2,1,0:T(8,128)S(1)}, u32[]{:S(2)}, u32[]{:S(2)}) %collective-permute-start.14) | collective-permute-done | bytes 524320 | tf_op jit(solution)/shard_map/ppermute | solution.py:356
  53.0 2.3 %collective-permute-start.15 = (bf16[8,32,256]{2,1,0:T(8,128)(2,1)S(1)}, bf16[8,32,256]{2,1,0:T(8,128)(2,1)S(1)}, u32[]{:S(2)}, u32[]{:S(2)}) collective-permute-start(bf16[8,32,256]{2,1,0:T(8,128)(2,1)S(1)} %get-tuple-element.38), channel_id=1, source_target_pairs={{0,2},{1,3},{2,0},{3,1},{4,6},{5,7},{6,4},{7,5},{8,10},{9,11},{10,... | collective-permute-start | bytes 393224 | tf_op jit(solution)/shard_map/ppermute | solution.py:356
  55.4 3.8 %collective-permute-done.15.refs_0_ = bf16[8,32,256]{2,1,0:T(8,128)(2,1)S(1)} collective-permute-done((bf16[8,32,256]{2,1,0:T(8,128)(2,1)S(1)}, bf16[8,32,256]{2,1,0:T(8,128)(2,1)S(1)}, u32[]{:S(2)}, u32[]{:S(2)}) %collective-permute-start.15) | collective-permute-done | bytes 131104 | tf_op jit(solution)/shard_map/ppermute | solution.py:356
  59.2 1.1 %back.1 = f32[32,2048]{1,0:T(8,128)} custom-call(f32[8,32,256]{2,1,0:T(8,128)S(1)} %get-tuple-element.37.own_ref, bf16[8,32,256]{2,1,0:T(8,128)(2,1)S(1)} %collective-permute-done.15.refs_0_), custom_call_target="tpu_custom_call" | custom-call | bytes 1048576 | tf_op jit(solution)/shard_map/back/pallas_call | solution.py:515
  (28 shorter events, 2.7 us)
Async XLA Ops:
  0.0 1.8 %collective-permute-start = (f32[32,2048]{1,0:T(8,128)}, f32[32,2048]{1,0:T(8,128)S(1)}, u32[]{:S(2)}, u32[]{:S(2)}) collective-permute-start(f32[32,2048]{1,0:T(8,128)} %sources_ref.1), channel_id=1, source_target_pairs={{0,1},{1,0},{2,3},{3,2},{4,5},{5,4},{6,7},{7,6},{8,9},{9,8},{10,11... | collective-permute-start | bytes 786440 | tf_op jit(solution)/shard_map/ppermute | solution.py:356
  3.3 5.6 %collective-permute-start.1 = (bf16[384,256]{1,0:T(8,128)(2,1)S(1)}, bf16[384,256]{1,0:T(8,128)(2,1)S(1)}, u32[]{:S(2)}, u32[]{:S(2)}) collective-permute-start(bf16[384,256]{1,0:T(8,128)(2,1)S(1)} %get-tuple-element.23), channel_id=1, source_target_pairs={{0,0},{1,16},{2,8},{3,24},{4,4},{5,20},{6,12},{7,28},{8,1},{9,17},... | collective-permute-start | bytes 589832 | tf_op jit(solution)/shard_map/ppermute | solution.py:356
  4.0 24.8 %collective-permute-start.4 = (bf16[384,256]{1,0:T(8,128)(2,1)S(1)}, bf16[384,256]{1,0:T(8,128)(2,1)S(1)}, u32[]{:S(2)}, u32[]{:S(2)}) collective-permute-start(bf16[384,256]{1,0:T(8,128)(2,1)S(1)} %get-tuple-element.23), channel_id=1, source_target_pairs={{0,8},{1,24},{2,0},{3,16},{4,12},{5,28},{6,4},{7,20},{8,9},{9,25},... | collective-permute-start | bytes 589832 | tf_op jit(solution)/shard_map/ppermute | solution.py:356
  12.4 2.7 %copy-start = (bf16[48,256,256]{2,1,0:T(8,128)(2,1)}, bf16[48,256,256]{2,1,0:T(8,128)(2,1)S(1)}, u32[]{:S(2)}) copy-start(bf16[48,256,256]{2,1,0:T(8,128)(2,1)S(1)} %get-tuple-element.26.tiles_ref) | copy-start | bytes 18874372
  15.1 3.8 %collective-permute-start.2 = (f32[24,256]{1,0:T(8,128)S(1)}, f32[24,256]{1,0:T(8,128)S(1)}, u32[]{:S(2)}, u32[]{:S(2)}) collective-permute-start(f32[24,256]{1,0:T(8,128)S(1)} %get-tuple-element.28.refs_0_), channel_id=1, source_target_pairs={{0,4},{1,5},{2,6},{3,7},{4,0},{5,1},{6,2},{7,3},{8,12},{9,13},{10,... | collective-permute-start | bytes 73736 | tf_op jit(solution)/shard_map/ppermute | solution.py:356
  18.9 13.2 %collective-permute-start.10 = (f32[16,256]{1,0:T(8,128)S(1)}, f32[16,256]{1,0:T(8,128)S(1)}, u32[]{:S(2)}, u32[]{:S(2)}) collective-permute-start(f32[16,256]{1,0:T(8,128)S(1)} %get-tuple-element.31), channel_id=1, source_target_pairs={{0,16},{1,17},{2,18},{3,19},{4,20},{5,21},{6,22},{7,23},{8,24},{9,... | collective-permute-start | bytes 49160 | tf_op jit(solution)/shard_map/ppermute | solution.py:356
  27.2 17.0 %collective-permute-start.6 = (bf16[384,256]{1,0:T(8,128)(2,1)S(1)}, bf16[384,256]{1,0:T(8,128)(2,1)S(1)}, u32[]{:S(2)}, u32[]{:S(2)}) collective-permute-start(bf16[384,256]{1,0:T(8,128)(2,1)S(1)} %collective-permute-done.1._.refs_0_), channel_id=1, source_target_pairs={{0,4},{1,5},{2,6},{3,7},{4,0},{5,1},{6,2},{7,3},{8,12},{9,13},{10,... | collective-permute-start | bytes 589832 | tf_op jit(solution)/shard_map/ppermute | solution.py:356
  28.8 15.4 %collective-permute-start.7 = (bf16[384,256]{1,0:T(8,128)(2,1)S(1)}, bf16[384,256]{1,0:T(8,128)(2,1)S(1)}, u32[]{:S(2)}, u32[]{:S(2)}) collective-permute-start(bf16[384,256]{1,0:T(8,128)(2,1)S(1)} %collective-permute-done.4.refs_2_), channel_id=1, source_target_pairs={{0,4},{1,5},{2,6},{3,7},{4,0},{5,1},{6,2},{7,3},{8,12},{9,13},{10,... | collective-permute-start | bytes 589832 | tf_op jit(solution)/shard_map/ppermute | solution.py:356
  29.3 4.4 %collective-permute-start.5 = (bf16[144,256]{1,0:T(8,128)(2,1)S(1)}, bf16[144,256]{1,0:T(8,128)(2,1)S(1)}, u32[]{:S(2)}, u32[]{:S(2)}) collective-permute-start(bf16[144,256]{1,0:T(8,128)(2,1)S(1)} %get-tuple-element.29), channel_id=1, source_target_pairs={{0,8},{1,24},{2,0},{3,16},{4,12},{5,28},{6,4},{7,20},{8,9},{9,25},... | collective-permute-start | bytes 221192 | tf_op jit(solution)/shard_map/ppermute | solution.py:356
  31.5 2.1 %collective-permute-start.3 = (bf16[144,256]{1,0:T(8,128)(2,1)S(1)}, bf16[144,256]{1,0:T(8,128)(2,1)S(1)}, u32[]{:S(2)}, u32[]{:S(2)}) collective-permute-start(bf16[144,256]{1,0:T(8,128)(2,1)S(1)} %get-tuple-element.29), channel_id=1, source_target_pairs={{0,0},{1,16},{2,8},{3,24},{4,4},{5,20},{6,12},{7,28},{8,1},{9,17},... | collective-permute-start | bytes 221192 | tf_op jit(solution)/shard_map/ppermute | solution.py:356
  33.6 10.8 %collective-permute-start.11 = (f32[16,256]{1,0:T(8,128)S(1)}, f32[16,256]{1,0:T(8,128)S(1)}, u32[]{:S(2)}, u32[]{:S(2)}) collective-permute-start(f32[16,256]{1,0:T(8,128)S(1)} %multiply_select_fusion), channel_id=1, source_target_pairs={{0,8},{1,9},{2,10},{3,11},{4,12},{5,13},{6,14},{7,15},{8,0},{9,1},... | collective-permute-start | bytes 49160 | tf_op jit(solution)/shard_map/ppermute | solution.py:356
  38.8 11.0 %collective-permute-start.13 = (bf16[144,256]{1,0:T(8,128)(2,1)S(1)}, bf16[144,256]{1,0:T(8,128)(2,1)S(1)}, u32[]{:S(2)}, u32[]{:S(2)}) collective-permute-start(bf16[144,256]{1,0:T(8,128)(2,1)S(1)} %collective-permute-done.5.refs_3_.refs_1_), channel_id=1, source_target_pairs={{0,4},{1,5},{2,6},{3,7},{4,0},{5,1},{6,2},{7,3},{8,12},{9,13},{10,... | collective-permute-start | bytes 221192 | tf_op jit(solution)/shard_map/ppermute | solution.py:356
  40.2 9.6 %collective-permute-start.12 = (bf16[144,256]{1,0:T(8,128)(2,1)S(1)}, bf16[144,256]{1,0:T(8,128)(2,1)S(1)}, u32[]{:S(2)}, u32[]{:S(2)}) collective-permute-start(bf16[144,256]{1,0:T(8,128)(2,1)S(1)} %collective-permute-done.3.refs_1_.refs_0_), channel_id=1, source_target_pairs={{0,4},{1,5},{2,6},{3,7},{4,0},{5,1},{6,2},{7,3},{8,12},{9,13},{10,... | collective-permute-start | bytes 221192 | tf_op jit(solution)/shard_map/ppermute | solution.py:356
  40.8 2.8 %copy-start.1 = (bf16[48,256,256]{2,1,0:T(8,128)(2,1)S(1)}, bf16[48,256,256]{2,1,0:T(8,128)(2,1)}, u32[]{:S(2)}) copy-start(bf16[48,256,256]{2,1,0:T(8,128)(2,1)} %copy-done) | copy-start | bytes 18874372
  43.6 6.2 %copy-start.2 = (bf16[48,256,256]{2,1,0:T(8,128)(2,1)S(1)}, bf16[48,256,256]{2,1,0:T(8,128)(2,1)}, u32[]{:S(2)}) copy-start(bf16[48,256,256]{2,1,0:T(8,128)(2,1)} %copy-done) | copy-start | bytes 18874372
  44.3 1.2 %collective-permute-start.8 = (f32[16,128]{1,0:T(8,128)S(1)}, f32[16,128]{1,0:T(8,128)S(1)}, u32[]{:S(2)}, u32[]{:S(2)}) collective-permute-start(f32[16,128]{1,0:T(8,128)S(1)} %firsts.1), channel_id=1, source_target_pairs={{0,1},{1,0},{2,3},{3,2},{4,5},{5,4},{6,7},{7,6},{8,9},{9,8},{10,11... | collective-permute-start | bytes 24584 | tf_op jit(solution)/shard_map/ppermute | solution.py:465
  45.6 4.0 %collective-permute-start.9 = (f32[16,128]{1,0:T(8,128)S(1)}, f32[16,128]{1,0:T(8,128)S(1)}, u32[]{:S(2)}, u32[]{:S(2)}) collective-permute-start(f32[16,128]{1,0:T(8,128)S(1)} %multiply_select_fusion.1), channel_id=1, source_target_pairs={{0,2},{1,3},{2,0},{3,1},{4,6},{5,7},{6,4},{7,5},{8,10},{9,11},{10,... | collective-permute-start | bytes 24584 | tf_op jit(solution)/shard_map/ppermute | solution.py:465
  51.0 2.0 %collective-permute-start.14 = (f32[2,8,32,256]{3,2,1,0:T(8,128)S(1)}, f32[2,8,32,256]{3,2,1,0:T(8,128)S(1)}, u32[]{:S(2)}, u32[]{:S(2)}) collective-permute-start(f32[2,8,32,256]{3,2,1,0:T(8,128)S(1)} %get-tuple-element.36), channel_id=1, source_target_pairs={{0,1},{1,0},{2,3},{3,2},{4,5},{5,4},{6,7},{7,6},{8,9},{9,8},{10,11... | collective-permute-start | bytes 1572872 | tf_op jit(solution)/shard_map/ppermute | solution.py:356
  53.0 6.1 %collective-permute-start.15 = (bf16[8,32,256]{2,1,0:T(8,128)(2,1)S(1)}, bf16[8,32,256]{2,1,0:T(8,128)(2,1)S(1)}, u32[]{:S(2)}, u32[]{:S(2)}) collective-permute-start(bf16[8,32,256]{2,1,0:T(8,128)(2,1)S(1)} %get-tuple-element.38), channel_id=1, source_target_pairs={{0,2},{1,3},{2,0},{3,1},{4,6},{5,7},{6,4},{7,5},{8,10},{9,11},{10,... | collective-permute-start | bytes 393224 | tf_op jit(solution)/shard_map/ppermute | solution.py:356
where the time goes:
time: 60.1 us; the launch traced here: 60.2 us
  starting transfers between devices  32.3 us (54%)
  waiting for transfers between devices  13.4 us (22%)
  Pallas kernels  8.08 us (13%)
  local copies, waits for them, and re-layouts  5.43 us (9%)
  between operations  0.81 us (1%)
    ppermute x14, starting transfers between devices, moved(): return lax.ppermute(value, ('row', 'col'), pairs)  29.8 us
    ppermute x14, waiting for transfers between devices, moved(): return lax.ppermute(value, ('row', 'col'), pairs)  10.7 us
    unnamed x6, local copies, waits for them, and re-layouts  5.43 us
    pallas_call x1, Pallas kernels, local(): call(edge_kernel, 'edges', [f32(length, extent), f32(length + 8, extent),...  3.53 us
    ppermute x2, waiting for transfers between devices, local(): partner = lax.ppermute(firsts, 'col', pairs)  2.76 us
    ppermute x2, starting transfers between devices, local(): partner = lax.ppermute(firsts, 'col', pairs)  2.48 us
    pallas_call x1, Pallas kernels, local(): call(front_kernel, 'front', [bf16((blocks - last) * pair, extent), bf16(l...  1.44 us
    pallas_call x1, Pallas kernels, local(): call(far_kernel, 'far', [f32(*shape)] * 2, [smem] * 3 + [vmem] * (5 + len...  1.22 us
  transfers between devices with their start and end apart: 16, of which 7 were waited for; matrix products, arithmetic and copies ran while one was open for 0% of the time, Pallas kernels for 7%

commit v1 on v0

v1 whole, which is shorter than its diff:
```python
import functools
import math

import jax
import jax.numpy as jnp
from jax import lax
from jax.experimental import pallas as pl
from jax.experimental.pallas import tpu as pltpu
from jax.sharding import PartitionSpec as P

ROOT_HALF = 1.0 / math.sqrt(2.0)
SIDE_ROWS = 16
UNROLL = 4
MIB = 2**20


def haar_parts(extent, transposed):
    k = lax.broadcasted_iota(jnp.int32, (extent, extent), 1 if transposed else 0)
    n = lax.broadcasted_iota(jnp.int32, (extent, extent), 0 if transposed else 1)
    stride = jnp.where(n == 0, extent, n & -n)
    signs = jnp.where((k ^ n) < 2 * stride, jnp.where((k & stride) == 0, 1.0, -1.0), 0.0)
    n = lax.broadcasted_iota(jnp.int32, (1, extent), 1)
    scale = jnp.full((1, extent), 1.0 / math.sqrt(extent), jnp.float32)
    level = 1
    while level < extent:
        scale = jnp.where((n & -n) == level, 1.0 / math.sqrt(2 * level), scale)
        level *= 2
    return signs.astype(jnp.bfloat16), scale


def three_terms(value):
    high = value.astype(jnp.bfloat16)
    rest = value - high.astype(jnp.float32)
    middle = rest.astype(jnp.bfloat16)
    low = (rest - middle.astype(jnp.float32)).astype(jnp.bfloat16)
    return high, middle, low


def exact_dot(value, signs):
    return sum(jnp.dot(term, signs, preferred_element_type=jnp.float32) for term in three_terms(value))


def block_forward(columns):
    columns = list(columns)
    stride = 1
    while stride < len(columns):
        for p in range(0, len(columns), 2 * stride):
            u, v = columns[p], columns[p + stride]
            columns[p], columns[p + stride] = (u + v) * ROOT_HALF, (u - v) * ROOT_HALF
        stride *= 2
    return columns


def block_inverse(columns):
    columns = list(columns)
    stride = len(columns) // 2
    while stride >= 1:
        for p in range(0, len(columns), 2 * stride):
            u, v = columns[p], columns[p + stride]
            columns[p], columns[p + stride] = (u + v) * ROOT_HALF, (u - v) * ROOT_HALF
        stride //= 2
    return columns


def packed_place(core, span, x, z):
    return (core + 2 * span + 256 * x + 65536 * z).astype(jnp.int32).reshape(1)


def core_of(place_ref):
    return place_ref[0] & 1


def span_of(place_ref):
    return (place_ref[0] >> 1) & 127


def x_of(place_ref):
    return (place_ref[0] >> 8) & 255


def source_span(place_ref, m, spans):
    return lax.rem((place_ref[0] >> 16) - m + spans * 256, spans)


def front_kernel(place_ref, sources_ref, other_ref, out_ref, mine_ref, sem, *, blocks, extent):
    copy = pltpu.make_async_copy(sources_ref, mine_ref, sem)
    copy.start()
    height = mine_ref.shape[0]
    pair = 2 * height
    signs, scale = haar_parts(extent, False)
    copy.wait()
    mine, other = mine_ref[...], other_ref[...]
    first_core = core_of(place_ref) == 0
    both = jnp.concatenate([jnp.where(first_core, mine, other), jnp.where(first_core, other, mine)], axis=0)
    parts = [both[:, b * extent : (b + 1) * extent] for b in range(blocks)]
    coef = exact_dot(jnp.concatenate(parts, axis=0), signs) * scale
    columns = block_forward([coef[b * pair : (b + 1) * pair, 0:1] for b in range(blocks)])
    lane = lax.broadcasted_iota(jnp.int32, (pair, extent), 1)
    for b in range(blocks):
        column = jnp.zeros_like(columns[0]) if b == 0 else columns[b]
        block = jnp.where(lane == 0, column, coef[b * pair : (b + 1) * pair, :])
        out_ref[b * pair : (b + 1) * pair, :] = block.astype(jnp.bfloat16)
    total = functools.reduce(jnp.add, parts)
    ones = jnp.ones((SIDE_ROWS, extent), jnp.bfloat16)
    first = sum(
        lax.dot_general(ones, term, (((1,), (1,)), ((), ())), preferred_element_type=jnp.float32)
        for term in three_terms(total)
    ) * (1.0 / math.sqrt(blocks * extent))
    high, middle, low = (term.astype(jnp.float32) for term in three_terms(first))
    row = lax.broadcasted_iota(jnp.int32, first.shape, 0)
    side = jnp.where(row == 0, high, jnp.where(row == 1, middle, jnp.where(row == 2, low, 0.0)))
    out_ref[blocks * pair :, :] = jnp.zeros((SIDE_ROWS, extent), jnp.bfloat16)
    out_ref[blocks * pair :, 0:pair] = side.astype(jnp.bfloat16)


def list_kernel(place_ref, rows_ref, cols_ref, count_ref, order_ref, sizes_ref, *, blocks, owners):
    x = x_of(place_ref)

    def visit(slot, sizes):
        row, col = rows_ref[slot], cols_ref[slot]
        owner, block = col // blocks, lax.rem(col, blocks)
        behind = lax.rem(x - owner + owners, owners)
        near = behind == 0
        side = jnp.where(near, block, (behind - 1) * blocks + block)
        entry = (slot << 16) + (side << 8) + row
        plain = (slot << 16) + (col << 8) + row
        near_size, far_size, row_size, col_size = sizes
        order_ref[jnp.where(near, 0, 1), jnp.where(near, near_size, far_size)] = entry
        order_ref[2, row_size] = plain
        order_ref[3, col_size] = plain
        one = near.astype(jnp.int32)
        return (
            near_size + one,
            far_size + 1 - one,
            row_size + (row == 0).astype(jnp.int32),
            col_size + (block == 0).astype(jnp.int32),
        )

    sizes = lax.fori_loop(0, count_ref[0], visit, (jnp.int32(0),) * 4)
    for which in range(4):
        sizes_ref[which] = sizes[which]
    for which in range(2):
        for k in range(UNROLL - 1):
            order_ref[which, sizes[which] + k] = blocks


def edge_kernel(_, order_ref, sizes_ref, tiles_ref, cols_ref, line_ref, strips, held, strip_sems, held_sems):
    extent = tiles_ref.shape[-1]

    def strip_copy(index):
        slot = order_ref[3, index] >> 16
        return pltpu.make_async_copy(tiles_ref.at[slot, 0:SIDE_ROWS, :], strips.at[index], strip_sems.at[index])

    def tile_copy(index):
        slot = order_ref[2, index] >> 16
        return pltpu.make_async_copy(tiles_ref.at[slot], held.at[index], held_sems.at[index])

    lax.fori_loop(0, sizes_ref[2], lambda i, _: (tile_copy(i).start(), 0)[1], 0)
    lax.fori_loop(0, sizes_ref[3], lambda i, _: (strip_copy(i).start(), 0)[1], 0)
    cols_ref[...] = jnp.zeros_like(cols_ref)
    line_ref[...] = jnp.zeros_like(line_ref)
    pick = (lax.broadcasted_iota(jnp.int32, (SIDE_ROWS, extent), 1) == 0).astype(jnp.bfloat16)

    def add_strip(index, _):
        entry = order_ref[3, index]
        strip_copy(index).wait()
        at = pl.ds(((entry >> 8) & 255) + (entry & 255), 1)
        cols_ref[at, :] += strips[index].astype(jnp.float32)[0:1, :]
        return 0

    def add_column(index, _):
        tile_copy(index).wait()
        column = lax.dot_general(pick, held[index], (((1,), (1,)), ((), ())), preferred_element_type=jnp.float32)
        line_ref[pl.ds((order_ref[2, index] >> 8) & 255, 1), :] += column[0:1, :]
        return 0

    lax.fori_loop(0, sizes_ref[3], add_strip, 0)
    lax.fori_loop(0, sizes_ref[2], add_column, 0)


def corner_kernel(place_ref, lead_ref, partner_ref, cols_ref, *refs, blocks, owners):
    lines, (out_ref, line_ref, rest_ref) = refs[:owners], refs[owners:]
    lead, partner = lead_ref[...], partner_ref[...]
    lead = jnp.where(core_of(place_ref) == 1, partner - lead, partner + lead) * ROOT_HALF
    columns = [lead[0:blocks, :]] + [cols_ref[i * blocks : (i + 1) * blocks, :] for i in range(1, owners)]
    for i, column in enumerate(block_inverse(columns)):
        out_ref[i * blocks : (i + 1) * blocks, :] = column
    index = lax.broadcasted_iota(jnp.int32, line_ref.shape, 0)
    lane = lax.broadcasted_iota(jnp.int32, line_ref.shape, 1)
    for x in range(owners):
        line = lines[x][...]
        corner = [lead[blocks + x : blocks + x + 1, :]] + [line[i * blocks : i * blocks + 1, :] for i in range(1, owners)]
        for i, value in enumerate(block_inverse(corner)):
            line = jnp.where((index == i * blocks) & (lane == 0), value[:, 0:1], line)
        if x == 0:
            line_ref[...] = line
        else:
            rest_ref[x - 1] = line


def fill_sides(sides, messages, place_ref, blocks, spans):
    pair = sides.shape[1] // spans
    for index, message in enumerate(messages):
        behind, m = index // spans, index % spans
        rows = pl.ds(pl.multiple_of(source_span(place_ref, m, spans) * pair, pair), pair)
        for b in range(blocks):
            sides[behind * blocks + b, rows, :] = message[b * pair : (b + 1) * pair, :]


def start_tiles(order_ref, sizes_ref, which, tiles_ref, held, sems):
    def start(index, _):
        slot = order_ref[which, index] >> 16
        pltpu.make_async_copy(tiles_ref.at[slot], held.at[index], sems.at[index]).start()
        return 0

    lax.fori_loop(0, (sizes_ref[which] + UNROLL - 1) // UNROLL * UNROLL, start, 0)


def add_products(order_ref, sizes_ref, which, tiles_ref, held, sems, sides, acc):
    def group(index, _):
        for k in range(UNROLL):
            at = index * UNROLL + k
            pltpu.make_async_copy(tiles_ref.at[0], held.at[at], sems.at[at]).wait()
        for k in range(UNROLL):
            at = index * UNROLL + k
            entry = order_ref[which, at]
            side, row = (entry >> 8) & 255, entry & 255
            acc[row] += jnp.dot(sides[side], held[at], preferred_element_type=jnp.float32)
        return 0

    lax.fori_loop(0, (sizes_ref[which] + UNROLL - 1) // UNROLL, group, 0)


def near_kernel(place_ref, order_ref, sizes_ref, tiles_ref, *refs, blocks, spans):
    *messages, acc_ref, sides, held, sems = refs
    start_tiles(order_ref, sizes_ref, 0, tiles_ref, held, sems)
    fill_sides(sides, messages, place_ref, blocks, spans)
    acc_ref[...] = jnp.zeros_like(acc_ref)
    add_products(order_ref, sizes_ref, 0, tiles_ref, held, sems, sides, acc_ref)


def far_kernel(place_ref, order_ref, sizes_ref, tiles_ref, near_ref, cols_ref, row_ref, *refs, blocks, owners, spans):
    direct, swapped = refs[:spans], refs[spans : owners * spans]
    keep_ref, send_ref, sides, acc, firsts, held, sems = refs[owners * spans :]
    start_tiles(order_ref, sizes_ref, 1, tiles_ref, held, sems)
    extent = tiles_ref.shape[-1]
    pair = sides.shape[1] // spans
    height = pair // 2
    x = x_of(place_ref)
    fill_sides(sides, swapped, place_ref, blocks, spans)
    messages = (*direct, *swapped)
    for index, message in enumerate(messages):
        owner = lax.rem(x - index // spans + owners, owners)
        side = jnp.transpose(message[blocks * pair :, :].astype(jnp.float32))
        column = side[0:pair, 0:1] + side[0:pair, 1:2] + side[0:pair, 2:3]
        rows = pl.ds(pl.multiple_of(source_span(place_ref, index % spans, spans) * pair, pair), pair)
        firsts[owner, rows, :] = jnp.broadcast_to(column, (pair, firsts.shape[2]))
    for i in range(blocks):
        total = near_ref[i]
        for owner in range(owners):
            total += firsts[owner][:, 0:1] * cols_ref[owner * blocks + i : owner * blocks + i + 1, :]
        acc[i] = total
    add_products(order_ref, sizes_ref, 1, tiles_ref, held, sems, sides, acc)

    lane = lax.broadcasted_iota(jnp.int32, (pair, extent), 1)
    for m in range(spans):
        rows = pl.ds(pl.multiple_of(source_span(place_ref, m, spans) * pair, pair), pair)
        total = jnp.zeros((pair, extent), jnp.float32)
        top = jnp.zeros((pair, 1), jnp.float32)
        for behind in range(owners):
            owner = lax.rem(x - behind + owners, owners)
            message = messages[behind * spans + m]
            for b in range(blocks):
                line = row_ref[pl.ds(owner * blocks + b, 1), :]
                total += message[b * pair : (b + 1) * pair, :].astype(jnp.float32) * line
                if b == 0:
                    top += firsts[owner, rows, :][:, 0:1] * line[:, 0:1]
        top += jnp.sum(total, axis=1, keepdims=True)
        acc[0, rows, :] = jnp.where(lane == 0, top, acc[0, rows, :])
    first_core = core_of(place_ref) == 0
    for i in range(blocks):
        value = acc[i]
        for y in range(spans):
            one = value[y * pair : y * pair + height, :]
            two = value[y * pair + height : (y + 1) * pair, :]
            keep_ref[y, i] = jnp.where(first_core, one, two)
            send_ref[y, i] = jnp.where(first_core, two, one)


def combine_kernel(place_ref, keep_ref, arrived_ref, own_ref, *out_refs):
    spans = keep_ref.shape[0]
    span = span_of(place_ref)
    own_ref[...] = keep_ref[span] + arrived_ref[span]
    for j, out_ref in enumerate(out_refs, 1):
        at = lax.rem(span + j, spans)
        out_ref[...] = (keep_ref[at] + arrived_ref[at]).astype(jnp.bfloat16)


def back_kernel(own_ref, *refs):
    *arrived, out_ref = refs
    blocks, height, extent = own_ref.shape
    total = own_ref[...]
    for part in arrived:
        total = total + part[...].astype(jnp.float32)
    columns = block_inverse([total[b][:, 0:1] for b in range(blocks)])
    lane = lax.broadcasted_iota(jnp.int32, (height, extent), 1)
    fixed = jnp.concatenate([jnp.where(lane == 0, columns[b], total[b]) for b in range(blocks)], axis=0)
    signs, scale = haar_parts(extent, True)
    result = exact_dot(fixed * scale, signs)
    for b in range(blocks):
        out_ref[:, b * extent : (b + 1) * extent] = result[b * height : (b + 1) * height, :]


def butterfly(value, partner, index, bit):
    active = index % 2**bit == 0
    upper = index // 2**bit % 2 == 1
    combined = jnp.where(upper, partner - value, partner + value) * ROOT_HALF
    return jnp.where(active, combined, value)


def local(sources, tiles, tile_row, tile_col, tile_count):
    n_row, n_col = lax.axis_size("row"), lax.axis_size("col")
    owners = n_row // n_col
    spans = n_col // 2
    extent = tiles.shape[-1]
    slots = tiles.shape[2]
    height = sources.shape[0]
    blocks = sources.shape[1] // extent
    pair = 2 * height
    row_index, col_index = lax.axis_index("row"), lax.axis_index("col")
    z, x = row_index // owners, row_index % owners
    span, core = col_index // 2, col_index % 2

    def moved(value, to):
        pairs = []
        for a in range(n_row):
            for b in range(n_col):
                zz, xx, yy, cc = to(a // owners, a % owners, b // 2, b % 2)
                pairs.append((a * n_col + b, (zz * owners + xx) * n_col + yy * 2 + cc))
        return lax.ppermute(value, ("row", "col"), pairs)

    def other_core(value):
        return moved(value, lambda zz, xx, yy, cc: (zz, xx, yy, 1 - cc))

    def along_x(value, j):
        return moved(value, lambda zz, xx, yy, cc: (zz, (xx + j) % owners, yy, cc))

    smem = pl.BlockSpec(memory_space=pltpu.SMEM)
    vmem = pl.BlockSpec(memory_space=pltpu.VMEM)
    hbm = pl.BlockSpec(memory_space=pltpu.HBM)

    def call(kernel, name, out_shape, in_specs, out_specs, limit=16, scratch=(), flops=0, moved_bytes=MIB, **sizes):
        return pl.pallas_call(
            functools.partial(kernel, **sizes) if sizes else kernel,
            out_shape=out_shape,
            in_specs=in_specs,
            out_specs=out_specs,
            scratch_shapes=scratch,
            name=name,
            compiler_params=pltpu.CompilerParams(vmem_limit_bytes=int(limit * MIB)),
            cost_estimate=pl.CostEstimate(flops=flops, bytes_accessed=moved_bytes, transcendentals=0),
        )

    def in_hbm(value):
        return pltpu.with_memory_space_constraint(value, pltpu.HBM)

    def f32(*dims):
        return jax.ShapeDtypeStruct(dims, jnp.float32)

    def bf16(*dims):
        return jax.ShapeDtypeStruct(dims, jnp.bfloat16)

    place = packed_place(core, span, x, z)

    def after(value, *others):
        return lax.optimization_barrier((value, *others))[0]

    def apart(body, state):
        return lax.fori_loop(0, jnp.minimum(tile_count.reshape(()), 1), body, tuple(state))

    length = owners * blocks
    stack = tiles.reshape(slots, extent, extent)
    from_core = other_core(sources)
    order, sizes = call(
        list_kernel,
        "lists",
        [pltpu.SMEM((4, slots + UNROLL), jnp.int32), pltpu.SMEM((4,), jnp.int32)],
        [smem] * 4,
        [smem] * 2,
        blocks=blocks,
        owners=owners,
    )(place, in_hbm(tile_row.reshape(-1)), in_hbm(tile_col.reshape(-1)), tile_count.reshape(1))
    message = call(
        front_kernel,
        "front",
        bf16(blocks * pair + SIDE_ROWS, extent),
        [smem, hbm, vmem],
        vmem,
        scratch=[pltpu.VMEM(sources.shape, jnp.float32), pltpu.SemaphoreType.DMA],
        blocks=blocks,
        extent=extent,
    )(place, in_hbm(sources), from_core)

    direct = [
        moved(message, lambda zz, xx, yy, cc, m=m: (cc * spans + (yy + m) % spans, xx, zz // 2, zz % 2))
        for m in range(spans)
    ]

    def early(trip, _):
        cols, line = call(
            edge_kernel,
            "edges",
            [f32(length, extent)] * 2,
            [smem, smem, smem, hbm],
            [vmem] * 2,
            scratch=[
                pltpu.VMEM((slots, SIDE_ROWS, extent), jnp.bfloat16),
                pltpu.VMEM((slots, extent, extent), jnp.bfloat16),
                pltpu.SemaphoreType.DMA((slots,)),
                pltpu.SemaphoreType.DMA((slots,)),
            ],
        )(trip.reshape(1), order, sizes, in_hbm(stack))
        behind = [line] + [along_x(line, j) for j in range(1, owners)]
        lines = []
        for i in range(owners):
            value = behind[0]
            for j in range(1, owners):
                value = jnp.where((x - i) % owners == j, behind[j], value)
            lines.append(value)
        lead = jnp.concatenate([cols[0:blocks]] + [value[0:1] for value in lines] + [cols[0 : blocks - owners]])
        for bit in reversed(range(1, n_col.bit_length() - 1)):
            step = 2 ** (bit - 1)
            partner = moved(lead, lambda zz, xx, yy, cc, step=step: (zz, xx, yy ^ step, cc))
            lead = butterfly(lead, partner, col_index, bit)
        return (lead, cols, *lines)

    sized = [jnp.zeros((2 * blocks, extent), jnp.float32)] + [jnp.zeros((length, extent), jnp.float32)] * (1 + owners)
    lead, cols, *lines = apart(early, sized)
    swapped = [along_x(after(piece, lead), j) for j in range(1, owners) for piece in direct]
    lead = after(lead, direct[0])

    def late(_, state):
        lead, cols, *lines = state
        first_cols, line, rest = call(
            corner_kernel,
            "corner",
            [f32(length, extent)] * 2 + [f32(owners - 1, length, extent)],
            [smem] + [vmem] * (3 + owners),
            [vmem] * 3,
            blocks=blocks,
            owners=owners,
        )(place, lead, other_core(lead), cols, *lines)
        for bit in reversed(range((n_row // owners).bit_length() - 1)):
            partner = moved(line, lambda zz, xx, yy, cc, bit=bit: (zz ^ 2**bit, xx, yy, cc))
            line = butterfly(line, partner, z, bit)
        by_x = block_inverse([line] + [rest[i] for i in range(owners - 1)])
        first_row = by_x[0]
        for i in range(1, owners):
            first_row = jnp.where(x == i, by_x[i], first_row)
        return (lead, first_cols, first_row, *lines[1:])

    _, first_cols, first_row, *_ = apart(late, [lead, cols, *lines])

    every = (spans * pair, extent)
    held_tiles = [
        pltpu.VMEM((slots + UNROLL, extent, extent), jnp.bfloat16),
        pltpu.SemaphoreType.DMA((slots + UNROLL,)),
    ]
    near = call(
        near_kernel,
        "near",
        f32(blocks + 1, *every),
        [smem] * 3 + [hbm] + [vmem] * len(direct),
        vmem,
        limit=24,
        scratch=[pltpu.VMEM((blocks, *every), jnp.bfloat16), *held_tiles],
        blocks=blocks,
        spans=spans,
    )(place, order, sizes, in_hbm(stack), *direct)

    shape = (spans, blocks, height, extent)
    keep, send = call(
        far_kernel,
        "far",
        [f32(*shape)] * 2,
        [smem] * 3 + [hbm] + [vmem] * (3 + len(direct) + len(swapped)),
        [vmem] * 2,
        limit=24,
        scratch=[
            pltpu.VMEM(((owners - 1) * blocks, *every), jnp.bfloat16),
            pltpu.VMEM((blocks + 1, *every), jnp.float32),
            pltpu.VMEM((owners, spans * pair, 128), jnp.float32),
            *held_tiles,
        ],
        blocks=blocks,
        owners=owners,
        spans=spans,
    )(place, order, sizes, in_hbm(stack), near, first_cols, first_row, *direct, *swapped)

    own, *outgoing = call(
        combine_kernel,
        "combine",
        [f32(*shape[1:])] + [bf16(*shape[1:])] * (spans - 1),
        [smem, vmem, vmem],
        [vmem] * spans,
    )(place, keep, other_core(send))
    arrived = [
        moved(value, lambda zz, xx, yy, cc, j=j: (zz, xx, (yy + j) % spans, cc)) for j, value in enumerate(outgoing, 1)
    ]
    return call(back_kernel, "back", f32(*sources.shape), [vmem] * spans, vmem)(own, *arrived)


def solution(mesh):
    return jax.shard_map(
        local,
        mesh=mesh,
        in_specs=(
            P("col", "row"),
            P("row", "col", None, None, None),
            P("row", "col", None),
            P("row", "col", None),
            P("row", "col"),
        ),
        out_specs=P("col", "row"),
        check_vma=False,
    )
```

time: 60.1 us -> 49.5 us (0.82); the launches traced: 60.2 us -> 48.6 us
  starting transfers between devices: 32.3 us -> 18.2 us
  local copies, waits for them, and re-layouts: 5.43 us -> 2.45 us
  Pallas kernels: 8.08 us -> 10.8 us
  waiting for transfers between devices: 13.4 us -> 15.5 us
    ppermute x14 -> x12, starting transfers between devices: 29.8 us -> 18.2 us  [moved(): return lax.ppermute(value, ('row', 'col'), pairs)]
    unnamed x6 -> x8, local copies, waits for them, and re-layouts: 5.43 us -> 0.02 us
    ppermute x14 -> x12, waiting for transfers between devices: 10.7 us -> 15.5 us  [moved(): return lax.ppermute(value, ('row', 'col'), pairs)]
    pallas_call x6, Pallas kernels: 6.92 us -> 9.73 us  [the longest x1 2.71 us: local(): call(far_kernel, 'far', [f32(*shape)] * 2, [smem] * 3 + [hbm] + [vmem] *...]
    ppermute x2 -> x0, waiting for transfers between devices: 2.76 us -> none  [local(): partner = lax.ppermute(firsts, 'col', pairs)]
    ppermute x2 -> x0, starting transfers between devices: 2.48 us -> none  [local(): partner = lax.ppermute(firsts, 'col', pairs)]
    another operation x0 -> x4, local copies, waits for them, and re-layouts: none -> 2.41 us
    select_n x1 -> x2, other arithmetic: 0.01 us -> 0.62 us  [butterfly(): return jnp.where(active, combined, value)]
  transfers between devices with their start and end apart: 16 -> 12, of which waited for: 7 -> 7; matrix products, arithmetic and copies ran while one was open for 0% -> 6% of each run, Pallas kernels for 7% -> 11%
where the time goes in v1:
time: 49.5 us; the launch traced here: 48.6 us
  starting transfers between devices  18.2 us (37%)
  waiting for transfers between devices  15.5 us (31%)
  Pallas kernels  10.8 us (22%)
  local copies, waits for them, and re-layouts  2.45 us (5%)
  between operations  0.82 us (2%)
  other arithmetic  0.65 us (1%)
    ppermute x12, starting transfers between devices, moved(): return lax.ppermute(value, ('row', 'col'), pairs)  18.2 us
    ppermute x12, waiting for transfers between devices, moved(): return lax.ppermute(value, ('row', 'col'), pairs)  15.5 us
    pallas_call x1, Pallas kernels, local(): call(far_kernel, 'far', [f32(*shape)] * 2, [smem] * 3 + [hbm] + [vmem] *...  2.71 us
    another operation x4, local copies, waits for them, and re-layouts  2.41 us
    pallas_call x1, Pallas kernels, early(): call(edge_kernel, 'edges', [f32(length, extent)] * 2, [smem, smem, smem,...  2.34 us
    pallas_call x1, Pallas kernels, local(): call(near_kernel, 'near', f32(blocks + 1, *every), [smem] * 3 + [hbm] + [...  2.06 us
    pallas_call x1, Pallas kernels, local(): call(front_kernel, 'front', bf16(blocks * pair + SIDE_ROWS, extent), [sme...  1.44 us
    pallas_call x1, Pallas kernels, local(): call(list_kernel, 'lists', [pltpu.SMEM((4, slots + UNROLL), jnp.int32), p...  1.13 us
  transfers between devices with their start and end apart: 12, of which 7 were waited for; matrix products, arithmetic and copies ran while one was open for 6% of the time, Pallas kernels for 11%

profile of v1, /device:TPU:0, one launch (start us, length us, event | category | flops | bytes accessed | tf_op | source)
XLA Modules:
  0.0 48.6 jit_solution(16570814360816953011)
XLA Ops:
  1.1 1.1 %lists.1 = (s32[4,52]{1,0:T(4,128)S(4)}, s32[4]{0:T(128)S(4)}) custom-call(s32[1]{0:T(128)} %bitcast.2.place_ref, s32[48]{0:T(128)} %bitcast.24, s32[48]{0:T(128)} %bitcast.25, s32[1]{0:T(128)} %bitcast.22.count_ref), custom_call_target="tpu_custom_call" | custom-call | bytes 1048576 | tf_op jit(solution)/shard_map/lists/pallas_call | solution.py:384
  2.3 1.4 %front.1 = bf16[528,256]{1,0:T(8,128)(2,1)S(1)} custom-call(s32[1]{0:T(128)} %bitcast.2.place_ref, f32[32,2048]{1,0:T(8,128)} %sources_ref.1, f32[32,2048]{1,0:T(8,128)S(1)} %collective-permute-done.4.other_ref), custom_call_target="tpu_custom_call" | custom-call | bytes 1048576 | tf_op jit(solution)/shard_map/front/pallas_call | solution.py:393
  3.7 2.6 %collective-permute-start.6 = (bf16[528,256]{1,0:T(8,128)(2,1)S(1)}, bf16[528,256]{1,0:T(8,128)(2,1)S(1)}, u32[]{:S(2)}, u32[]{:S(2)}) collective-permute-start(bf16[528,256]{1,0:T(8,128)(2,1)S(1)} %front.1), channel_id=1, source_target_pairs={{0,8},{1,24},{2,0},{3,16},{4,12},{5,28},{6,4},{7,20},{8,9},{9,25},... | collective-permute-start | bytes 811016 | tf_op jit(solution)/shard_map/ppermute | solution.py:340
  6.3 0.7 %collective-permute-start.5 = (bf16[528,256]{1,0:T(8,128)(2,1)S(1)}, bf16[528,256]{1,0:T(8,128)(2,1)S(1)}, u32[]{:S(2)}, u32[]{:S(2)}) collective-permute-start(bf16[528,256]{1,0:T(8,128)(2,1)S(1)} %front.1), channel_id=1, source_target_pairs={{0,0},{1,16},{2,8},{3,24},{4,4},{5,20},{6,12},{7,28},{8,1},{9,17},... | collective-permute-start | bytes 811016 | tf_op jit(solution)/shard_map/ppermute | solution.py:340
  9.4 12.6 %while.36 = (s32[]{:T(128)}, f32[16,256]{1,0:T(8,128)}, f32[16,256]{1,0:T(8,128)}, f32[16,256]{1,0:T(8,128)}, f32[16,256]{1,0:T(8,128)}, /*index=5*/s32[]{:T(128...) while((s32[]{:T(128)}, f32[16,256]{1,0:T(8,128)}, ...), condition=%wide.region_1.2_spmd, body=%wide.region_0.1_spmd.sunk | while | flops 53250 | bytes 1556781 | solution.py:379
  9.4 2.3 %edges.5 = (f32[16,256]{1,0:T(8,128)S(1)}, f32[16,256]{1,0:T(8,128)S(1)}) custom-call(s32[1]{0:T(128)} %bitcast.20._, s32[4,52]{1,0:T(4,128)S(4)} %get-tuple-element.1134.order_ref, s32[4]{0:T(128)S(4)} %get-tuple-element.1135.sizes_ref, bf16[48,256,256]{2,1,0:T(8,128)(2,1)} %get-tuple-element.1136.tiles_ref), custom_call_target="tpu_custom_call" | custom-call | bytes 1048576 | tf_op jit(solution)/shard_map/while/body/edges/pallas_call | solution.py:410
  11.7 1.8 %collective-permute-start = (f32[16,256]{1,0:T(8,128)S(1)}, f32[16,256]{1,0:T(8,128)S(1)}, u32[]{:S(2)}, u32[]{:S(2)}) collective-permute-start(f32[16,256]{1,0:T(8,128)S(1)} %get-tuple-element.1080), channel_id=1, source_target_pairs={{0,4},{1,5},{2,6},{3,7},{4,0},{5,1},{6,2},{7,3},{8,12},{9,13},{10,... | collective-permute-start | bytes 49160 | tf_op jit(solution)/shard_map/while/body/ppermute | solution.py:340
  13.6 1.9 %collective-permute-done = f32[16,256]{1,0:T(8,128)S(1)} collective-permute-done((f32[16,256]{1,0:T(8,128)S(1)}, f32[16,256]{1,0:T(8,128)S(1)}, u32[]{:S(2)}, u32[]{:S(2)}) %collective-permute-start) | collective-permute-done | bytes 16416 | tf_op jit(solution)/shard_map/while/body/ppermute | solution.py:340
  15.6 3.9 %collective-permute-start.1 = (f32[16,256]{1,0:T(8,128)S(1)}, f32[16,256]{1,0:T(8,128)S(1)}, u32[]{:S(2)}, u32[]{:S(2)}) collective-permute-start(f32[16,256]{1,0:T(8,128)S(1)} %pad_maximum_fusion.2), channel_id=1, source_target_pairs={{0,2},{1,3},{2,0},{3,1},{4,6},{5,7},{6,4},{7,5},{8,10},{9,11},{10,... | collective-permute-start | bytes 49160 | tf_op jit(solution)/shard_map/while/body/ppermute | solution.py:340
  19.5 1.8 %collective-permute-done.1 = f32[16,256]{1,0:T(8,128)S(1)} collective-permute-done((f32[16,256]{1,0:T(8,128)S(1)}, f32[16,256]{1,0:T(8,128)S(1)}, u32[]{:S(2)}, u32[]{:S(2)}) %collective-permute-start.1) | collective-permute-done | bytes 16416 | tf_op jit(solution)/shard_map/while/body/ppermute | solution.py:340
  21.3 0.6 %multiply_select_fusion.4 = f32[16,256]{1,0:T(8,128)} fusion(f32[16,256]{1,0:T(8,128)S(1)} %collective-permute-done.1, pred[]{:T(512)} %get-tuple-element.1133, pred[]{:T(512)} %get-tuple-element.1132, f32[6,256]{1,0:T(8,128)S(1)} %slice.34, f32[1,256]{1,0:T(1,128)S(1)} %slice.35, f32[1,256]{1,0:T(1,128)S(1)} %slice.36, f32[8,256]{1,0:T(8,128)S(1)} %slice.37), kind=kLoop, calls=%fused_computation.1.clone.1 | loop fusion | flops 32768 | bytes 49154 | tf_op jit(solution)/shard_map/while/body/jit(_where)/select_n | solution.py:318
  22.1 2.2 %collective-permute-start.9 = (bf16[528,256]{1,0:T(8,128)(2,1)S(1)}, bf16[528,256]{1,0:T(8,128)(2,1)S(1)}, u32[]{:S(2)}, u32[]{:S(2)}) collective-permute-start(bf16[528,256]{1,0:T(8,128)(2,1)S(1)} %collective-permute-done.6.refs_1_), channel_id=1, source_target_pairs={{0,4},{1,5},{2,6},{3,7},{4,0},{5,1},{6,2},{7,3},{8,12},{9,13},{10,... | collective-permute-start | bytes 811016 | tf_op jit(solution)/shard_map/ppermute | solution.py:340
  24.4 2.1 %near.1.near_ref = f32[9,128,256]{2,1,0:T(8,128)S(1)} custom-call(s32[1]{0:T(128)} %bitcast.2.place_ref, s32[4,52]{1,0:T(4,128)S(4)} %get-tuple-element.1106.order_ref, s32[4]{0:T(128)S(4)} %get-tuple-element.1107.sizes_ref, bf16[48,256,256]{2,1,0:T(8,128)(2,1)} %get-tuple-element.1194, bf16[528,256]{1,0:T(8,128)(2,1)S(1)} %collective-permute-done.5.refs_0_, ...), custom_call_target="tpu_custom_call" | custom-call | bytes 1048576 | tf_op jit(solution)/shard_map/near/pallas_call | solution.py:469
  26.5 8.7 %while.37 = (s32[]{:T(128)}, f32[16,256]{1,0:T(8,128)S(1)}, f32[16,256]{1,0:T(8,128)S(1)}, s32[]{:T(128)}, s32[1]{0:T(128)}, /*index=5*/f32[16,256]{1,0:T(8,128)...) while((s32[]{:T(128)}, f32[16,256]{1,0:T(8,128)S(1)}, ...), condition=%wide.region_3.4_spmd, body=%wide.region_2.3_spmd.sunk | while | flops 57346 | bytes 1327313 | solution.py:379
  26.6 2.4 %collective-permute-start.2 = (f32[16,256]{1,0:T(8,128)S(1)}, f32[16,256]{1,0:T(8,128)S(1)}, u32[]{:S(2)}, u32[]{:S(2)}) collective-permute-start(f32[16,256]{1,0:T(8,128)S(1)} %get-tuple-element.1097), channel_id=1, source_target_pairs={{0,16},{1,17},{2,18},{3,19},{4,20},{5,21},{6,22},{7,23},{8,24},{9,... | collective-permute-start | bytes 49160 | tf_op jit(solution)/shard_map/while/body/ppermute | solution.py:340
  29.0 2.3 %collective-permute-done.2 = f32[16,256]{1,0:T(8,128)S(1)} collective-permute-done((f32[16,256]{1,0:T(8,128)S(1)}, f32[16,256]{1,0:T(8,128)S(1)}, u32[]{:S(2)}, u32[]{:S(2)}) %collective-permute-start.2) | collective-permute-done | bytes 16416 | tf_op jit(solution)/shard_map/while/body/ppermute | solution.py:340
  31.3 2.2 %collective-permute-start.3 = (f32[16,256]{1,0:T(8,128)S(1)}, f32[16,256]{1,0:T(8,128)S(1)}, u32[]{:S(2)}, u32[]{:S(2)}) collective-permute-start(f32[16,256]{1,0:T(8,128)S(1)} %multiply_select_fusion.5), channel_id=1, source_target_pairs={{0,8},{1,9},{2,10},{3,11},{4,12},{5,13},{6,14},{7,15},{8,0},{9,1},... | collective-permute-start | bytes 49160 | tf_op jit(solution)/shard_map/while/body/ppermute | solution.py:340
  33.5 1.7 %collective-permute-done.3 = f32[16,256]{1,0:T(8,128)S(1)} collective-permute-done((f32[16,256]{1,0:T(8,128)S(1)}, f32[16,256]{1,0:T(8,128)S(1)}, u32[]{:S(2)}, u32[]{:S(2)}) %collective-permute-start.3) | collective-permute-done | bytes 16416 | tf_op jit(solution)/shard_map/while/body/ppermute | solution.py:340
  35.2 1.9 %collective-permute-done.8.refs_2_ = bf16[528,256]{1,0:T(8,128)(2,1)S(1)} collective-permute-done((bf16[528,256]{1,0:T(8,128)(2,1)S(1)}, bf16[528,256]{1,0:T(8,128)(2,1)S(1)}, u32[]{:S(2)}, u32[]{:S(2)}) %collective-permute-start.8) | collective-permute-done | bytes 270368 | tf_op jit(solution)/shard_map/ppermute | solution.py:340
  37.1 2.7 %far.1 = (f32[2,8,32,256]{3,2,1,0:T(8,128)S(1)}, f32[2,8,32,256]{3,2,1,0:T(8,128)S(1)}) custom-call(s32[1]{0:T(128)} %bitcast.2.place_ref, s32[4,52]{1,0:T(4,128)S(4)} %get-tuple-element.1106.order_ref, s32[4]{0:T(128)S(4)} %get-tuple-element.1107.sizes_ref, bf16[48,256,256]{2,1,0:T(8,128)(2,1)} %get-tuple-element.1194, f32[9,128,256]{2,1,0:T(8,128)S(1)} %near.1.near_ref, ...), custom_call_target="tpu_custom_call" | custom-call | bytes 1048576 | tf_op jit(solution)/shard_map/far/pallas_call | solution.py:482
  39.9 1.9 %collective-permute-done.10.arrived_ref = f32[2,8,32,256]{3,2,1,0:T(8,128)S(1)} collective-permute-done((f32[2,8,32,256]{3,2,1,0:T(8,128)S(1)}, f32[2,8,32,256]{3,2,1,0:T(8,128)S(1)}, u32[]{:S(2)}, u32[]{:S(2)}) %collective-permute-start.10) | collective-permute-done | bytes 524320 | tf_op jit(solution)/shard_map/ppermute | solution.py:340
  41.8 1.7 %collective-permute-start.11 = (bf16[8,32,256]{2,1,0:T(8,128)(2,1)S(1)}, bf16[8,32,256]{2,1,0:T(8,128)(2,1)S(1)}, u32[]{:S(2)}, u32[]{:S(2)}) collective-permute-start(bf16[8,32,256]{2,1,0:T(8,128)(2,1)S(1)} %get-tuple-element.885), channel_id=1, source_target_pairs={{0,2},{1,3},{2,0},{3,1},{4,6},{5,7},{6,4},{7,5},{8,10},{9,11},{10,... | collective-permute-start | bytes 393224 | tf_op jit(solution)/shard_map/ppermute | solution.py:340
  43.5 4.0 %collective-permute-done.11.refs_0_ = bf16[8,32,256]{2,1,0:T(8,128)(2,1)S(1)} collective-permute-done((bf16[8,32,256]{2,1,0:T(8,128)(2,1)S(1)}, bf16[8,32,256]{2,1,0:T(8,128)(2,1)S(1)}, u32[]{:S(2)}, u32[]{:S(2)}) %collective-permute-start.11) | collective-permute-done | bytes 131104 | tf_op jit(solution)/shard_map/ppermute | solution.py:340
  47.5 1.1 %back.1 = f32[32,2048]{1,0:T(8,128)} custom-call(f32[8,32,256]{2,1,0:T(8,128)S(1)} %get-tuple-element.884.own_ref, bf16[8,32,256]{2,1,0:T(8,128)(2,1)S(1)} %collective-permute-done.11.refs_0_), custom_call_target="tpu_custom_call" | custom-call | bytes 1048576 | tf_op jit(solution)/shard_map/back/pallas_call | solution.py:510
  (38 shorter events, 3.3 us)
Async XLA Ops:
  0.0 2.3 %collective-permute-start.4 = (f32[32,2048]{1,0:T(8,128)}, f32[32,2048]{1,0:T(8,128)S(1)}, u32[]{:S(2)}, u32[]{:S(2)}) collective-permute-start(f32[32,2048]{1,0:T(8,128)} %sources_ref.1), channel_id=1, source_target_pairs={{0,1},{1,0},{2,3},{3,2},{4,5},{5,4},{6,7},{7,6},{8,9},{9,8},{10,11... | collective-permute-start | bytes 786440 | tf_op jit(solution)/shard_map/ppermute | solution.py:340
  3.7 18.4 %collective-permute-start.6 = (bf16[528,256]{1,0:T(8,128)(2,1)S(1)}, bf16[528,256]{1,0:T(8,128)(2,1)S(1)}, u32[]{:S(2)}, u32[]{:S(2)}) collective-permute-start(bf16[528,256]{1,0:T(8,128)(2,1)S(1)} %front.1), channel_id=1, source_target_pairs={{0,8},{1,24},{2,0},{3,16},{4,12},{5,28},{6,4},{7,20},{8,9},{9,25},... | collective-permute-start | bytes 811016 | tf_op jit(solution)/shard_map/ppermute | solution.py:340
  6.3 15.7 %collective-permute-start.5 = (bf16[528,256]{1,0:T(8,128)(2,1)S(1)}, bf16[528,256]{1,0:T(8,128)(2,1)S(1)}, u32[]{:S(2)}, u32[]{:S(2)}) collective-permute-start(bf16[528,256]{1,0:T(8,128)(2,1)S(1)} %front.1), channel_id=1, source_target_pairs={{0,0},{1,16},{2,8},{3,24},{4,4},{5,20},{6,12},{7,28},{8,1},{9,17},... | collective-permute-start | bytes 811016 | tf_op jit(solution)/shard_map/ppermute | solution.py:340
  11.7 10.2 %copy-start = (f32[16,256]{1,0:T(8,128)}, f32[16,256]{1,0:T(8,128)S(1)}, u32[]{:S(2)}) copy-start(f32[16,256]{1,0:T(8,128)S(1)} %get-tuple-element.1128) | copy-start | bytes 49156 | tf_op jit(solution)/shard_map/while
  11.7 3.8 %collective-permute-start = (f32[16,256]{1,0:T(8,128)S(1)}, f32[16,256]{1,0:T(8,128)S(1)}, u32[]{:S(2)}, u32[]{:S(2)}) collective-permute-start(f32[16,256]{1,0:T(8,128)S(1)} %get-tuple-element.1080), channel_id=1, source_target_pairs={{0,4},{1,5},{2,6},{3,7},{4,0},{5,1},{6,2},{7,3},{8,12},{9,13},{10,... | collective-permute-start | bytes 49160 | tf_op jit(solution)/shard_map/while/body/ppermute | solution.py:340
  15.5 6.4 %copy-start.2 = (f32[16,256]{1,0:T(8,128)}, f32[16,256]{1,0:T(8,128)S(1)}, u32[]{:S(2)}) copy-start(f32[16,256]{1,0:T(8,128)S(1)} %get-tuple-element.1129) | copy-start | bytes 49156 | tf_op jit(solution)/shard_map/while
  15.5 6.4 %copy-start.4 = (f32[16,256]{1,0:T(8,128)}, f32[16,256]{1,0:T(8,128)S(1)}, u32[]{:S(2)}) copy-start(f32[16,256]{1,0:T(8,128)S(1)} %get-tuple-element.1130) | copy-start | bytes 49156 | tf_op jit(solution)/shard_map/while
  15.6 5.7 %collective-permute-start.1 = (f32[16,256]{1,0:T(8,128)S(1)}, f32[16,256]{1,0:T(8,128)S(1)}, u32[]{:S(2)}, u32[]{:S(2)}) collective-permute-start(f32[16,256]{1,0:T(8,128)S(1)} %pad_maximum_fusion.2), channel_id=1, source_target_pairs={{0,2},{1,3},{2,0},{3,1},{4,6},{5,7},{6,4},{7,5},{8,10},{9,11},{10,... | collective-permute-start | bytes 49160 | tf_op jit(solution)/shard_map/while/body/ppermute | solution.py:340
  21.9 4.5 %copy-start.1 = (f32[16,256]{1,0:T(8,128)S(1)}, f32[16,256]{1,0:T(8,128)}, u32[]{:S(2)}) copy-start(f32[16,256]{1,0:T(8,128)} %get-tuple-element.1141) | copy-start | bytes 49156
  21.9 4.5 %copy-start.3 = (f32[16,256]{1,0:T(8,128)S(1)}, f32[16,256]{1,0:T(8,128)}, u32[]{:S(2)}) copy-start(f32[16,256]{1,0:T(8,128)} %get-tuple-element.1142) | copy-start | bytes 49156
  21.9 4.5 %copy-start.5 = (f32[16,256]{1,0:T(8,128)S(1)}, f32[16,256]{1,0:T(8,128)}, u32[]{:S(2)}) copy-start(f32[16,256]{1,0:T(8,128)} %get-tuple-element.1147) | copy-start | bytes 49156
  21.9 4.5 %copy-start.6 = (f32[16,256]{1,0:T(8,128)S(1)}, f32[16,256]{1,0:T(8,128)}, u32[]{:S(2)}) copy-start(f32[16,256]{1,0:T(8,128)} %get-tuple-element.1145) | copy-start | bytes 49156
  22.0 4.5 %collective-permute-start.7 = (f32[16,256]{1,0:T(8,128)}, f32[16,256]{1,0:T(8,128)S(1)}, u32[]{:S(2)}, u32[]{:S(2)}) collective-permute-start(f32[16,256]{1,0:T(8,128)} %get-tuple-element.1145), channel_id=1, source_target_pairs={{0,1},{1,0},{2,3},{3,2},{4,5},{5,4},{6,7},{7,6},{8,9},{9,8},{10,11... | collective-permute-start | bytes 49160 | tf_op jit(solution)/shard_map/while/body/ppermute | solution.py:340
  22.1 13.1 %collective-permute-start.9 = (bf16[528,256]{1,0:T(8,128)(2,1)S(1)}, bf16[528,256]{1,0:T(8,128)(2,1)S(1)}, u32[]{:S(2)}, u32[]{:S(2)}) collective-permute-start(bf16[528,256]{1,0:T(8,128)(2,1)S(1)} %collective-permute-done.6.refs_1_), channel_id=1, source_target_pairs={{0,4},{1,5},{2,6},{3,7},{4,0},{5,1},{6,2},{7,3},{8,12},{9,13},{10,... | collective-permute-start | bytes 811016 | tf_op jit(solution)/shard_map/ppermute | solution.py:340
  24.3 12.8 %collective-permute-start.8 = (bf16[528,256]{1,0:T(8,128)(2,1)S(1)}, bf16[528,256]{1,0:T(8,128)(2,1)S(1)}, u32[]{:S(2)}, u32[]{:S(2)}) collective-permute-start(bf16[528,256]{1,0:T(8,128)(2,1)S(1)} %collective-permute-done.5.refs_0_), channel_id=1, source_target_pairs={{0,4},{1,5},{2,6},{3,7},{4,0},{5,1},{6,2},{7,3},{8,12},{9,13},{10,... | collective-permute-start | bytes 811016 | tf_op jit(solution)/shard_map/ppermute | solution.py:340
  26.6 4.7 %collective-permute-start.2 = (f32[16,256]{1,0:T(8,128)S(1)}, f32[16,256]{1,0:T(8,128)S(1)}, u32[]{:S(2)}, u32[]{:S(2)}) collective-permute-start(f32[16,256]{1,0:T(8,128)S(1)} %get-tuple-element.1097), channel_id=1, source_target_pairs={{0,16},{1,17},{2,18},{3,19},{4,20},{5,21},{6,22},{7,23},{8,24},{9,... | collective-permute-start | bytes 49160 | tf_op jit(solution)/shard_map/while/body/ppermute | solution.py:340
  31.3 3.9 %collective-permute-start.3 = (f32[16,256]{1,0:T(8,128)S(1)}, f32[16,256]{1,0:T(8,128)S(1)}, u32[]{:S(2)}, u32[]{:S(2)}) collective-permute-start(f32[16,256]{1,0:T(8,128)S(1)} %multiply_select_fusion.5), channel_id=1, source_target_pairs={{0,8},{1,9},{2,10},{3,11},{4,12},{5,13},{6,14},{7,15},{8,0},{9,1},... | collective-permute-start | bytes 49160 | tf_op jit(solution)/shard_map/while/body/ppermute | solution.py:340
  39.8 2.0 %collective-permute-start.10 = (f32[2,8,32,256]{3,2,1,0:T(8,128)S(1)}, f32[2,8,32,256]{3,2,1,0:T(8,128)S(1)}, u32[]{:S(2)}, u32[]{:S(2)}) collective-permute-start(f32[2,8,32,256]{3,2,1,0:T(8,128)S(1)} %get-tuple-element.883), channel_id=1, source_target_pairs={{0,1},{1,0},{2,3},{3,2},{4,5},{5,4},{6,7},{7,6},{8,9},{9,8},{10,11... | collective-permute-start | bytes 1572872 | tf_op jit(solution)/shard_map/ppermute | solution.py:340
  41.8 5.7 %collective-permute-start.11 = (bf16[8,32,256]{2,1,0:T(8,128)(2,1)S(1)}, bf16[8,32,256]{2,1,0:T(8,128)(2,1)S(1)}, u32[]{:S(2)}, u32[]{:S(2)}) collective-permute-start(bf16[8,32,256]{2,1,0:T(8,128)(2,1)S(1)} %get-tuple-element.885), channel_id=1, source_target_pairs={{0,2},{1,3},{2,0},{3,1},{4,6},{5,7},{6,4},{7,5},{8,10},{9,11},{10,... | collective-permute-start | bytes 393224 | tf_op jit(solution)/shard_map/ppermute | solution.py:340

commit v2 on v1

--- a/solution.py
+++ b/solution.py
@@ -11,6 +11,7 @@
 ROOT_HALF = 1.0 / math.sqrt(2.0)
 SIDE_ROWS = 16
 UNROLL = 4
+LANES = 128
 MIB = 2**20
 
 
@@ -78,11 +79,15 @@
     return (place_ref[0] >> 8) & 255
 
 
+def z_of(place_ref):
+    return place_ref[0] >> 16
+
+
 def source_span(place_ref, m, spans):
-    return lax.rem((place_ref[0] >> 16) - m + spans * 256, spans)
-
-
-def front_kernel(place_ref, sources_ref, other_ref, out_ref, mine_ref, sem, *, blocks, extent):
+    return lax.rem(z_of(place_ref) - m + spans * 256, spans)
+
+
+def front_kernel(place_ref, sources_ref, other_ref, _, out_ref, mine_ref, sem, *, blocks, extent):
     copy = pltpu.make_async_copy(sources_ref, mine_ref, sem)
     copy.start()
     height = mine_ref.shape[0]
@@ -113,7 +118,11 @@
     out_ref[blocks * pair :, 0:pair] = side.astype(jnp.bfloat16)
 
 
-def list_kernel(place_ref, rows_ref, cols_ref, count_ref, order_ref, sizes_ref, *, blocks, owners):
+def list_kernel(
+    place_ref, rows_ref, cols_ref, count_ref, order_ref, sizes_ref, lead_ref, others_ref, *, blocks, owners
+):
+    lead_ref[...] = jnp.zeros_like(lead_ref)
+    others_ref[...] = jnp.zeros_like(others_ref)
     x = x_of(place_ref)
 
     def visit(slot, sizes):
@@ -144,22 +153,22 @@
             order_ref[which, sizes[which] + k] = blocks
 
 
-def edge_kernel(_, order_ref, sizes_ref, tiles_ref, cols_ref, line_ref, strips, held, strip_sems, held_sems):
-    extent = tiles_ref.shape[-1]
-
+def edge_kernel(
+    _, order_ref, sizes_ref, tiles_ref, cols_ref, line_ref, strips, columns, summed, strip_sems, column_sems
+):
     def strip_copy(index):
         slot = order_ref[3, index] >> 16
         return pltpu.make_async_copy(tiles_ref.at[slot, 0:SIDE_ROWS, :], strips.at[index], strip_sems.at[index])
 
-    def tile_copy(index):
+    def column_copy(index):
         slot = order_ref[2, index] >> 16
-        return pltpu.make_async_copy(tiles_ref.at[slot], held.at[index], held_sems.at[index])
-
-    lax.fori_loop(0, sizes_ref[2], lambda i, _: (tile_copy(i).start(), 0)[1], 0)
+        return pltpu.make_async_copy(tiles_ref.at[slot, :, 0:LANES], columns.at[index], column_sems.at[index])
+
+    lax.fori_loop(0, sizes_ref[2], lambda i, _: (column_copy(i).start(), 0)[1], 0)
     lax.fori_loop(0, sizes_ref[3], lambda i, _: (strip_copy(i).start(), 0)[1], 0)
     cols_ref[...] = jnp.zeros_like(cols_ref)
-    line_ref[...] = jnp.zeros_like(line_ref)
-    pick = (lax.broadcasted_iota(jnp.int32, (SIDE_ROWS, extent), 1) == 0).astype(jnp.bfloat16)
+    summed[...] = jnp.zeros_like(summed)
+    lane = lax.broadcasted_iota(jnp.int32, summed.shape, 1)
 
     def add_strip(index, _):
         entry = order_ref[3, index]
@@ -169,33 +178,85 @@
         return 0
 
     def add_column(index, _):
-        tile_copy(index).wait()
-        column = lax.dot_general(pick, held[index], (((1,), (1,)), ((), ())), preferred_element_type=jnp.float32)
-        line_ref[pl.ds((order_ref[2, index] >> 8) & 255, 1), :] += column[0:1, :]
+        column_copy(index).wait()
+        column = columns[index].astype(jnp.float32)[:, 0:1]
+        summed[...] += jnp.where(lane == ((order_ref[2, index] >> 8) & 255), column, 0.0)
         return 0
 
     lax.fori_loop(0, sizes_ref[3], add_strip, 0)
     lax.fori_loop(0, sizes_ref[2], add_column, 0)
-
-
-def corner_kernel(place_ref, lead_ref, partner_ref, cols_ref, *refs, blocks, owners):
-    lines, (out_ref, line_ref, rest_ref) = refs[:owners], refs[owners:]
-    lead, partner = lead_ref[...], partner_ref[...]
-    lead = jnp.where(core_of(place_ref) == 1, partner - lead, partner + lead) * ROOT_HALF
+    line_ref[...] = jnp.transpose(summed[...])[0 : line_ref.shape[0], :]
+
+
+def butterfly(value, partner, index, bit):
+    active = lax.rem(index, 2**bit) == 0
+    upper = ((index >> bit) & 1) == 1
+    return jnp.where(active, jnp.where(upper, partner - value, partner + value) * ROOT_HALF, value)
+
+
+def pack_kernel(cols_ref, *refs, blocks):
+    lines, lead_ref = refs[:-1], refs[-1]
+    lead_ref[...] = jnp.zeros_like(lead_ref)
+    lead_ref[0:blocks, :] = cols_ref[0:blocks, :]
+    for j, line in enumerate(lines):
+        lead_ref[blocks + j : blocks + j + 1, :] = line[0:1, :]
+
+
+def col_level_kernel(place_ref, value_ref, partner_ref, out_ref, *, bit):
+    index = 2 * span_of(place_ref) + core_of(place_ref)
+    out_ref[...] = butterfly(value_ref[...], partner_ref[...], index, bit)
+
+
+def join_kernel(*refs):
+    *parts, out_ref = refs
+    at = 0
+    for part in parts:
+        out_ref[at : at + part.shape[0], :] = part[...]
+        at += part.shape[0]
+
+
+def row_level_kernel(place_ref, value_ref, partner_ref, out_ref, *, bit):
+    out_ref[...] = butterfly(value_ref[...], partner_ref[...], z_of(place_ref), bit)
+
+
+def x_levels_kernel(place_ref, cols_ref, line_ref, rest_ref, out_ref):
+    x = x_of(place_ref)
+    by_x = block_inverse([line_ref[...]] + [rest_ref[i] for i in range(rest_ref.shape[0])])
+    value = by_x[0]
+    for i in range(1, len(by_x)):
+        value = jnp.where(x == i, by_x[i], value)
+    length = value.shape[0]
+    out_ref[0:length, :] = cols_ref[...]
+    out_ref[length : 2 * length, :] = value
+    out_ref[2 * length :, :] = jnp.zeros((out_ref.shape[0] - 2 * length, value.shape[1]), jnp.float32)
+
+
+def corner_kernel(place_ref, lead_ref, partner_ref, others_ref, out_ref, line_ref, rest_ref, *, blocks, owners):
+    x = x_of(place_ref)
+    length = owners * blocks
+    cols_ref = others_ref.at[0:length]
+    behind = [others_ref.at[(j + 1) * length : (j + 2) * length] for j in range(owners)]
+    lead = butterfly(lead_ref[...], partner_ref[...], core_of(place_ref), 0)
     columns = [lead[0:blocks, :]] + [cols_ref[i * blocks : (i + 1) * blocks, :] for i in range(1, owners)]
     for i, column in enumerate(block_inverse(columns)):
         out_ref[i * blocks : (i + 1) * blocks, :] = column
     index = lax.broadcasted_iota(jnp.int32, line_ref.shape, 0)
     lane = lax.broadcasted_iota(jnp.int32, line_ref.shape, 1)
-    for x in range(owners):
-        line = lines[x][...]
-        corner = [lead[blocks + x : blocks + x + 1, :]] + [line[i * blocks : i * blocks + 1, :] for i in range(1, owners)]
+    fixed = []
+    for j in range(owners):
+        line = behind[j][...]
+        corner = [lead[blocks + j : blocks + j + 1, :]] + [line[i * blocks : i * blocks + 1, :] for i in range(1, owners)]
         for i, value in enumerate(block_inverse(corner)):
             line = jnp.where((index == i * blocks) & (lane == 0), value[:, 0:1], line)
-        if x == 0:
+        fixed.append(line)
+    for i in range(owners):
+        line = fixed[0]
+        for j in range(1, owners):
+            line = jnp.where(lax.rem(x - i + owners, owners) == j, fixed[j], line)
+        if i == 0:
             line_ref[...] = line
         else:
-            rest_ref[x - 1] = line
+            rest_ref[i - 1] = line
 
 
 def fill_sides(sides, messages, place_ref, blocks, spans):
@@ -207,45 +268,51 @@
             sides[behind * blocks + b, rows, :] = message[b * pair : (b + 1) * pair, :]
 
 
-def start_tiles(order_ref, sizes_ref, which, tiles_ref, held, sems):
-    def start(index, _):
+def add_products(order_ref, sizes_ref, which, first, tiles_ref, sides, acc, sems=None):
+    def group(index, _):
+        if sems is not None:
+            for k in range(UNROLL):
+                at = first + index * UNROLL + k
+                pltpu.make_async_copy(tiles_ref.at[at], tiles_ref.at[at], sems.at[at]).wait()
+        for k in range(UNROLL):
+            entry = order_ref[which, index * UNROLL + k]
+            side, row = (entry >> 8) & 255, entry & 255
+            tile = tiles_ref[first + index * UNROLL + k]
+            acc[row] += jnp.dot(sides[side], tile, preferred_element_type=jnp.float32)
+        return 0
+
+    lax.fori_loop(0, groups_of(sizes_ref, which), group, 0)
+
+
+def groups_of(sizes_ref, which):
+    return (sizes_ref[which] + UNROLL - 1) // UNROLL
+
+
+def near_kernel(place_ref, order_ref, sizes_ref, tiles_ref, _, *refs, blocks, spans):
+    *messages, acc_ref, held_ref, sides, sems = refs
+    near_places = groups_of(sizes_ref, 0) * UNROLL
+    far_places = groups_of(sizes_ref, 1) * UNROLL
+
+    def fetch(which, index, at):
         slot = order_ref[which, index] >> 16
-        pltpu.make_async_copy(tiles_ref.at[slot], held.at[index], sems.at[index]).start()
-        return 0
-
-    lax.fori_loop(0, (sizes_ref[which] + UNROLL - 1) // UNROLL * UNROLL, start, 0)
-
-
-def add_products(order_ref, sizes_ref, which, tiles_ref, held, sems, sides, acc):
-    def group(index, _):
-        for k in range(UNROLL):
-            at = index * UNROLL + k
-            pltpu.make_async_copy(tiles_ref.at[0], held.at[at], sems.at[at]).wait()
-        for k in range(UNROLL):
-            at = index * UNROLL + k
-            entry = order_ref[which, at]
-            side, row = (entry >> 8) & 255, entry & 255
-            acc[row] += jnp.dot(sides[side], held[at], preferred_element_type=jnp.float32)
-        return 0
-
-    lax.fori_loop(0, (sizes_ref[which] + UNROLL - 1) // UNROLL, group, 0)
-
-
-def near_kernel(place_ref, order_ref, sizes_ref, tiles_ref, *refs, blocks, spans):
-    *messages, acc_ref, sides, held, sems = refs
-    start_tiles(order_ref, sizes_ref, 0, tiles_ref, held, sems)
+        return pltpu.make_async_copy(tiles_ref.at[slot], held_ref.at[at], sems.at[at])
+
+    lax.fori_loop(0, near_places, lambda i, _: (fetch(0, i, i).start(), 0)[1], 0)
+    lax.fori_loop(0, far_places, lambda i, _: (fetch(1, i, near_places + i).start(), 0)[1], 0)
     fill_sides(sides, messages, place_ref, blocks, spans)
     acc_ref[...] = jnp.zeros_like(acc_ref)
-    add_products(order_ref, sizes_ref, 0, tiles_ref, held, sems, sides, acc_ref)
-
-
-def far_kernel(place_ref, order_ref, sizes_ref, tiles_ref, near_ref, cols_ref, row_ref, *refs, blocks, owners, spans):
+    add_products(order_ref, sizes_ref, 0, 0, held_ref, sides, acc_ref, sems)
+    lax.fori_loop(0, far_places, lambda i, _: (fetch(1, i, near_places + i).wait(), 0)[1], 0)
+
+
+def far_kernel(place_ref, order_ref, sizes_ref, tiles_ref, near_ref, others_ref, *refs, blocks, owners, spans):
     direct, swapped = refs[:spans], refs[spans : owners * spans]
-    keep_ref, send_ref, sides, acc, firsts, held, sems = refs[owners * spans :]
-    start_tiles(order_ref, sizes_ref, 1, tiles_ref, held, sems)
+    keep_ref, send_ref, sides, acc, firsts = refs[owners * spans :]
     extent = tiles_ref.shape[-1]
     pair = sides.shape[1] // spans
     height = pair // 2
+    length = owners * blocks
+    cols_ref, row_ref = others_ref.at[0:length], others_ref.at[length : 2 * length]
     x = x_of(place_ref)
     fill_sides(sides, swapped, place_ref, blocks, spans)
     messages = (*direct, *swapped)
@@ -260,7 +327,7 @@
         for owner in range(owners):
             total += firsts[owner][:, 0:1] * cols_ref[owner * blocks + i : owner * blocks + i + 1, :]
         acc[i] = total
-    add_products(order_ref, sizes_ref, 1, tiles_ref, held, sems, sides, acc)
+    add_products(order_ref, sizes_ref, 1, groups_of(sizes_ref, 0) * UNROLL, tiles_ref, sides, acc)
 
     lane = lax.broadcasted_iota(jnp.int32, (pair, extent), 1)
     for m in range(spans):
@@ -311,13 +378,6 @@
         out_ref[:, b * extent : (b + 1) * extent] = result[b * height : (b + 1) * height, :]
 
 
-def butterfly(value, partner, index, bit):
-    active = index % 2**bit == 0
-    upper = index // 2**bit % 2 == 1
-    combined = jnp.where(upper, partner - value, partner + value) * ROOT_HALF
-    return jnp.where(active, combined, value)
-
-
 def local(sources, tiles, tile_row, tile_col, tile_count):
     n_row, n_col = lax.axis_size("row"), lax.axis_size("col")
     owners = n_row // n_col
@@ -348,17 +408,19 @@
     smem = pl.BlockSpec(memory_space=pltpu.SMEM)
     vmem = pl.BlockSpec(memory_space=pltpu.VMEM)
     hbm = pl.BlockSpec(memory_space=pltpu.HBM)
-
-    def call(kernel, name, out_shape, in_specs, out_specs, limit=16, scratch=(), flops=0, moved_bytes=MIB, **sizes):
+    unread = pl.BlockSpec(memory_space=pl.ANY)
+
+    def call(kernel, name, out_shape, in_specs, out_specs, limit=16, scratch=(), aliases=None, **sizes):
         return pl.pallas_call(
             functools.partial(kernel, **sizes) if sizes else kernel,
             out_shape=out_shape,
             in_specs=in_specs,
             out_specs=out_specs,
             scratch_shapes=scratch,
+            input_output_aliases=aliases or {},
             name=name,
             compiler_params=pltpu.CompilerParams(vmem_limit_bytes=int(limit * MIB)),
-            cost_estimate=pl.CostEstimate(flops=flops, bytes_accessed=moved_bytes, transcendentals=0),
+            cost_estimate=pl.CostEstimate(flops=0, bytes_accessed=MIB, transcendentals=0),
         )
 
     def in_hbm(value):
@@ -367,6 +429,9 @@
     def f32(*dims):
         return jax.ShapeDtypeStruct(dims, jnp.float32)
 
+    def kept(*dims):
+        return pltpu.VMEM(dims, jnp.float32)
+
     def bf16(*dims):
         return jax.ShapeDtypeStruct(dims, jnp.bfloat16)
 
@@ -375,18 +440,23 @@
     def after(value, *others):
         return lax.optimization_barrier((value, *others))[0]
 
-    def apart(body, state):
-        return lax.fori_loop(0, jnp.minimum(tile_count.reshape(()), 1), body, tuple(state))
+    def apart(body, *state):
+        return lax.fori_loop(0, jnp.minimum(tile_count.reshape(()), 1), body, state)
 
     length = owners * blocks
-    stack = tiles.reshape(slots, extent, extent)
+    stack = in_hbm(tiles.reshape(slots, extent, extent))
     from_core = other_core(sources)
-    order, sizes = call(
+    order, sizes, blank_lead, blank = call(
         list_kernel,
         "lists",
-        [pltpu.SMEM((4, slots + UNROLL), jnp.int32), pltpu.SMEM((4,), jnp.int32)],
+        [
+            pltpu.SMEM((4, slots + UNROLL), jnp.int32),
+            pltpu.SMEM((4,), jnp.int32),
+            kept(2 * blocks, extent),
+            kept((owners + 1) * length, extent),
+        ],
         [smem] * 4,
-        [smem] * 2,
+        [smem] * 2 + [vmem] * 2,
         blocks=blocks,
         owners=owners,
     )(place, in_hbm(tile_row.reshape(-1)), in_hbm(tile_col.reshape(-1)), tile_count.reshape(1))
@@ -394,108 +464,103 @@
         front_kernel,
         "front",
         bf16(blocks * pair + SIDE_ROWS, extent),
-        [smem, hbm, vmem],
+        [smem, hbm, vmem, unread],
         vmem,
         scratch=[pltpu.VMEM(sources.shape, jnp.float32), pltpu.SemaphoreType.DMA],
         blocks=blocks,
         extent=extent,
-    )(place, in_hbm(sources), from_core)
+    )(place, in_hbm(sources), from_core, blank)
 
     direct = [
         moved(message, lambda zz, xx, yy, cc, m=m: (cc * spans + (yy + m) % spans, xx, zz // 2, zz % 2))
         for m in range(spans)
     ]
+
+    def col_level(value, bit):
+        if bit == 0:
+            return other_core(value)
+        step = 2 ** (bit - 1)
+        return moved(value, lambda zz, xx, yy, cc: (zz, xx, yy ^ step, cc))
 
     def early(trip, _):
         cols, line = call(
             edge_kernel,
             "edges",
             [f32(length, extent)] * 2,
-            [smem, smem, smem, hbm],
+            [smem] * 3 + [hbm],
             [vmem] * 2,
             scratch=[
                 pltpu.VMEM((slots, SIDE_ROWS, extent), jnp.bfloat16),
-                pltpu.VMEM((slots, extent, extent), jnp.bfloat16),
+                pltpu.VMEM((slots, extent, LANES), jnp.bfloat16),
+                pltpu.VMEM((extent, LANES), jnp.float32),
                 pltpu.SemaphoreType.DMA((slots,)),
                 pltpu.SemaphoreType.DMA((slots,)),
             ],
-        )(trip.reshape(1), order, sizes, in_hbm(stack))
+        )(trip.reshape(1), order, sizes, stack)
         behind = [line] + [along_x(line, j) for j in range(1, owners)]
-        lines = []
-        for i in range(owners):
-            value = behind[0]
-            for j in range(1, owners):
-                value = jnp.where((x - i) % owners == j, behind[j], value)
-            lines.append(value)
-        lead = jnp.concatenate([cols[0:blocks]] + [value[0:1] for value in lines] + [cols[0 : blocks - owners]])
+        lead = call(pack_kernel, "pack", f32(2 * blocks, extent), [vmem] * (1 + owners), vmem, blocks=blocks)(cols, *behind)
+        others = call(join_kernel, "join", kept(*blank.shape), [vmem] * (1 + owners), vmem)(cols, *behind)
         for bit in reversed(range(1, n_col.bit_length() - 1)):
-            step = 2 ** (bit - 1)
-            partner = moved(lead, lambda zz, xx, yy, cc, step=step: (zz, xx, yy ^ step, cc))
-            lead = butterfly(lead, partner, col_index, bit)
-        return (lead, cols, *lines)
-
-    sized = [jnp.zeros((2 * blocks, extent), jnp.float32)] + [jnp.zeros((length, extent), jnp.float32)] * (1 + owners)
-    lead, cols, *lines = apart(early, sized)
+            lead = call(col_level_kernel, "col_level", kept(2 * blocks, extent), [smem, vmem, vmem], vmem, bit=bit)(
+                place, lead, col_level(lead, bit)
+            )
+        return lead, others
+
+    lead, others = apart(early, blank_lead, blank)
     swapped = [along_x(after(piece, lead), j) for j in range(1, owners) for piece in direct]
-    lead = after(lead, direct[0])
 
     def late(_, state):
-        lead, cols, *lines = state
+        lead, others = state
         first_cols, line, rest = call(
             corner_kernel,
             "corner",
             [f32(length, extent)] * 2 + [f32(owners - 1, length, extent)],
-            [smem] + [vmem] * (3 + owners),
+            [smem] + [vmem] * 3,
             [vmem] * 3,
             blocks=blocks,
             owners=owners,
-        )(place, lead, other_core(lead), cols, *lines)
+        )(place, lead, col_level(lead, 0), others)
         for bit in reversed(range((n_row // owners).bit_length() - 1)):
             partner = moved(line, lambda zz, xx, yy, cc, bit=bit: (zz ^ 2**bit, xx, yy, cc))
-            line = butterfly(line, partner, z, bit)
-        by_x = block_inverse([line] + [rest[i] for i in range(owners - 1)])
-        first_row = by_x[0]
-        for i in range(1, owners):
-            first_row = jnp.where(x == i, by_x[i], first_row)
-        return (lead, first_cols, first_row, *lines[1:])
-
-    _, first_cols, first_row, *_ = apart(late, [lead, cols, *lines])
+            line = call(row_level_kernel, "row_level", f32(length, extent), [smem, vmem, vmem], vmem, bit=bit)(
+                place, line, partner
+            )
+        others = call(x_levels_kernel, "x_levels", kept(*blank.shape), [smem, vmem, vmem, vmem], vmem)(
+            place, first_cols, line, rest
+        )
+        return lead, others
+
+    _, others = apart(late, after(lead, *direct), others)
 
     every = (spans * pair, extent)
-    held_tiles = [
-        pltpu.VMEM((slots + UNROLL, extent, extent), jnp.bfloat16),
-        pltpu.SemaphoreType.DMA((slots + UNROLL,)),
-    ]
-    near = call(
+    places = slots + 2 * UNROLL
+    near, held = call(
         near_kernel,
         "near",
-        f32(blocks + 1, *every),
-        [smem] * 3 + [hbm] + [vmem] * len(direct),
-        vmem,
-        limit=24,
-        scratch=[pltpu.VMEM((blocks, *every), jnp.bfloat16), *held_tiles],
+        [f32(blocks + 1, *every), pltpu.VMEM((places, extent, extent), jnp.bfloat16)],
+        [smem] * 3 + [hbm, unread] + [vmem] * len(direct),
+        [vmem] * 2,
+        scratch=[pltpu.VMEM((blocks, *every), jnp.bfloat16), pltpu.SemaphoreType.DMA((places,))],
         blocks=blocks,
         spans=spans,
-    )(place, order, sizes, in_hbm(stack), *direct)
+    )(place, order, sizes, stack, others, *direct)
 
     shape = (spans, blocks, height, extent)
     keep, send = call(
         far_kernel,
         "far",
         [f32(*shape)] * 2,
-        [smem] * 3 + [hbm] + [vmem] * (3 + len(direct) + len(swapped)),
+        [smem] * 3 + [vmem] * (3 + len(direct) + len(swapped)),
         [vmem] * 2,
-        limit=24,
         scratch=[
             pltpu.VMEM(((owners - 1) * blocks, *every), jnp.bfloat16),
             pltpu.VMEM((blocks + 1, *every), jnp.float32),
             pltpu.VMEM((owners, spans * pair, 128), jnp.float32),
-            *held_tiles,
         ],
         blocks=blocks,
         owners=owners,
         spans=spans,
-    )(place, order, sizes, in_hbm(stack), near, first_cols, first_row, *direct, *swapped)
+    )(place, order, sizes, held, near, others, *direct, *swapped)
 
     own, *outgoing = call(
         combine_kernel,

time: 49.5 us -> 47.7 us (0.964); the launches traced: 48.6 us -> 47.5 us
  waiting for transfers between devices: 15.5 us -> 18.6 us
  local copies, waits for them, and re-layouts: 2.45 us -> 0 us
  Pallas kernels: 10.8 us -> 8.98 us
  starting transfers between devices: 18.2 us -> 19.1 us
  other arithmetic: 0.65 us -> 0 us
    ppermute x12, waiting for transfers between devices: 15.5 us -> 18.6 us  [moved(): return lax.ppermute(value, ('row', 'col'), pairs)]
    another operation x4 -> x0, local copies, waits for them, and re-layouts: 2.41 us -> none
    pallas_call x3 -> x9, Pallas kernels: 7.11 us -> 5.4 us  [the longest x1 2.15 us: local(): call(near_kernel, 'near', [f32(blocks + 1, *every), pltpu.VMEM((places, e...]
    ppermute x12, starting transfers between devices: 18.2 us -> 19.1 us  [moved(): return lax.ppermute(value, ('row', 'col'), pairs)]
    select_n x4 -> x0, other arithmetic: 0.64 us -> none  [the longest x2 0.62 us: butterfly(): return jnp.where(active, combined, value)]
  transfers between devices with their start and end apart: 12 -> 12, of which waited for: 7 -> 7; matrix products, arithmetic and copies ran while one was open for 6% -> 0% of each run, Pallas kernels for 11% -> 11%
where the time goes in v2:
time: 47.7 us; the launch traced here: 47.5 us
  starting transfers between devices  19.1 us (40%)
  waiting for transfers between devices  18.6 us (39%)
  Pallas kernels  8.98 us (19%)
  between operations  0.76 us (2%)
    ppermute x12, starting transfers between devices, moved(): return lax.ppermute(value, ('row', 'col'), pairs)  19.1 us
    ppermute x12, waiting for transfers between devices, moved(): return lax.ppermute(value, ('row', 'col'), pairs)  18.6 us
    pallas_call x1, Pallas kernels, local(): call(near_kernel, 'near', [f32(blocks + 1, *every), pltpu.VMEM((places, e...  2.15 us
    pallas_call x1, Pallas kernels, early(): call(edge_kernel, 'edges', [f32(length, extent)] * 2, [smem] * 3 + [hbm],...  1.96 us
    pallas_call x1, Pallas kernels, local(): call(front_kernel, 'front', bf16(blocks * pair + SIDE_ROWS, extent), [sme...  1.44 us
    pallas_call x1, Pallas kernels, local(): call(far_kernel, 'far', [f32(*shape)] * 2, [smem] * 3 + [vmem] * (3 + len...  1.25 us
    pallas_call x1, Pallas kernels, local(): call(back_kernel, 'back', f32(*sources.shape), [vmem] * spans, vmem)  1.07 us
    pallas_call x1, Pallas kernels, local(): call(list_kernel, 'lists', [pltpu.SMEM((4, slots + UNROLL), jnp.int32), p...  0.98 us
  transfers between devices with their start and end apart: 12, of which 7 were waited for; matrix products, arithmetic and copies ran while one was open for 0% of the time, Pallas kernels for 11%

profile of v2, /device:TPU:0, one launch (start us, length us, event | category | flops | bytes accessed | tf_op | source)
XLA Modules:
  0.0 47.5 jit_solution(14103984327712701469)
XLA Ops:
  0.0 0.5 collective-permute-start.4
  1.1 1.0 %lists.1 = (s32[4,52]{1,0:T(4,128)S(4)}, s32[4]{0:T(128)S(4)}, f32[16,256]{1,0:T(8,128)S(1)}, f32[48,256]{1,0:T(8,128)S(1)}) custom-call(s32[1]{0:T(128)} %bitcast.1.place_ref, s32[48]{0:T(128)} %bitcast.11, s32[48]{0:T(128)} %bitcast.12, s32[1]{0:T(128)} %bitcast.9.count_ref), custom_call_target="tpu_custom_call" | custom-call | bytes 1048576 | tf_op jit(solution)/shard_map/lists/pallas_call | solution.py:449
  2.1 1.4 %front.1 = bf16[528,256]{1,0:T(8,128)(2,1)S(1)} custom-call(s32[1]{0:T(128)} %bitcast.1.place_ref, f32[32,2048]{1,0:T(8,128)} %sources_ref.1, f32[32,2048]{1,0:T(8,128)S(1)} %collective-permute-done.4.other_ref, f32[48,256]{1,0:T(8,128)S(1)} %get-tuple-element.255._), custom_call_target="tpu_custom_call" | custom-call | bytes 1048576 | tf_op jit(solution)/shard_map/front/pallas_call | solution.py:463
  3.6 3.3 %collective-permute-start.6 = (bf16[528,256]{1,0:T(8,128)(2,1)S(1)}, bf16[528,256]{1,0:T(8,128)(2,1)S(1)}, u32[]{:S(2)}, u32[]{:S(2)}) collective-permute-start(bf16[528,256]{1,0:T(8,128)(2,1)S(1)} %front.1), channel_id=1, source_target_pairs={{0,8},{1,24},{2,0},{3,16},{4,12},{5,28},{6,4},{7,20},{8,9},{9,25},... | collective-permute-start | bytes 811016 | tf_op jit(solution)/shard_map/ppermute | solution.py:400
  6.8 0.7 %collective-permute-start.5 = (bf16[528,256]{1,0:T(8,128)(2,1)S(1)}, bf16[528,256]{1,0:T(8,128)(2,1)S(1)}, u32[]{:S(2)}, u32[]{:S(2)}) collective-permute-start(bf16[528,256]{1,0:T(8,128)(2,1)S(1)} %front.1), channel_id=1, source_target_pairs={{0,0},{1,16},{2,8},{3,24},{4,4},{5,20},{6,12},{7,28},{8,1},{9,17},... | collective-permute-start | bytes 811016 | tf_op jit(solution)/shard_map/ppermute | solution.py:400
  7.5 10.3 %while.23 = (s32[]{:T(128)}, f32[16,256]{1,0:T(8,128)S(1)}, f32[48,256]{1,0:T(8,128)S(1)}, s32[]{:T(128)}, s32[4,52]{1,0:T(4,128)S(4)}, /*index=5*/s32[4]{0:T(12...) while((s32[]{:T(128)}, f32[16,256]{1,0:T(8,128)S(1)}, f32[48,256]{1,0:T(8,128)S(1)}, s32[]{:T(128)}, ...), condition=%wide.region_1.2_spmd, body=%wide.region_0.1_spmd.sunk | while | flops 2 | bytes 4325549 | solution.py:444
  7.5 2.0 %edges.1 = (f32[16,256]{1,0:T(8,128)S(1)}, f32[16,256]{1,0:T(8,128)S(1)}) custom-call(s32[1]{0:T(128)} %bitcast.8._, s32[4,52]{1,0:T(4,128)S(4)} %get-tuple-element.275.order_ref, s32[4]{0:T(128)S(4)} %get-tuple-element.276.sizes_ref, bf16[48,256,256]{2,1,0:T(8,128)(2,1)} %get-tuple-element.277.tiles_ref), custom_call_target="tpu_custom_call" | custom-call | bytes 1048576 | tf_op jit(solution)/shard_map/while/body/edges/pallas_call | solution.py:486
  9.5 1.0 %collective-permute-start = (f32[16,256]{1,0:T(8,128)S(1)}, f32[16,256]{1,0:T(8,128)S(1)}, u32[]{:S(2)}, u32[]{:S(2)}) collective-permute-start(f32[16,256]{1,0:T(8,128)S(1)} %get-tuple-element.243.refs_0_.refs_1_), channel_id=1, source_target_pairs={{0,4},{1,5},{2,6},{3,7},{4,0},{5,1},{6,2},{7,3},{8,12},{9,13},{10,... | collective-permute-start | bytes 49160 | tf_op jit(solution)/shard_map/while/body/ppermute | solution.py:400
  10.5 2.8 %collective-permute-done.refs_1_.refs_2_ = f32[16,256]{1,0:T(8,128)S(1)} collective-permute-done((f32[16,256]{1,0:T(8,128)S(1)}, f32[16,256]{1,0:T(8,128)S(1)}, u32[]{:S(2)}, u32[]{:S(2)}) %collective-permute-start) | collective-permute-done | bytes 16416 | tf_op jit(solution)/shard_map/while/body/ppermute | solution.py:400
  13.3 2.8 %collective-permute-start.1 = (f32[16,256]{1,0:T(8,128)S(1)}, f32[16,256]{1,0:T(8,128)S(1)}, u32[]{:S(2)}, u32[]{:S(2)}) collective-permute-start(f32[16,256]{1,0:T(8,128)S(1)} %pack.1.value_ref), channel_id=1, source_target_pairs={{0,2},{1,3},{2,0},{3,1},{4,6},{5,7},{6,4},{7,5},{8,10},{9,11},{10,... | collective-permute-start | bytes 49160 | tf_op jit(solution)/shard_map/while/body/ppermute | solution.py:400
  16.1 1.7 %collective-permute-done.1.partner_ref = f32[16,256]{1,0:T(8,128)S(1)} collective-permute-done((f32[16,256]{1,0:T(8,128)S(1)}, f32[16,256]{1,0:T(8,128)S(1)}, u32[]{:S(2)}, u32[]{:S(2)}) %collective-permute-start.1) | collective-permute-done | bytes 16416 | tf_op jit(solution)/shard_map/while/body/ppermute | solution.py:400
  17.8 2.0 %collective-permute-start.9 = (bf16[528,256]{1,0:T(8,128)(2,1)S(1)}, bf16[528,256]{1,0:T(8,128)(2,1)S(1)}, u32[]{:S(2)}, u32[]{:S(2)}) collective-permute-start(bf16[528,256]{1,0:T(8,128)(2,1)S(1)} %collective-permute-done.6.refs_1_), channel_id=1, source_target_pairs={{0,4},{1,5},{2,6},{3,7},{4,0},{5,1},{6,2},{7,3},{8,12},{9,13},{10,... | collective-permute-start | bytes 811016 | tf_op jit(solution)/shard_map/ppermute | solution.py:400
  19.9 4.0 %collective-permute-start.7 = (f32[16,256]{1,0:T(8,128)S(1)}, f32[16,256]{1,0:T(8,128)S(1)}, u32[]{:S(2)}, u32[]{:S(2)}) collective-permute-start(f32[16,256]{1,0:T(8,128)S(1)} %get-tuple-element.284), channel_id=1, source_target_pairs={{0,1},{1,0},{2,3},{3,2},{4,5},{5,4},{6,7},{7,6},{8,9},{9,8},{10,11... | collective-permute-start | bytes 49160 | tf_op jit(solution)/shard_map/while/body/ppermute | solution.py:400
  23.9 0.8 %collective-permute-done.7 = f32[16,256]{1,0:T(8,128)S(1)} collective-permute-done((f32[16,256]{1,0:T(8,128)S(1)}, f32[16,256]{1,0:T(8,128)S(1)}, u32[]{:S(2)}, u32[]{:S(2)}) %collective-permute-start.7) | collective-permute-done | bytes 16416 | tf_op jit(solution)/shard_map/while/body/ppermute | solution.py:400
  24.8 8.6 %while.24 = (s32[]{:T(128)}, f32[48,256]{1,0:T(8,128)S(1)}, s32[]{:T(128)}, s32[1]{0:T(128)}, f32[16,256]{1,0:T(8,128)S(1)}, /*index=5*/f32[16,256]{1,0:T(8,128)S(1)}, s32[]{:T(128)}) while((s32[]{:T(128)}, f32[48,256]{1,0:T(8,128)S(1)}, s32[]{:T(128)}, s32[1]{0:T(128)}, f32[16,256]{1,0:T(8,128)S(1)}, /*index=5*/f32[16,256]{1,0:T(8,128)S(1)}, ...), condition=%wide.region_3.4_spmd, body=%wide.region_2.3_spmd.sunk | while | flops 2 | bytes 4325533 | solution.py:444
  24.9 4.6 %collective-permute-done.2.partner_ref = f32[16,256]{1,0:T(8,128)S(1)} collective-permute-done((f32[16,256]{1,0:T(8,128)S(1)}, f32[16,256]{1,0:T(8,128)S(1)}, u32[]{:S(2)}, u32[]{:S(2)}) %collective-permute-start.2) | collective-permute-done | bytes 16416 | tf_op jit(solution)/shard_map/while/body/ppermute | solution.py:400
  29.5 0.8 %collective-permute-start.3 = (f32[16,256]{1,0:T(8,128)S(1)}, f32[16,256]{1,0:T(8,128)S(1)}, u32[]{:S(2)}, u32[]{:S(2)}) collective-permute-start(f32[16,256]{1,0:T(8,128)S(1)} %row_level.2.value_ref), channel_id=1, source_target_pairs={{0,8},{1,9},{2,10},{3,11},{4,12},{5,13},{6,14},{7,15},{8,0},{9,1},... | collective-permute-start | bytes 49160 | tf_op jit(solution)/shard_map/while/body/ppermute | solution.py:400
  30.3 3.0 %collective-permute-done.3.partner_ref = f32[16,256]{1,0:T(8,128)S(1)} collective-permute-done((f32[16,256]{1,0:T(8,128)S(1)}, f32[16,256]{1,0:T(8,128)S(1)}, u32[]{:S(2)}, u32[]{:S(2)}) %collective-permute-start.3) | collective-permute-done | bytes 16416 | tf_op jit(solution)/shard_map/while/body/ppermute | solution.py:400
  33.4 2.1 %near.1 = (f32[9,128,256]{2,1,0:T(8,128)S(1)}, bf16[56,256,256]{2,1,0:T(8,128)(2,1)S(1)}) custom-call(s32[1]{0:T(128)} %bitcast.1.place_ref, s32[4,52]{1,0:T(4,128)S(4)} %get-tuple-element.257.order_ref, s32[4]{0:T(128)S(4)} %get-tuple-element.258.sizes_ref, bf16[48,256,256]{2,1,0:T(8,128)(2,1)} %get-tuple-element.323, ...), custom_call_target="tpu_custom_call" | custom-call | bytes 1048576 | tf_op jit(solution)/shard_map/near/pallas_call | solution.py:537
  35.5 1.2 %far.1 = (f32[2,8,32,256]{3,2,1,0:T(8,128)S(1)}, f32[2,8,32,256]{3,2,1,0:T(8,128)S(1)}) custom-call(s32[1]{0:T(128)} %bitcast.1.place_ref, s32[4,52]{1,0:T(4,128)S(4)} %get-tuple-element.257.order_ref, s32[4]{0:T(128)S(4)} %get-tuple-element.258.sizes_ref, bf16[56,256,256]{2,1,0:T(8,128)(2,1)S(1)} %get-tuple-element.123.tiles_ref, ...), custom_call_target="tpu_custom_call" | custom-call | bytes 1048576 | tf_op jit(solution)/shard_map/far/pallas_call | solution.py:549
  36.9 1.9 %collective-permute-done.10.arrived_ref = f32[2,8,32,256]{3,2,1,0:T(8,128)S(1)} collective-permute-done((f32[2,8,32,256]{3,2,1,0:T(8,128)S(1)}, f32[2,8,32,256]{3,2,1,0:T(8,128)S(1)}, u32[]{:S(2)}, u32[]{:S(2)}) %collective-permute-start.10) | collective-permute-done | bytes 524320 | tf_op jit(solution)/shard_map/ppermute | solution.py:400
  38.8 3.8 %collective-permute-start.11 = (bf16[8,32,256]{2,1,0:T(8,128)(2,1)S(1)}, bf16[8,32,256]{2,1,0:T(8,128)(2,1)S(1)}, u32[]{:S(2)}, u32[]{:S(2)}) collective-permute-start(bf16[8,32,256]{2,1,0:T(8,128)(2,1)S(1)} %get-tuple-element.130), channel_id=1, source_target_pairs={{0,2},{1,3},{2,0},{3,1},{4,6},{5,7},{6,4},{7,5},{8,10},{9,11},{10,... | collective-permute-start | bytes 393224 | tf_op jit(solution)/shard_map/ppermute | solution.py:400
  42.6 3.8 %collective-permute-done.11.refs_0_ = bf16[8,32,256]{2,1,0:T(8,128)(2,1)S(1)} collective-permute-done((bf16[8,32,256]{2,1,0:T(8,128)(2,1)S(1)}, bf16[8,32,256]{2,1,0:T(8,128)(2,1)S(1)}, u32[]{:S(2)}, u32[]{:S(2)}) %collective-permute-start.11) | collective-permute-done | bytes 131104 | tf_op jit(solution)/shard_map/ppermute | solution.py:400
  46.4 1.1 %back.1 = f32[32,2048]{1,0:T(8,128)} custom-call(f32[8,32,256]{2,1,0:T(8,128)S(1)} %get-tuple-element.129.own_ref, bf16[8,32,256]{2,1,0:T(8,128)(2,1)S(1)} %collective-permute-done.11.refs_0_), custom_call_target="tpu_custom_call" | custom-call | bytes 1048576 | tf_op jit(solution)/shard_map/back/pallas_call | solution.py:575
  (16 shorter events, 0.4 us)
Async XLA Ops:
  0.0 2.1 %collective-permute-start.4 = (f32[32,2048]{1,0:T(8,128)}, f32[32,2048]{1,0:T(8,128)S(1)}, u32[]{:S(2)}, u32[]{:S(2)}) collective-permute-start(f32[32,2048]{1,0:T(8,128)} %sources_ref.1), channel_id=1, source_target_pairs={{0,1},{1,0},{2,3},{3,2},{4,5},{5,4},{6,7},{7,6},{8,9},{9,8},{10,11... | collective-permute-start | bytes 786440 | tf_op jit(solution)/shard_map/ppermute | solution.py:400
  3.6 14.3 %collective-permute-start.6 = (bf16[528,256]{1,0:T(8,128)(2,1)S(1)}, bf16[528,256]{1,0:T(8,128)(2,1)S(1)}, u32[]{:S(2)}, u32[]{:S(2)}) collective-permute-start(bf16[528,256]{1,0:T(8,128)(2,1)S(1)} %front.1), channel_id=1, source_target_pairs={{0,8},{1,24},{2,0},{3,16},{4,12},{5,28},{6,4},{7,20},{8,9},{9,25},... | collective-permute-start | bytes 811016 | tf_op jit(solution)/shard_map/ppermute | solution.py:400
  6.8 13.0 %collective-permute-start.5 = (bf16[528,256]{1,0:T(8,128)(2,1)S(1)}, bf16[528,256]{1,0:T(8,128)(2,1)S(1)}, u32[]{:S(2)}, u32[]{:S(2)}) collective-permute-start(bf16[528,256]{1,0:T(8,128)(2,1)S(1)} %front.1), channel_id=1, source_target_pairs={{0,0},{1,16},{2,8},{3,24},{4,4},{5,20},{6,12},{7,28},{8,1},{9,17},... | collective-permute-start | bytes 811016 | tf_op jit(solution)/shard_map/ppermute | solution.py:400
  9.5 3.8 %collective-permute-start = (f32[16,256]{1,0:T(8,128)S(1)}, f32[16,256]{1,0:T(8,128)S(1)}, u32[]{:S(2)}, u32[]{:S(2)}) collective-permute-start(f32[16,256]{1,0:T(8,128)S(1)} %get-tuple-element.243.refs_0_.refs_1_), channel_id=1, source_target_pairs={{0,4},{1,5},{2,6},{3,7},{4,0},{5,1},{6,2},{7,3},{8,12},{9,13},{10,... | collective-permute-start | bytes 49160 | tf_op jit(solution)/shard_map/while/body/ppermute | solution.py:400
  13.3 4.5 %collective-permute-start.1 = (f32[16,256]{1,0:T(8,128)S(1)}, f32[16,256]{1,0:T(8,128)S(1)}, u32[]{:S(2)}, u32[]{:S(2)}) collective-permute-start(f32[16,256]{1,0:T(8,128)S(1)} %pack.1.value_ref), channel_id=1, source_target_pairs={{0,2},{1,3},{2,0},{3,1},{4,6},{5,7},{6,4},{7,5},{8,10},{9,11},{10,... | collective-permute-start | bytes 49160 | tf_op jit(solution)/shard_map/while/body/ppermute | solution.py:400
  17.8 17.7 %collective-permute-start.9 = (bf16[528,256]{1,0:T(8,128)(2,1)S(1)}, bf16[528,256]{1,0:T(8,128)(2,1)S(1)}, u32[]{:S(2)}, u32[]{:S(2)}) collective-permute-start(bf16[528,256]{1,0:T(8,128)(2,1)S(1)} %collective-permute-done.6.refs_1_), channel_id=1, source_target_pairs={{0,4},{1,5},{2,6},{3,7},{4,0},{5,1},{6,2},{7,3},{8,12},{9,13},{10,... | collective-permute-start | bytes 811016 | tf_op jit(solution)/shard_map/ppermute | solution.py:400
  19.8 15.7 %collective-permute-start.8 = (bf16[528,256]{1,0:T(8,128)(2,1)S(1)}, bf16[528,256]{1,0:T(8,128)(2,1)S(1)}, u32[]{:S(2)}, u32[]{:S(2)}) collective-permute-start(bf16[528,256]{1,0:T(8,128)(2,1)S(1)} %collective-permute-done.5.refs_0_), channel_id=1, source_target_pairs={{0,4},{1,5},{2,6},{3,7},{4,0},{5,1},{6,2},{7,3},{8,12},{9,13},{10,... | collective-permute-start | bytes 811016 | tf_op jit(solution)/shard_map/ppermute | solution.py:400
  19.9 4.8 %collective-permute-start.7 = (f32[16,256]{1,0:T(8,128)S(1)}, f32[16,256]{1,0:T(8,128)S(1)}, u32[]{:S(2)}, u32[]{:S(2)}) collective-permute-start(f32[16,256]{1,0:T(8,128)S(1)} %get-tuple-element.284), channel_id=1, source_target_pairs={{0,1},{1,0},{2,3},{3,2},{4,5},{5,4},{6,7},{7,6},{8,9},{9,8},{10,11... | collective-permute-start | bytes 49160 | tf_op jit(solution)/shard_map/while/body/ppermute | solution.py:400
  24.8 4.7 %collective-permute-start.2 = (f32[16,256]{1,0:T(8,128)S(1)}, f32[16,256]{1,0:T(8,128)S(1)}, u32[]{:S(2)}, u32[]{:S(2)}) collective-permute-start(f32[16,256]{1,0:T(8,128)S(1)} %get-tuple-element.251.value_ref), channel_id=1, source_target_pairs={{0,16},{1,17},{2,18},{3,19},{4,20},{5,21},{6,22},{7,23},{8,24},{9,... | collective-permute-start | bytes 49160 | tf_op jit(solution)/shard_map/while/body/ppermute | solution.py:400
  29.5 3.8 %collective-permute-start.3 = (f32[16,256]{1,0:T(8,128)S(1)}, f32[16,256]{1,0:T(8,128)S(1)}, u32[]{:S(2)}, u32[]{:S(2)}) collective-permute-start(f32[16,256]{1,0:T(8,128)S(1)} %row_level.2.value_ref), channel_id=1, source_target_pairs={{0,8},{1,9},{2,10},{3,11},{4,12},{5,13},{6,14},{7,15},{8,0},{9,1},... | collective-permute-start | bytes 49160 | tf_op jit(solution)/shard_map/while/body/ppermute | solution.py:400
  36.8 2.0 %collective-permute-start.10 = (f32[2,8,32,256]{3,2,1,0:T(8,128)S(1)}, f32[2,8,32,256]{3,2,1,0:T(8,128)S(1)}, u32[]{:S(2)}, u32[]{:S(2)}) collective-permute-start(f32[2,8,32,256]{3,2,1,0:T(8,128)S(1)} %get-tuple-element.128), channel_id=1, source_target_pairs={{0,1},{1,0},{2,3},{3,2},{4,5},{5,4},{6,7},{7,6},{8,9},{9,8},{10,11... | collective-permute-start | bytes 1572872 | tf_op jit(solution)/shard_map/ppermute | solution.py:400
  38.8 7.6 %collective-permute-start.11 = (bf16[8,32,256]{2,1,0:T(8,128)(2,1)S(1)}, bf16[8,32,256]{2,1,0:T(8,128)(2,1)S(1)}, u32[]{:S(2)}, u32[]{:S(2)}) collective-permute-start(bf16[8,32,256]{2,1,0:T(8,128)(2,1)S(1)} %get-tuple-element.130), channel_id=1, source_target_pairs={{0,2},{1,3},{2,0},{3,1},{4,6},{5,7},{6,4},{7,5},{8,10},{9,11},{10,... | collective-permute-start | bytes 393224 | tf_op jit(solution)/shard_map/ppermute | solution.py:400

commit v3 on v2

--- a/solution.py
+++ b/solution.py
@@ -84,10 +84,10 @@
 
 
 def source_span(place_ref, m, spans):
-    return lax.rem(z_of(place_ref) - m + spans * 256, spans)
-
-
-def front_kernel(place_ref, sources_ref, other_ref, _, out_ref, mine_ref, sem, *, blocks, extent):
+    return (z_of(place_ref) & (spans - 1)) ^ m
+
+
+def front_kernel(place_ref, sources_ref, other_ref, _, out_ref, first_ref, mine_ref, sem, *, blocks, extent):
     copy = pltpu.make_async_copy(sources_ref, mine_ref, sem)
     copy.start()
     height = mine_ref.shape[0]
@@ -110,19 +110,16 @@
     first = sum(
         lax.dot_general(ones, term, (((1,), (1,)), ((), ())), preferred_element_type=jnp.float32)
         for term in three_terms(total)
-    ) * (1.0 / math.sqrt(blocks * extent))
-    high, middle, low = (term.astype(jnp.float32) for term in three_terms(first))
-    row = lax.broadcasted_iota(jnp.int32, first.shape, 0)
-    side = jnp.where(row == 0, high, jnp.where(row == 1, middle, jnp.where(row == 2, low, 0.0)))
-    out_ref[blocks * pair :, :] = jnp.zeros((SIDE_ROWS, extent), jnp.bfloat16)
-    out_ref[blocks * pair :, 0:pair] = side.astype(jnp.bfloat16)
+    )
+    first_ref[...] = jnp.zeros_like(first_ref)
+    first_ref[:, 0:pair] = first[0:8, :] * (1.0 / math.sqrt(blocks * extent))
 
 
 def list_kernel(
-    place_ref, rows_ref, cols_ref, count_ref, order_ref, sizes_ref, lead_ref, others_ref, *, blocks, owners
+    place_ref, rows_ref, cols_ref, count_ref, order_ref, sizes_ref, walk_ref, rest_ref, *, blocks, owners
 ):
-    lead_ref[...] = jnp.zeros_like(lead_ref)
-    others_ref[...] = jnp.zeros_like(others_ref)
+    walk_ref[...] = jnp.zeros_like(walk_ref)
+    rest_ref[...] = jnp.zeros_like(rest_ref)
     x = x_of(place_ref)
 
     def visit(slot, sizes):
@@ -154,7 +151,21 @@
 
 
 def edge_kernel(
-    _, order_ref, sizes_ref, tiles_ref, cols_ref, line_ref, strips, columns, summed, strip_sems, column_sems
+    place_ref,
+    _,
+    order_ref,
+    sizes_ref,
+    tiles_ref,
+    first_ref,
+    cols_ref,
+    line_ref,
+    strips,
+    columns,
+    summed,
+    strip_sems,
+    column_sems,
+    *,
+    owners,
 ):
     def strip_copy(index):
         slot = order_ref[3, index] >> 16
@@ -185,7 +196,11 @@
 
     lax.fori_loop(0, sizes_ref[3], add_strip, 0)
     lax.fori_loop(0, sizes_ref[2], add_column, 0)
-    line_ref[...] = jnp.transpose(summed[...])[0 : line_ref.shape[0], :]
+    length = cols_ref.shape[0]
+    line_ref[0:length, :] = jnp.transpose(summed[...])[0:length, :]
+    index = lax.broadcasted_iota(jnp.int32, (line_ref.shape[0] - length, line_ref.shape[1]), 0)
+    own = z_of(place_ref) * owners + x_of(place_ref)
+    line_ref[length:, :] = jnp.where(index == own, first_ref[0:1, :], 0.0)
 
 
 def butterfly(value, partner, index, bit):
@@ -194,69 +209,49 @@
     return jnp.where(active, jnp.where(upper, partner - value, partner + value) * ROOT_HALF, value)
 
 
-def pack_kernel(cols_ref, *refs, blocks):
-    lines, lead_ref = refs[:-1], refs[-1]
-    lead_ref[...] = jnp.zeros_like(lead_ref)
-    lead_ref[0:blocks, :] = cols_ref[0:blocks, :]
-    for j, line in enumerate(lines):
-        lead_ref[blocks + j : blocks + j + 1, :] = line[0:1, :]
-
-
-def col_level_kernel(place_ref, value_ref, partner_ref, out_ref, *, bit):
-    index = 2 * span_of(place_ref) + core_of(place_ref)
-    out_ref[...] = butterfly(value_ref[...], partner_ref[...], index, bit)
-
-
-def join_kernel(*refs):
-    *parts, out_ref = refs
-    at = 0
-    for part in parts:
-        out_ref[at : at + part.shape[0], :] = part[...]
-        at += part.shape[0]
-
-
-def row_level_kernel(place_ref, value_ref, partner_ref, out_ref, *, bit):
-    out_ref[...] = butterfly(value_ref[...], partner_ref[...], z_of(place_ref), bit)
-
-
-def x_levels_kernel(place_ref, cols_ref, line_ref, rest_ref, out_ref):
+def arrange_kernel(place_ref, cols_ref, *refs):
+    *behind, walk_ref, rest_ref = refs
+    owners = len(behind)
+    length = cols_ref.shape[0]
     x = x_of(place_ref)
-    by_x = block_inverse([line_ref[...]] + [rest_ref[i] for i in range(rest_ref.shape[0])])
+    rest_ref[0:length, :] = cols_ref[...]
+    gathered = behind[0][length:, :]
+    for j in range(1, owners):
+        gathered = gathered + behind[j][length:, :]
+    walk_ref[length:, :] = gathered
+    for i in range(owners):
+        value = behind[0][0:length, :]
+        for j in range(1, owners):
+            value = jnp.where(lax.rem(x - i + owners, owners) == j, behind[j][0:length, :], value)
+        if i == 0:
+            walk_ref[0:length, :] = value
+        else:
+            rest_ref[i * length : (i + 1) * length, :] = value
+
+
+def z_level_kernel(place_ref, walk_ref, partner_ref, out_ref, *, bit, length):
+    walk, partner = walk_ref[...], partner_ref[...]
+    row = lax.broadcasted_iota(jnp.int32, walk.shape, 0)
+    out_ref[...] = jnp.where(row < length, butterfly(walk, partner, z_of(place_ref), bit), walk + partner)
+
+
+def coarse_kernel(place_ref, walk_ref, rest_ref, row_ref, cols_ref, firsts_ref, *, blocks, rows):
+    x = x_of(place_ref)
+    length = row_ref.shape[0]
+    owners = length // blocks
+    by_x = [walk_ref[0:length, :]] + [rest_ref[i * length : (i + 1) * length, :] for i in range(1, owners)]
+    by_x = block_inverse(by_x)
     value = by_x[0]
-    for i in range(1, len(by_x)):
+    for i in range(1, owners):
         value = jnp.where(x == i, by_x[i], value)
-    length = value.shape[0]
-    out_ref[0:length, :] = cols_ref[...]
-    out_ref[length : 2 * length, :] = value
-    out_ref[2 * length :, :] = jnp.zeros((out_ref.shape[0] - 2 * length, value.shape[1]), jnp.float32)
-
-
-def corner_kernel(place_ref, lead_ref, partner_ref, others_ref, out_ref, line_ref, rest_ref, *, blocks, owners):
-    x = x_of(place_ref)
-    length = owners * blocks
-    cols_ref = others_ref.at[0:length]
-    behind = [others_ref.at[(j + 1) * length : (j + 2) * length] for j in range(owners)]
-    lead = butterfly(lead_ref[...], partner_ref[...], core_of(place_ref), 0)
-    columns = [lead[0:blocks, :]] + [cols_ref[i * blocks : (i + 1) * blocks, :] for i in range(1, owners)]
-    for i, column in enumerate(block_inverse(columns)):
-        out_ref[i * blocks : (i + 1) * blocks, :] = column
-    index = lax.broadcasted_iota(jnp.int32, line_ref.shape, 0)
-    lane = lax.broadcasted_iota(jnp.int32, line_ref.shape, 1)
-    fixed = []
-    for j in range(owners):
-        line = behind[j][...]
-        corner = [lead[blocks + j : blocks + j + 1, :]] + [line[i * blocks : i * blocks + 1, :] for i in range(1, owners)]
-        for i, value in enumerate(block_inverse(corner)):
-            line = jnp.where((index == i * blocks) & (lane == 0), value[:, 0:1], line)
-        fixed.append(line)
-    for i in range(owners):
-        line = fixed[0]
-        for j in range(1, owners):
-            line = jnp.where(lax.rem(x - i + owners, owners) == j, fixed[j], line)
-        if i == 0:
-            line_ref[...] = line
-        else:
-            rest_ref[i - 1] = line
+    row_ref[...] = value
+    cols = rest_ref[0:length, :]
+    index = lax.broadcasted_iota(jnp.int32, cols.shape, 0)
+    lane = lax.broadcasted_iota(jnp.int32, cols.shape, 1)
+    cols_ref[...] = jnp.where((lax.rem(index, blocks) == 0) & (lane == 0), value, cols)
+    firsts_ref[...] = jnp.zeros_like(firsts_ref)
+    for i, first in enumerate(block_forward([walk_ref[length + i : length + i + 1, :] for i in range(rows)])):
+        firsts_ref[i : i + 1, :] = first
 
 
 def fill_sides(sides, messages, place_ref, blocks, spans):
@@ -305,44 +300,30 @@
     lax.fori_loop(0, far_places, lambda i, _: (fetch(1, i, near_places + i).wait(), 0)[1], 0)
 
 
-def far_kernel(place_ref, order_ref, sizes_ref, tiles_ref, near_ref, others_ref, *refs, blocks, owners, spans):
-    direct, swapped = refs[:spans], refs[spans : owners * spans]
-    keep_ref, send_ref, sides, acc, firsts = refs[owners * spans :]
+def far_kernel(
+    place_ref, order_ref, sizes_ref, tiles_ref, near_ref, row_ref, cols_ref, *refs, blocks, owners, spans
+):
+    messages = refs[: owners * spans]
+    keep_ref, send_ref, sides, acc = refs[owners * spans :]
     extent = tiles_ref.shape[-1]
     pair = sides.shape[1] // spans
     height = pair // 2
-    length = owners * blocks
-    cols_ref, row_ref = others_ref.at[0:length], others_ref.at[length : 2 * length]
     x = x_of(place_ref)
-    fill_sides(sides, swapped, place_ref, blocks, spans)
-    messages = (*direct, *swapped)
-    for index, message in enumerate(messages):
-        owner = lax.rem(x - index // spans + owners, owners)
-        side = jnp.transpose(message[blocks * pair :, :].astype(jnp.float32))
-        column = side[0:pair, 0:1] + side[0:pair, 1:2] + side[0:pair, 2:3]
-        rows = pl.ds(pl.multiple_of(source_span(place_ref, index % spans, spans) * pair, pair), pair)
-        firsts[owner, rows, :] = jnp.broadcast_to(column, (pair, firsts.shape[2]))
-    for i in range(blocks):
-        total = near_ref[i]
-        for owner in range(owners):
-            total += firsts[owner][:, 0:1] * cols_ref[owner * blocks + i : owner * blocks + i + 1, :]
-        acc[i] = total
+    fill_sides(sides, messages[spans:], place_ref, blocks, spans)
+    acc[...] = near_ref[...]
     add_products(order_ref, sizes_ref, 1, groups_of(sizes_ref, 0) * UNROLL, tiles_ref, sides, acc)
 
     lane = lax.broadcasted_iota(jnp.int32, (pair, extent), 1)
     for m in range(spans):
         rows = pl.ds(pl.multiple_of(source_span(place_ref, m, spans) * pair, pair), pair)
         total = jnp.zeros((pair, extent), jnp.float32)
-        top = jnp.zeros((pair, 1), jnp.float32)
         for behind in range(owners):
             owner = lax.rem(x - behind + owners, owners)
             message = messages[behind * spans + m]
             for b in range(blocks):
                 line = row_ref[pl.ds(owner * blocks + b, 1), :]
                 total += message[b * pair : (b + 1) * pair, :].astype(jnp.float32) * line
-                if b == 0:
-                    top += firsts[owner, rows, :][:, 0:1] * line[:, 0:1]
-        top += jnp.sum(total, axis=1, keepdims=True)
+        top = jnp.sum(total, axis=1, keepdims=True)
         acc[0, rows, :] = jnp.where(lane == 0, top, acc[0, rows, :])
     first_core = core_of(place_ref) == 0
     for i in range(blocks):
@@ -350,28 +331,65 @@
         for y in range(spans):
             one = value[y * pair : y * pair + height, :]
             two = value[y * pair + height : (y + 1) * pair, :]
-            keep_ref[y, i] = jnp.where(first_core, one, two)
-            send_ref[y, i] = jnp.where(first_core, two, one)
-
-
-def combine_kernel(place_ref, keep_ref, arrived_ref, own_ref, *out_refs):
-    spans = keep_ref.shape[0]
+            at = (y * blocks + i) * height
+            keep_ref[at : at + height, :] = jnp.where(first_core, one, two)
+            send_ref[at : at + height, :] = jnp.where(first_core, two, one)
+    send_ref[spans * blocks * height :, :] = cols_ref[...]
+
+
+def combine_kernel(place_ref, keep_ref, arrived_ref, cols_ref, own_ref, both_ref, *out_refs):
+    spans = len(out_refs) + 1
     span = span_of(place_ref)
-    own_ref[...] = keep_ref[span] + arrived_ref[span]
+    rows = own_ref.shape[0]
+    length = cols_ref.shape[0]
+    first_core = core_of(place_ref) == 0
+    mine, other = cols_ref[...], arrived_ref[spans * rows :, :]
+    both_ref[0:length, :] = jnp.where(first_core, mine, other)
+    both_ref[length:, :] = jnp.where(first_core, other, mine)
+    at = pl.ds(pl.multiple_of(span * rows, rows), rows)
+    own_ref[...] = keep_ref[at, :] + arrived_ref[at, :]
+    high, low, _ = three_terms(both_ref[...])
     for j, out_ref in enumerate(out_refs, 1):
-        at = lax.rem(span + j, spans)
-        out_ref[...] = (keep_ref[at] + arrived_ref[at]).astype(jnp.bfloat16)
-
-
-def back_kernel(own_ref, *refs):
+        at = pl.ds(pl.multiple_of(lax.rem(span + j, spans) * rows, rows), rows)
+        out_ref[0:rows, :] = (keep_ref[at, :] + arrived_ref[at, :]).astype(jnp.bfloat16)
+        out_ref[rows : rows + 2 * length, :] = high
+        out_ref[rows + 2 * length :, :] = low
+
+
+def back_kernel(place_ref, own_ref, both_ref, firsts_ref, *refs, blocks, owners):
     *arrived, out_ref = refs
-    blocks, height, extent = own_ref.shape
+    spans = len(arrived) + 1
+    extent = own_ref.shape[1]
+    rows = own_ref.shape[0]
+    height = rows // blocks
+    length = owners * blocks
+    span = span_of(place_ref)
     total = own_ref[...]
     for part in arrived:
-        total = total + part[...].astype(jnp.float32)
-    columns = block_inverse([total[b][:, 0:1] for b in range(blocks)])
+        total = total + part[0:rows, :].astype(jnp.float32)
+    tables, picked = [both_ref[...]], []
+    for part in arrived:
+        high, low = part[rows : rows + 2 * length, :], part[rows + 2 * length :, :]
+        tables.append(high.astype(jnp.float32) + low.astype(jnp.float32))
+    for j in range(spans):
+        source = lax.rem(span - j + spans, spans)
+        for k in range(2 * owners):
+            picked.append(firsts_ref[pl.ds(source * 2 * owners + k, 1), :])
+    picked += [jnp.zeros_like(picked[0])] * (-len(picked) % 16)
+    columns = jnp.transpose(jnp.concatenate(picked, axis=0))
+    columns = jnp.where(core_of(place_ref) == 0, columns[0:height, :], columns[height : 2 * height, :])
+    blocks_of = []
+    for b in range(blocks):
+        value = total[b * height : (b + 1) * height, :]
+        for j, table in enumerate(tables):
+            for k in range(2 * owners):
+                at = k * blocks + b
+                index = j * 2 * owners + k
+                value = value + columns[:, index : index + 1] * table[at : at + 1, :]
+        blocks_of.append(value)
+    columns = block_inverse([value[:, 0:1] for value in blocks_of])
     lane = lax.broadcasted_iota(jnp.int32, (height, extent), 1)
-    fixed = jnp.concatenate([jnp.where(lane == 0, columns[b], total[b]) for b in range(blocks)], axis=0)
+    fixed = jnp.concatenate([jnp.where(lane == 0, columns[b], blocks_of[b]) for b in range(blocks)], axis=0)
     signs, scale = haar_parts(extent, True)
     result = exact_dot(fixed * scale, signs)
     for b in range(blocks):
@@ -441,53 +459,48 @@
         return lax.optimization_barrier((value, *others))[0]
 
     def apart(body, *state):
-        return lax.fori_loop(0, jnp.minimum(tile_count.reshape(()), 1), body, state)
+        return lax.fori_loop(0, jnp.minimum(tile_count.reshape(()), 1), body, state if len(state) > 1 else state[0])
 
     length = owners * blocks
     stack = in_hbm(tiles.reshape(slots, extent, extent))
     from_core = other_core(sources)
-    order, sizes, blank_lead, blank = call(
+    gathered = -(-n_row // 8) * 8
+    order, sizes, blank_walk, blank_rest = call(
         list_kernel,
         "lists",
         [
             pltpu.SMEM((4, slots + UNROLL), jnp.int32),
             pltpu.SMEM((4,), jnp.int32),
-            kept(2 * blocks, extent),
-            kept((owners + 1) * length, extent),
+            kept(length + gathered, extent),
+            kept(owners * length, extent),
         ],
         [smem] * 4,
         [smem] * 2 + [vmem] * 2,
         blocks=blocks,
         owners=owners,
     )(place, in_hbm(tile_row.reshape(-1)), in_hbm(tile_col.reshape(-1)), tile_count.reshape(1))
-    message = call(
+    message, first = call(
         front_kernel,
         "front",
-        bf16(blocks * pair + SIDE_ROWS, extent),
+        [bf16(blocks * pair, extent), f32(8, extent)],
         [smem, hbm, vmem, unread],
-        vmem,
+        [vmem] * 2,
         scratch=[pltpu.VMEM(sources.shape, jnp.float32), pltpu.SemaphoreType.DMA],
         blocks=blocks,
         extent=extent,
-    )(place, in_hbm(sources), from_core, blank)
-
-    direct = [
-        moved(message, lambda zz, xx, yy, cc, m=m: (cc * spans + (yy + m) % spans, xx, zz // 2, zz % 2))
-        for m in range(spans)
-    ]
-
-    def col_level(value, bit):
-        if bit == 0:
-            return other_core(value)
-        step = 2 ** (bit - 1)
-        return moved(value, lambda zz, xx, yy, cc: (zz, xx, yy ^ step, cc))
+    )(place, in_hbm(sources), from_core, blank_rest)
+
+    def spread(message, m):
+        return moved(message, lambda zz, xx, yy, cc: (cc * spans + (yy ^ m), xx, zz // 2, zz % 2))
+
+    direct = [spread(message, m) for m in range(spans)]
 
     def early(trip, _):
         cols, line = call(
             edge_kernel,
             "edges",
-            [f32(length, extent)] * 2,
-            [smem] * 3 + [hbm],
+            [f32(length, extent), f32(length + gathered, extent)],
+            [smem] * 4 + [hbm, vmem],
             [vmem] * 2,
             scratch=[
                 pltpu.VMEM((slots, SIDE_ROWS, extent), jnp.bfloat16),
@@ -496,41 +509,39 @@
                 pltpu.SemaphoreType.DMA((slots,)),
                 pltpu.SemaphoreType.DMA((slots,)),
             ],
-        )(trip.reshape(1), order, sizes, stack)
-        behind = [line] + [along_x(line, j) for j in range(1, owners)]
-        lead = call(pack_kernel, "pack", f32(2 * blocks, extent), [vmem] * (1 + owners), vmem, blocks=blocks)(cols, *behind)
-        others = call(join_kernel, "join", kept(*blank.shape), [vmem] * (1 + owners), vmem)(cols, *behind)
-        for bit in reversed(range(1, n_col.bit_length() - 1)):
-            lead = call(col_level_kernel, "col_level", kept(2 * blocks, extent), [smem, vmem, vmem], vmem, bit=bit)(
-                place, lead, col_level(lead, bit)
-            )
-        return lead, others
-
-    lead, others = apart(early, blank_lead, blank)
-    swapped = [along_x(after(piece, lead), j) for j in range(1, owners) for piece in direct]
-
-    def late(_, state):
-        lead, others = state
-        first_cols, line, rest = call(
-            corner_kernel,
-            "corner",
-            [f32(length, extent)] * 2 + [f32(owners - 1, length, extent)],
-            [smem] + [vmem] * 3,
-            [vmem] * 3,
-            blocks=blocks,
             owners=owners,
-        )(place, lead, col_level(lead, 0), others)
-        for bit in reversed(range((n_row // owners).bit_length() - 1)):
-            partner = moved(line, lambda zz, xx, yy, cc, bit=bit: (zz ^ 2**bit, xx, yy, cc))
-            line = call(row_level_kernel, "row_level", f32(length, extent), [smem, vmem, vmem], vmem, bit=bit)(
-                place, line, partner
-            )
-        others = call(x_levels_kernel, "x_levels", kept(*blank.shape), [smem, vmem, vmem, vmem], vmem)(
-            place, first_cols, line, rest
-        )
-        return lead, others
-
-    _, others = apart(late, after(lead, *direct), others)
+        )(place, trip.reshape(1), order, sizes, stack, first)
+        behind = [along_x(line, j) for j in range(1, owners)]
+        return call(
+            arrange_kernel,
+            "arrange",
+            [kept(*blank_walk.shape), kept(*blank_rest.shape)],
+            [smem] + [vmem] * (1 + owners),
+            [vmem] * 2,
+        )(place, cols, line, *behind)
+
+    def z_levels(walk, bits):
+        for bit in bits:
+            partner = moved(walk, lambda zz, xx, yy, cc, bit=bit: (zz ^ 2**bit, xx, yy, cc))
+            walk = call(
+                z_level_kernel, "z_level", kept(*walk.shape), [smem, vmem, vmem], vmem, bit=bit, length=length
+            )(place, walk, partner)
+        return walk
+
+    walk, rest = apart(early, blank_walk, blank_rest)
+    swapped = [along_x(after(piece, walk), j) for j in range(1, owners) for piece in direct]
+    z_bits = list(reversed(range((n_row // owners).bit_length() - 1)))
+    walk = apart(lambda _, walk: z_levels(walk, z_bits), after(walk, *direct))
+
+    first_row, first_cols, firsts = call(
+        coarse_kernel,
+        "coarse",
+        [f32(length, extent), f32(length, extent), f32(gathered, extent)],
+        [smem, vmem, vmem],
+        [vmem] * 3,
+        blocks=blocks,
+        rows=n_row,
+    )(place, walk, rest)
 
     every = (spans * pair, extent)
     places = slots + 2 * UNROLL
@@ -543,36 +554,43 @@
         scratch=[pltpu.VMEM((blocks, *every), jnp.bfloat16), pltpu.SemaphoreType.DMA((places,))],
         blocks=blocks,
         spans=spans,
-    )(place, order, sizes, stack, others, *direct)
-
-    shape = (spans, blocks, height, extent)
+    )(place, order, sizes, stack, first_row, *direct)
+
+    part = blocks * height
     keep, send = call(
         far_kernel,
         "far",
-        [f32(*shape)] * 2,
-        [smem] * 3 + [vmem] * (3 + len(direct) + len(swapped)),
+        [f32(spans * part, extent), f32(spans * part + length, extent)],
+        [smem] * 3 + [vmem] * (4 + len(direct) + len(swapped)),
         [vmem] * 2,
         scratch=[
             pltpu.VMEM(((owners - 1) * blocks, *every), jnp.bfloat16),
             pltpu.VMEM((blocks + 1, *every), jnp.float32),
-            pltpu.VMEM((owners, spans * pair, 128), jnp.float32),
         ],
         blocks=blocks,
         owners=owners,
         spans=spans,
-    )(place, order, sizes, held, near, others, *direct, *swapped)
-
-    own, *outgoing = call(
+    )(place, order, sizes, held, near, first_row, first_cols, *direct, *swapped)
+
+    own, both, *outgoing = call(
         combine_kernel,
         "combine",
-        [f32(*shape[1:])] + [bf16(*shape[1:])] * (spans - 1),
-        [smem, vmem, vmem],
-        [vmem] * spans,
-    )(place, keep, other_core(send))
+        [f32(part, extent), f32(2 * length, extent)] + [bf16(part + 4 * length, extent)] * (spans - 1),
+        [smem, vmem, vmem, vmem],
+        [vmem] * (spans + 1),
+    )(place, keep, other_core(send), first_cols)
     arrived = [
         moved(value, lambda zz, xx, yy, cc, j=j: (zz, xx, (yy + j) % spans, cc)) for j, value in enumerate(outgoing, 1)
     ]
-    return call(back_kernel, "back", f32(*sources.shape), [vmem] * spans, vmem)(own, *arrived)
+    return call(
+        back_kernel,
+        "back",
+        f32(*sources.shape),
+        [smem] + [vmem] * (2 + spans),
+        vmem,
+        blocks=blocks,
+        owners=owners,
+    )(place, own, both, firsts, *arrived)
 
 
 def solution(mesh):

time: 47.7 us -> 44.6 us (0.935)
  waiting for transfers between devices: 18.6 us -> 12.7 us
  starting transfers between devices: 19.1 us -> 22 us
    ppermute x12 -> x10, waiting for transfers between devices: 18.6 us -> 12.7 us  [moved(): return lax.ppermute(value, ('row', 'col'), pairs)]
    ppermute x12 -> x10, starting transfers between devices: 19.1 us -> 22 us  [moved(): return lax.ppermute(value, ('row', 'col'), pairs)]
    pallas_call x12 -> x9, Pallas kernels: 5.85 us -> 5.74 us  [the longest x1 1.87 us: early(): call(edge_kernel, 'edges', [f32(length, extent), f32(length + gathered, e...]
  transfers between devices with their start and end apart: 12 -> 10, of which waited for: 7 -> 5; matrix products, arithmetic and copies ran while one was open for 0% -> 0% of each run, Pallas kernels for 11% -> 12%
where the time goes in v3:
time: 44.6 us; the launch traced here: 44.5 us
  starting transfers between devices  22 us (49%)
  waiting for transfers between devices  12.7 us (28%)
  Pallas kernels  8.98 us (20%)
  between operations  0.77 us (2%)
    ppermute x10, starting transfers between devices, moved(): return lax.ppermute(value, ('row', 'col'), pairs)  22 us
    ppermute x10, waiting for transfers between devices, moved(): return lax.ppermute(value, ('row', 'col'), pairs)  12.7 us
    pallas_call x1, Pallas kernels, local(): call(near_kernel, 'near', [f32(blocks + 1, *every), pltpu.VMEM((places, e...  2.19 us
    pallas_call x1, Pallas kernels, early(): call(edge_kernel, 'edges', [f32(length, extent), f32(length + gathered, e...  1.87 us
    pallas_call x1, Pallas kernels, local(): call(front_kernel, 'front', [bf16(blocks * pair, extent), f32(8, extent)]...  1.44 us
    pallas_call x1, Pallas kernels, local(): call(back_kernel, 'back', f32(*sources.shape), [smem] + [vmem] * (2 + spa...  1.34 us
    pallas_call x1, Pallas kernels, local(): call(list_kernel, 'lists', [pltpu.SMEM((4, slots + UNROLL), jnp.int32), p...  1.05 us
    pallas_call x1, Pallas kernels, local(): call(far_kernel, 'far', [f32(spans * part, extent), f32(spans * part + le...  0.99 us
  transfers between devices with their start and end apart: 10, of which 5 were waited for; matrix products, arithmetic and copies ran while one was open for 0% of the time, Pallas kernels for 12%

profile of v3, /device:TPU:0, one launch (start us, length us, event | category | flops | bytes accessed | tf_op | source)
XLA Modules:
  0.0 44.5 jit_solution(4010801299491956612)
XLA Ops:
  0.0 0.5 %collective-permute-start.3 = (f32[32,2048]{1,0:T(8,128)}, f32[32,2048]{1,0:T(8,128)S(1)}, u32[]{:S(2)}, u32[]{:S(2)}) collective-permute-start(f32[32,2048]{1,0:T(8,128)} %sources_ref.1), channel_id=1, source_target_pairs={{0,1},{1,0},{2,3},{3,2},{4,5},{5,4},{6,7},{7,6},{8,9},{9,8},{10,11... | collective-permute-start | bytes 786440 | tf_op jit(solution)/shard_map/ppermute | solution.py:418
  1.1 1.1 %lists.1 = (s32[4,52]{1,0:T(4,128)S(4)}, s32[4]{0:T(128)S(4)}, f32[24,256]{1,0:T(8,128)S(1)}, f32[32,256]{1,0:T(8,128)S(1)}) custom-call(s32[1]{0:T(128)} %bitcast.1.place_ref, s32[48]{0:T(128)} %bitcast.11, s32[48]{0:T(128)} %bitcast.12, s32[1]{0:T(128)} %bitcast.9.count_ref), custom_call_target="tpu_custom_call" | custom-call | bytes 1048576 | tf_op jit(solution)/shard_map/lists/pallas_call | solution.py:468
  2.2 1.4 %front.1 = (bf16[512,256]{1,0:T(8,128)(2,1)S(1)}, f32[8,256]{1,0:T(8,128)S(1)}) custom-call(s32[1]{0:T(128)} %bitcast.1.place_ref, f32[32,2048]{1,0:T(8,128)} %sources_ref.1, f32[32,2048]{1,0:T(8,128)S(1)} %collective-permute-done.3.other_ref, f32[32,256]{1,0:T(8,128)S(1)} %get-tuple-element.234._), custom_call_target="tpu_custom_call" | custom-call | bytes 1048576 | tf_op jit(solution)/shard_map/front/pallas_call | solution.py:482
  3.6 3.0 %collective-permute-start.5 = (bf16[512,256]{1,0:T(8,128)(2,1)S(1)}, bf16[512,256]{1,0:T(8,128)(2,1)S(1)}, u32[]{:S(2)}, u32[]{:S(2)}) collective-permute-start(bf16[512,256]{1,0:T(8,128)(2,1)S(1)} %get-tuple-element.104), channel_id=1, source_target_pairs={{0,8},{1,24},{2,0},{3,16},{4,12},{5,28},{6,4},{7,20},{8,9},{9,25},... | collective-permute-start | bytes 786440 | tf_op jit(solution)/shard_map/ppermute | solution.py:418
  6.6 0.7 %collective-permute-start.4 = (bf16[512,256]{1,0:T(8,128)(2,1)S(1)}, bf16[512,256]{1,0:T(8,128)(2,1)S(1)}, u32[]{:S(2)}, u32[]{:S(2)}) collective-permute-start(bf16[512,256]{1,0:T(8,128)(2,1)S(1)} %get-tuple-element.104), channel_id=1, source_target_pairs={{0,0},{1,16},{2,8},{3,24},{4,4},{5,20},{6,12},{7,28},{8,1},{9,17},... | collective-permute-start | bytes 786440 | tf_op jit(solution)/shard_map/ppermute | solution.py:418
  7.3 5.8 %while.22 = (s32[]{:T(128)}, f32[24,256]{1,0:T(8,128)S(1)}, f32[32,256]{1,0:T(8,128)S(1)}, s32[]{:T(128)}, s32[1]{0:T(128)}, /*index=5*/s32[4,52]{1,0:T(4,128)S(...) while((s32[]{:T(128)}, f32[24,256]{1,0:T(8,128)S(1)}, ...), condition=%wide.region_1.2_spmd, body=%wide.region_0.1_spmd.sunk | while | flops 2 | bytes 2195597 | solution.py:462
  7.3 1.9 %edges.1 = (f32[16,256]{1,0:T(8,128)S(1)}, f32[24,256]{1,0:T(8,128)S(1)}) custom-call(s32[1]{0:T(128)} %get-tuple-element.256.place_ref, s32[1]{0:T(128)} %bitcast.8._, s32[4,52]{1,0:T(4,128)S(4)} %get-tuple-element.257.order_ref, s32[4]{0:T(128)S(4)} %get-tuple-element.258.sizes_ref, bf16[48,256,256]{2,1,0:T(8,128)(2,1)} %get-tuple-element.259.tiles_ref, ...), custom_call_target="tpu_custom_call" | custom-call | bytes 1048576 | tf_op jit(solution)/shard_map/while/body/edges/pallas_call | solution.py:499
  9.2 1.2 %collective-permute-start = (f32[24,256]{1,0:T(8,128)S(1)}, f32[24,256]{1,0:T(8,128)S(1)}, u32[]{:S(2)}, u32[]{:S(2)}) collective-permute-start(f32[24,256]{1,0:T(8,128)S(1)} %get-tuple-element.225.refs_0_), channel_id=1, source_target_pairs={{0,4},{1,5},{2,6},{3,7},{4,0},{5,1},{6,2},{7,3},{8,12},{9,13},{10,... | collective-permute-start | bytes 73736 | tf_op jit(solution)/shard_map/while/body/ppermute | solution.py:418
  10.4 2.7 %collective-permute-done.refs_1_ = f32[24,256]{1,0:T(8,128)S(1)} collective-permute-done((f32[24,256]{1,0:T(8,128)S(1)}, f32[24,256]{1,0:T(8,128)S(1)}, u32[]{:S(2)}, u32[]{:S(2)}) %collective-permute-start) | collective-permute-done | bytes 24608 | tf_op jit(solution)/shard_map/while/body/ppermute | solution.py:418
  13.1 1.2 %collective-permute-start.7 = (bf16[512,256]{1,0:T(8,128)(2,1)S(1)}, bf16[512,256]{1,0:T(8,128)(2,1)S(1)}, u32[]{:S(2)}, u32[]{:S(2)}) collective-permute-start(bf16[512,256]{1,0:T(8,128)(2,1)S(1)} %collective-permute-done.5.refs_1_), channel_id=1, source_target_pairs={{0,4},{1,5},{2,6},{3,7},{4,0},{5,1},{6,2},{7,3},{8,12},{9,13},{10,... | collective-permute-start | bytes 786440 | tf_op jit(solution)/shard_map/ppermute | solution.py:418
  14.3 0.9 %collective-permute-start.6 = (bf16[512,256]{1,0:T(8,128)(2,1)S(1)}, bf16[512,256]{1,0:T(8,128)(2,1)S(1)}, u32[]{:S(2)}, u32[]{:S(2)}) collective-permute-start(bf16[512,256]{1,0:T(8,128)(2,1)S(1)} %collective-permute-done.4.refs_0_), channel_id=1, source_target_pairs={{0,4},{1,5},{2,6},{3,7},{4,0},{5,1},{6,2},{7,3},{8,12},{9,13},{10,... | collective-permute-start | bytes 786440 | tf_op jit(solution)/shard_map/ppermute | solution.py:418
  15.2 15.0 %while.23 = (s32[]{:T(128)}, f32[24,256]{1,0:T(8,128)S(1)}, s32[]{:T(128)}, s32[1]{0:T(128)}, s32[]{:T(128)}) while((s32[]{:T(128)}, f32[24,256]{1,0:T(8,128)S(1)}, s32[]{:T(128)}, s32[1]{0:T(128)}, s32[]{:T(128)}) %tuple.40), condition=%wide.region_3.4_spmd, body=%wide.region_2.3_spmd.sunk | while | flops 2 | bytes 2293901 | solution.py:462
  15.2 7.5 %collective-permute-start.1 = (f32[24,256]{1,0:T(8,128)S(1)}, f32[24,256]{1,0:T(8,128)S(1)}, u32[]{:S(2)}, u32[]{:S(2)}) collective-permute-start(f32[24,256]{1,0:T(8,128)S(1)} %get-tuple-element.268.walk_ref), channel_id=1, source_target_pairs={{0,16},{1,17},{2,18},{3,19},{4,20},{5,21},{6,22},{7,23},{8,24},{9,... | collective-permute-start | bytes 73736 | tf_op jit(solution)/shard_map/while/body/ppermute | solution.py:418
  22.7 1.8 %collective-permute-done.1.partner_ref = f32[24,256]{1,0:T(8,128)S(1)} collective-permute-done((f32[24,256]{1,0:T(8,128)S(1)}, f32[24,256]{1,0:T(8,128)S(1)}, u32[]{:S(2)}, u32[]{:S(2)}) %collective-permute-start.1) | collective-permute-done | bytes 24608 | tf_op jit(solution)/shard_map/while/body/ppermute | solution.py:418
  24.5 3.9 %collective-permute-start.2 = (f32[24,256]{1,0:T(8,128)S(1)}, f32[24,256]{1,0:T(8,128)S(1)}, u32[]{:S(2)}, u32[]{:S(2)}) collective-permute-start(f32[24,256]{1,0:T(8,128)S(1)} %z_level.2.walk_ref), channel_id=1, source_target_pairs={{0,8},{1,9},{2,10},{3,11},{4,12},{5,13},{6,14},{7,15},{8,0},{9,1},... | collective-permute-start | bytes 73736 | tf_op jit(solution)/shard_map/while/body/ppermute | solution.py:418
  28.4 1.8 %collective-permute-done.2.partner_ref = f32[24,256]{1,0:T(8,128)S(1)} collective-permute-done((f32[24,256]{1,0:T(8,128)S(1)}, f32[24,256]{1,0:T(8,128)S(1)}, u32[]{:S(2)}, u32[]{:S(2)}) %collective-permute-start.2) | collective-permute-done | bytes 24608 | tf_op jit(solution)/shard_map/while/body/ppermute | solution.py:418
  30.3 2.2 %near.1 = (f32[9,128,256]{2,1,0:T(8,128)S(1)}, bf16[56,256,256]{2,1,0:T(8,128)(2,1)S(1)}) custom-call(s32[1]{0:T(128)} %bitcast.1.place_ref, s32[4,52]{1,0:T(4,128)S(4)} %get-tuple-element.237.order_ref, s32[4]{0:T(128)S(4)} %get-tuple-element.238.sizes_ref, bf16[48,256,256]{2,1,0:T(8,128)(2,1)} %get-tuple-element.296, ...), custom_call_target="tpu_custom_call" | custom-call | bytes 1048576 | tf_op jit(solution)/shard_map/near/pallas_call | solution.py:548
  32.5 1.0 %far.1 = (f32[512,256]{1,0:T(8,128)S(1)}, f32[528,256]{1,0:T(8,128)S(1)}) custom-call(s32[1]{0:T(128)} %bitcast.1.place_ref, s32[4,52]{1,0:T(4,128)S(4)} %get-tuple-element.237.order_ref, s32[4]{0:T(128)S(4)} %get-tuple-element.238.sizes_ref, bf16[56,256,256]{2,1,0:T(8,128)(2,1)S(1)} %get-tuple-element.109.tiles_ref, ...), custom_call_target="tpu_custom_call" | custom-call | bytes 1048576 | tf_op jit(solution)/shard_map/far/pallas_call | solution.py:560
  33.5 0.1 collective-permute-start.8
  33.5 1.9 %collective-permute-done.8.arrived_ref = f32[528,256]{1,0:T(8,128)S(1)} collective-permute-done((f32[528,256]{1,0:T(8,128)S(1)}, f32[528,256]{1,0:T(8,128)S(1)}, u32[]{:S(2)}, u32[]{:S(2)}) %collective-permute-start.8) | collective-permute-done | bytes 540704 | tf_op jit(solution)/shard_map/ppermute | solution.py:418
  35.5 0.1 combine.1
  35.5 3.1 %collective-permute-start.9 = (bf16[320,256]{1,0:T(8,128)(2,1)S(1)}, bf16[320,256]{1,0:T(8,128)(2,1)S(1)}, u32[]{:S(2)}, u32[]{:S(2)}) collective-permute-start(bf16[320,256]{1,0:T(8,128)(2,1)S(1)} %get-tuple-element.119), channel_id=1, source_target_pairs={{0,2},{1,3},{2,0},{3,1},{4,6},{5,7},{6,4},{7,5},{8,10},{9,11},{10,... | collective-permute-start | bytes 491528 | tf_op jit(solution)/shard_map/ppermute | solution.py:418
  38.7 4.5 %collective-permute-done.9.refs_0_ = bf16[320,256]{1,0:T(8,128)(2,1)S(1)} collective-permute-done((bf16[320,256]{1,0:T(8,128)(2,1)S(1)}, bf16[320,256]{1,0:T(8,128)(2,1)S(1)}, u32[]{:S(2)}, u32[]{:S(2)}) %collective-permute-start.9) | collective-permute-done | bytes 163872 | tf_op jit(solution)/shard_map/ppermute | solution.py:418
  43.2 1.3 %back.1 = f32[32,2048]{1,0:T(8,128)} custom-call(s32[1]{0:T(128)} %bitcast.1.place_ref, f32[256,256]{1,0:T(8,128)S(1)} %get-tuple-element.116.own_ref, f32[32,256]{1,0:T(8,128)S(1)} %get-tuple-element.117.both_ref, f32[8,256]{1,0:T(8,128)S(1)} %get-tuple-element.118.firsts_ref, bf16[320,256]{1,0:T(8,128)(2,1)S(1)} %collective-permute-done.9.refs_0_), custom_call_target="tpu_custom_call" | custom-call | bytes 1048576 | tf_op jit(solution)/shard_map/back/pallas_call | solution.py:585
  (9 shorter events, 0.1 us)
Async XLA Ops:
  0.0 2.2 %collective-permute-start.3 = (f32[32,2048]{1,0:T(8,128)}, f32[32,2048]{1,0:T(8,128)S(1)}, u32[]{:S(2)}, u32[]{:S(2)}) collective-permute-start(f32[32,2048]{1,0:T(8,128)} %sources_ref.1), channel_id=1, source_target_pairs={{0,1},{1,0},{2,3},{3,2},{4,5},{5,4},{6,7},{7,6},{8,9},{9,8},{10,11... | collective-permute-start | bytes 786440 | tf_op jit(solution)/shard_map/ppermute | solution.py:418
  3.6 9.5 %collective-permute-start.5 = (bf16[512,256]{1,0:T(8,128)(2,1)S(1)}, bf16[512,256]{1,0:T(8,128)(2,1)S(1)}, u32[]{:S(2)}, u32[]{:S(2)}) collective-permute-start(bf16[512,256]{1,0:T(8,128)(2,1)S(1)} %get-tuple-element.104), channel_id=1, source_target_pairs={{0,8},{1,24},{2,0},{3,16},{4,12},{5,28},{6,4},{7,20},{8,9},{9,25},... | collective-permute-start | bytes 786440 | tf_op jit(solution)/shard_map/ppermute | solution.py:418
  6.6 7.7 %collective-permute-start.4 = (bf16[512,256]{1,0:T(8,128)(2,1)S(1)}, bf16[512,256]{1,0:T(8,128)(2,1)S(1)}, u32[]{:S(2)}, u32[]{:S(2)}) collective-permute-start(bf16[512,256]{1,0:T(8,128)(2,1)S(1)} %get-tuple-element.104), channel_id=1, source_target_pairs={{0,0},{1,16},{2,8},{3,24},{4,4},{5,20},{6,12},{7,28},{8,1},{9,17},... | collective-permute-start | bytes 786440 | tf_op jit(solution)/shard_map/ppermute | solution.py:418
  9.2 3.9 %collective-permute-start = (f32[24,256]{1,0:T(8,128)S(1)}, f32[24,256]{1,0:T(8,128)S(1)}, u32[]{:S(2)}, u32[]{:S(2)}) collective-permute-start(f32[24,256]{1,0:T(8,128)S(1)} %get-tuple-element.225.refs_0_), channel_id=1, source_target_pairs={{0,4},{1,5},{2,6},{3,7},{4,0},{5,1},{6,2},{7,3},{8,12},{9,13},{10,... | collective-permute-start | bytes 73736 | tf_op jit(solution)/shard_map/while/body/ppermute | solution.py:418
  13.1 19.4 %collective-permute-start.7 = (bf16[512,256]{1,0:T(8,128)(2,1)S(1)}, bf16[512,256]{1,0:T(8,128)(2,1)S(1)}, u32[]{:S(2)}, u32[]{:S(2)}) collective-permute-start(bf16[512,256]{1,0:T(8,128)(2,1)S(1)} %collective-permute-done.5.refs_1_), channel_id=1, source_target_pairs={{0,4},{1,5},{2,6},{3,7},{4,0},{5,1},{6,2},{7,3},{8,12},{9,13},{10,... | collective-permute-start | bytes 786440 | tf_op jit(solution)/shard_map/ppermute | solution.py:418
  14.3 18.1 %collective-permute-start.6 = (bf16[512,256]{1,0:T(8,128)(2,1)S(1)}, bf16[512,256]{1,0:T(8,128)(2,1)S(1)}, u32[]{:S(2)}, u32[]{:S(2)}) collective-permute-start(bf16[512,256]{1,0:T(8,128)(2,1)S(1)} %collective-permute-done.4.refs_0_), channel_id=1, source_target_pairs={{0,4},{1,5},{2,6},{3,7},{4,0},{5,1},{6,2},{7,3},{8,12},{9,13},{10,... | collective-permute-start | bytes 786440 | tf_op jit(solution)/shard_map/ppermute | solution.py:418
  15.2 9.3 %collective-permute-start.1 = (f32[24,256]{1,0:T(8,128)S(1)}, f32[24,256]{1,0:T(8,128)S(1)}, u32[]{:S(2)}, u32[]{:S(2)}) collective-permute-start(f32[24,256]{1,0:T(8,128)S(1)} %get-tuple-element.268.walk_ref), channel_id=1, source_target_pairs={{0,16},{1,17},{2,18},{3,19},{4,20},{5,21},{6,22},{7,23},{8,24},{9,... | collective-permute-start | bytes 73736 | tf_op jit(solution)/shard_map/while/body/ppermute | solution.py:418
  24.5 5.7 %collective-permute-start.2 = (f32[24,256]{1,0:T(8,128)S(1)}, f32[24,256]{1,0:T(8,128)S(1)}, u32[]{:S(2)}, u32[]{:S(2)}) collective-permute-start(f32[24,256]{1,0:T(8,128)S(1)} %z_level.2.walk_ref), channel_id=1, source_target_pairs={{0,8},{1,9},{2,10},{3,11},{4,12},{5,13},{6,14},{7,15},{8,0},{9,1},... | collective-permute-start | bytes 73736 | tf_op jit(solution)/shard_map/while/body/ppermute | solution.py:418
  33.5 2.0 %collective-permute-start.8 = (f32[528,256]{1,0:T(8,128)S(1)}, f32[528,256]{1,0:T(8,128)S(1)}, u32[]{:S(2)}, u32[]{:S(2)}) collective-permute-start(f32[528,256]{1,0:T(8,128)S(1)} %get-tuple-element.115), channel_id=1, source_target_pairs={{0,1},{1,0},{2,3},{3,2},{4,5},{5,4},{6,7},{7,6},{8,9},{9,8},{10,11... | collective-permute-start | bytes 1622024 | tf_op jit(solution)/shard_map/ppermute | solution.py:418
  35.5 7.6 %collective-permute-start.9 = (bf16[320,256]{1,0:T(8,128)(2,1)S(1)}, bf16[320,256]{1,0:T(8,128)(2,1)S(1)}, u32[]{:S(2)}, u32[]{:S(2)}) collective-permute-start(bf16[320,256]{1,0:T(8,128)(2,1)S(1)} %get-tuple-element.119), channel_id=1, source_target_pairs={{0,2},{1,3},{2,0},{3,1},{4,6},{5,7},{6,4},{7,5},{8,10},{9,11},{10,... | collective-permute-start | bytes 491528 | tf_op jit(solution)/shard_map/ppermute | solution.py:418

commit v4 on v3

--- a/solution.py
+++ b/solution.py
@@ -11,6 +11,7 @@
 ROOT_HALF = 1.0 / math.sqrt(2.0)
 SIDE_ROWS = 16
 UNROLL = 4
+AHEAD = 16
 LANES = 128
 MIB = 2**20
 
@@ -37,8 +38,8 @@
     return high, middle, low
 
 
-def exact_dot(value, signs):
-    return sum(jnp.dot(term, signs, preferred_element_type=jnp.float32) for term in three_terms(value))
+def exact_dot(value, signs, terms=3):
+    return sum(jnp.dot(term, signs, preferred_element_type=jnp.float32) for term in three_terms(value)[:terms])
 
 
 def block_forward(columns):
@@ -84,7 +85,7 @@
 
 
 def source_span(place_ref, m, spans):
-    return (z_of(place_ref) & (spans - 1)) ^ m
+    return (z_of(place_ref) ^ m ^ (spans - 1)) & (spans - 1)
 
 
 def front_kernel(place_ref, sources_ref, other_ref, _, out_ref, first_ref, mine_ref, sem, *, blocks, extent):
@@ -229,7 +230,7 @@
             rest_ref[i * length : (i + 1) * length, :] = value
 
 
-def z_level_kernel(place_ref, walk_ref, partner_ref, out_ref, *, bit, length):
+def z_level_kernel(place_ref, walk_ref, partner_ref, _, out_ref, *, bit, length):
     walk, partner = walk_ref[...], partner_ref[...]
     row = lax.broadcasted_iota(jnp.int32, walk.shape, 0)
     out_ref[...] = jnp.where(row < length, butterfly(walk, partner, z_of(place_ref), bit), walk + partner)
@@ -263,55 +264,84 @@
             sides[behind * blocks + b, rows, :] = message[b * pair : (b + 1) * pair, :]
 
 
-def add_products(order_ref, sizes_ref, which, first, tiles_ref, sides, acc, sems=None):
-    def group(index, _):
-        if sems is not None:
-            for k in range(UNROLL):
-                at = first + index * UNROLL + k
-                pltpu.make_async_copy(tiles_ref.at[at], tiles_ref.at[at], sems.at[at]).wait()
-        for k in range(UNROLL):
-            entry = order_ref[which, index * UNROLL + k]
-            side, row = (entry >> 8) & 255, entry & 255
-            tile = tiles_ref[first + index * UNROLL + k]
-            acc[row] += jnp.dot(sides[side], tile, preferred_element_type=jnp.float32)
-        return 0
-
-    lax.fori_loop(0, groups_of(sizes_ref, which), group, 0)
-
-
 def groups_of(sizes_ref, which):
     return (sizes_ref[which] + UNROLL - 1) // UNROLL
 
 
-def near_kernel(place_ref, order_ref, sizes_ref, tiles_ref, _, *refs, blocks, spans):
-    *messages, acc_ref, held_ref, sides, sems = refs
-    near_places = groups_of(sizes_ref, 0) * UNROLL
-    far_places = groups_of(sizes_ref, 1) * UNROLL
-
-    def fetch(which, index, at):
-        slot = order_ref[which, index] >> 16
-        return pltpu.make_async_copy(tiles_ref.at[slot], held_ref.at[at], sems.at[at])
-
-    lax.fori_loop(0, near_places, lambda i, _: (fetch(0, i, i).start(), 0)[1], 0)
-    lax.fori_loop(0, far_places, lambda i, _: (fetch(1, i, near_places + i).start(), 0)[1], 0)
+def tile_copy(order_ref, which, index, tiles_ref, held, sems, at):
+    slot = order_ref[which, index] >> 16
+    return pltpu.make_async_copy(tiles_ref.at[slot], held.at[at], sems.at[at])
+
+
+def add_group(order_ref, which, index, held, sides, acc):
+    for k in range(UNROLL):
+        entry = order_ref[which, index * UNROLL + k]
+        side, row = (entry >> 8) & 255, entry & 255
+        acc[row] += jnp.dot(sides[side], held[index * UNROLL + k], preferred_element_type=jnp.float32)
+
+
+def blank_kernel(_, sum_ref, ahead_ref):
+    sum_ref[0] = jnp.zeros(sum_ref.shape[1:], jnp.float32)
+    ahead_ref[0] = jnp.zeros(ahead_ref.shape[1:], jnp.bfloat16)
+
+
+def near_kernel(place_ref, _, order_ref, sizes_ref, tiles_ref, *refs, blocks, spans):
+    *messages, acc_ref, ahead_ref, sides, held, sems, ahead_sems = refs
+    groups = groups_of(sizes_ref, 0)
+    ahead = jnp.minimum(groups_of(sizes_ref, 1) * UNROLL, AHEAD)
+
+    def own(i):
+        return tile_copy(order_ref, 0, i, tiles_ref, held, sems, i)
+
+    def other(i):
+        return tile_copy(order_ref, 1, i, tiles_ref, ahead_ref, ahead_sems, i)
+
+    lax.fori_loop(0, groups * UNROLL, lambda i, _: (own(i).start(), 0)[1], 0)
+    lax.fori_loop(0, ahead, lambda i, _: (other(i).start(), 0)[1], 0)
     fill_sides(sides, messages, place_ref, blocks, spans)
     acc_ref[...] = jnp.zeros_like(acc_ref)
-    add_products(order_ref, sizes_ref, 0, 0, held_ref, sides, acc_ref, sems)
-    lax.fori_loop(0, far_places, lambda i, _: (fetch(1, i, near_places + i).wait(), 0)[1], 0)
+
+    def group(index, _):
+        for k in range(UNROLL):
+            own(index * UNROLL + k).wait()
+        add_group(order_ref, 0, index, held, sides, acc_ref)
+        return 0
+
+    lax.fori_loop(0, groups, group, 0)
+    lax.fori_loop(0, ahead, lambda i, _: (other(i).wait(), 0)[1], 0)
 
 
 def far_kernel(
-    place_ref, order_ref, sizes_ref, tiles_ref, near_ref, row_ref, cols_ref, *refs, blocks, owners, spans
+    place_ref, order_ref, sizes_ref, tiles_ref, near_ref, ahead_ref, row_ref, cols_ref, *refs, blocks, owners, spans
 ):
     messages = refs[: owners * spans]
-    keep_ref, send_ref, sides, acc = refs[owners * spans :]
+    keep_ref, send_ref, sides, acc, held, sems = refs[owners * spans :]
+    groups = groups_of(sizes_ref, 1)
+    ahead = jnp.minimum(groups, AHEAD // UNROLL)
+
+    def fetch(i):
+        return tile_copy(order_ref, 1, i, tiles_ref, held, sems, i)
+
+    lax.fori_loop(ahead * UNROLL, groups * UNROLL, lambda i, _: (fetch(i).start(), 0)[1], 0)
     extent = tiles_ref.shape[-1]
     pair = sides.shape[1] // spans
     height = pair // 2
     x = x_of(place_ref)
     fill_sides(sides, messages[spans:], place_ref, blocks, spans)
     acc[...] = near_ref[...]
-    add_products(order_ref, sizes_ref, 1, groups_of(sizes_ref, 0) * UNROLL, tiles_ref, sides, acc)
+
+    def ready(index, _):
+        add_group(order_ref, 1, index, ahead_ref, sides, acc)
+        return 0
+
+    def group(index, _):
+        for k in range(UNROLL):
+            fetch(index * UNROLL + k).wait()
+        add_group(order_ref, 1, index, held, sides, acc)
+        return 0
+
+    lax.fori_loop(0, ahead, ready, 0)
+    lax.fori_loop(ahead, groups, group, 0)
 
     lane = lax.broadcasted_iota(jnp.int32, (pair, extent), 1)
     for m in range(spans):
@@ -348,12 +378,11 @@
     both_ref[length:, :] = jnp.where(first_core, other, mine)
     at = pl.ds(pl.multiple_of(span * rows, rows), rows)
     own_ref[...] = keep_ref[at, :] + arrived_ref[at, :]
-    high, low, _ = three_terms(both_ref[...])
+    both = both_ref[...].astype(jnp.bfloat16)
     for j, out_ref in enumerate(out_refs, 1):
         at = pl.ds(pl.multiple_of(lax.rem(span + j, spans) * rows, rows), rows)
         out_ref[0:rows, :] = (keep_ref[at, :] + arrived_ref[at, :]).astype(jnp.bfloat16)
-        out_ref[rows : rows + 2 * length, :] = high
-        out_ref[rows + 2 * length :, :] = low
+        out_ref[rows:, :] = both
 
 
 def back_kernel(place_ref, own_ref, both_ref, firsts_ref, *refs, blocks, owners):
@@ -362,15 +391,13 @@
     extent = own_ref.shape[1]
     rows = own_ref.shape[0]
     height = rows // blocks
-    length = owners * blocks
     span = span_of(place_ref)
     total = own_ref[...]
     for part in arrived:
         total = total + part[0:rows, :].astype(jnp.float32)
     tables, picked = [both_ref[...]], []
     for part in arrived:
-        high, low = part[rows : rows + 2 * length, :], part[rows + 2 * length :, :]
-        tables.append(high.astype(jnp.float32) + low.astype(jnp.float32))
+        tables.append(part[rows:, :].astype(jnp.float32))
     for j in range(spans):
         source = lax.rem(span - j + spans, spans)
         for k in range(2 * owners):
@@ -391,7 +418,7 @@
     lane = lax.broadcasted_iota(jnp.int32, (height, extent), 1)
     fixed = jnp.concatenate([jnp.where(lane == 0, columns[b], blocks_of[b]) for b in range(blocks)], axis=0)
     signs, scale = haar_parts(extent, True)
-    result = exact_dot(fixed * scale, signs)
+    result = exact_dot(fixed * scale, signs, 2)
     for b in range(blocks):
         out_ref[:, b * extent : (b + 1) * extent] = result[b * height : (b + 1) * height, :]
 
@@ -465,6 +492,7 @@
     stack = in_hbm(tiles.reshape(slots, extent, extent))
     from_core = other_core(sources)
     gathered = -(-n_row // 8) * 8
+    every = (spans * pair, extent)
     order, sizes, blank_walk, blank_rest = call(
         list_kernel,
         "lists",
@@ -490,10 +518,10 @@
         extent=extent,
     )(place, in_hbm(sources), from_core, blank_rest)
 
-    def spread(message, m):
-        return moved(message, lambda zz, xx, yy, cc: (cc * spans + (yy ^ m), xx, zz // 2, zz % 2))
-
-    direct = [spread(message, m) for m in range(spans)]
+    direct = [
+        moved(message, lambda zz, xx, yy, cc, m=m: (cc * spans + (yy ^ m ^ (spans - 1)), xx, zz // 2, zz % 2))
+        for m in range(spans)
+    ]
 
     def early(trip, _):
         cols, line = call(
@@ -520,19 +548,38 @@
             [vmem] * 2,
         )(place, cols, line, *behind)
 
-    def z_levels(walk, bits):
-        for bit in bits:
+    walk, rest = apart(early, blank_walk, blank_rest)
+    swapped = [along_x(after(piece, walk), j) for j in range(1, owners) for piece in direct]
+
+    held_tiles = [
+        pltpu.VMEM((slots + UNROLL, extent, extent), jnp.bfloat16),
+        pltpu.SemaphoreType.DMA((slots + UNROLL,)),
+    ]
+
+    sum_shape, ahead_shape = (blocks + 1, *every), (AHEAD, extent, extent)
+    later = [kept(*sum_shape), pltpu.VMEM(ahead_shape, jnp.bfloat16)]
+    blank_sum, blank_ahead = call(blank_kernel, "blank", later, [unread], [vmem] * 2)(walk)
+
+    def late(trip, state):
+        walk, *_ = state
+        near, ahead = call(
+            near_kernel,
+            "near",
+            later,
+            [smem] * 4 + [hbm] + [vmem] * len(direct),
+            [vmem] * 2,
+            scratch=[pltpu.VMEM((blocks, *every), jnp.bfloat16), *held_tiles, pltpu.SemaphoreType.DMA((AHEAD,))],
+            blocks=blocks,
+            spans=spans,
+        )(place, trip.reshape(1), order, sizes, stack, *direct)
+        for bit in reversed(range((n_row // owners).bit_length() - 1)):
             partner = moved(walk, lambda zz, xx, yy, cc, bit=bit: (zz ^ 2**bit, xx, yy, cc))
             walk = call(
-                z_level_kernel, "z_level", kept(*walk.shape), [smem, vmem, vmem], vmem, bit=bit, length=length
-            )(place, walk, partner)
-        return walk
-
-    walk, rest = apart(early, blank_walk, blank_rest)
-    swapped = [along_x(after(piece, walk), j) for j in range(1, owners) for piece in direct]
-    z_bits = list(reversed(range((n_row // owners).bit_length() - 1)))
-    walk = apart(lambda _, walk: z_levels(walk, z_bits), after(walk, *direct))
-
+                z_level_kernel, "z_level", kept(*walk.shape), [smem, vmem, vmem, unread], vmem, bit=bit, length=length
+            )(place, walk, partner, near)
+        return walk, near, ahead
+
+    walk, near, ahead = apart(late, after(walk, *direct), blank_sum, blank_ahead)
     first_row, first_cols, firsts = call(
         coarse_kernel,
         "coarse",
@@ -543,39 +590,27 @@
         rows=n_row,
     )(place, walk, rest)
 
-    every = (spans * pair, extent)
-    places = slots + 2 * UNROLL
-    near, held = call(
-        near_kernel,
-        "near",
-        [f32(blocks + 1, *every), pltpu.VMEM((places, extent, extent), jnp.bfloat16)],
-        [smem] * 3 + [hbm, unread] + [vmem] * len(direct),
-        [vmem] * 2,
-        scratch=[pltpu.VMEM((blocks, *every), jnp.bfloat16), pltpu.SemaphoreType.DMA((places,))],
-        blocks=blocks,
-        spans=spans,
-    )(place, order, sizes, stack, first_row, *direct)
-
     part = blocks * height
     keep, send = call(
         far_kernel,
         "far",
         [f32(spans * part, extent), f32(spans * part + length, extent)],
-        [smem] * 3 + [vmem] * (4 + len(direct) + len(swapped)),
+        [smem] * 3 + [hbm] + [vmem] * (4 + len(direct) + len(swapped)),
         [vmem] * 2,
         scratch=[
             pltpu.VMEM(((owners - 1) * blocks, *every), jnp.bfloat16),
             pltpu.VMEM((blocks + 1, *every), jnp.float32),
+            *held_tiles,
         ],
         blocks=blocks,
         owners=owners,
         spans=spans,
-    )(place, order, sizes, held, near, first_row, first_cols, *direct, *swapped)
+    )(place, order, sizes, stack, near, ahead, first_row, first_cols, *direct, *swapped)
 
     own, both, *outgoing = call(
         combine_kernel,
         "combine",
-        [f32(part, extent), f32(2 * length, extent)] + [bf16(part + 4 * length, extent)] * (spans - 1),
+        [f32(part, extent), f32(2 * length, extent)] + [bf16(part + 2 * length, extent)] * (spans - 1),
         [smem, vmem, vmem, vmem],
         [vmem] * (spans + 1),
     )(place, keep, other_core(send), first_cols)

time: 44.6 us -> 44.5 us (level)
  Pallas kernels: 8.98 us -> 13.6 us
  starting transfers between devices: 22 us -> 18.1 us
  waiting for transfers between devices: 12.7 us -> 12.1 us
    ppermute x10, starting transfers between devices: 22 us -> 18.1 us  [moved(): return lax.ppermute(value, ('row', 'col'), pairs)]
    pallas_call x1, Pallas kernels: 0.99 us -> 3.12 us  [local(): call(far_kernel, 'far', [f32(spans * part, extent), f32(spans * part + le...]
    pallas_call x3 -> x4, Pallas kernels: 2.21 us -> 3.91 us  [the longest x1 3.88 us: late(): call(near_kernel, 'near', later, [smem] * 4 + [hbm] + [vmem] * len(direct...]
    ppermute x10, waiting for transfers between devices: 12.7 us -> 12.1 us  [moved(): return lax.ppermute(value, ('row', 'col'), pairs)]
    pallas_call x1, Pallas kernels: 1.05 us -> 1.52 us  [local(): call(list_kernel, 'lists', [pltpu.SMEM((4, slots + UNROLL), jnp.int32), p...]
  transfers between devices with their start and end apart: 10 -> 10, of which waited for: 5 -> 4; matrix products, arithmetic and copies ran while one was open for 0% -> 0% of each run, Pallas kernels for 12% -> 17%
where the time goes in v4:
time: 44.5 us; the launch traced here: 44.6 us
  starting transfers between devices  18.1 us (41%)
  Pallas kernels  13.6 us (31%)
  waiting for transfers between devices  12.1 us (27%)
  between operations  0.74 us (2%)
    ppermute x10, starting transfers between devices, moved(): return lax.ppermute(value, ('row', 'col'), pairs)  18.1 us
    ppermute x10, waiting for transfers between devices, moved(): return lax.ppermute(value, ('row', 'col'), pairs)  12.1 us
    pallas_call x1, Pallas kernels, late(): call(near_kernel, 'near', later, [smem] * 4 + [hbm] + [vmem] * len(direct...  3.88 us
    pallas_call x1, Pallas kernels, local(): call(far_kernel, 'far', [f32(spans * part, extent), f32(spans * part + le...  3.12 us
    pallas_call x1, Pallas kernels, early(): call(edge_kernel, 'edges', [f32(length, extent), f32(length + gathered, e...  2.2 us
    pallas_call x1, Pallas kernels, local(): call(list_kernel, 'lists', [pltpu.SMEM((4, slots + UNROLL), jnp.int32), p...  1.52 us
    pallas_call x1, Pallas kernels, local(): call(front_kernel, 'front', [bf16(blocks * pair, extent), f32(8, extent)]...  1.45 us
    pallas_call x1, Pallas kernels, local(): call(back_kernel, 'back', f32(*sources.shape), [smem] + [vmem] * (2 + spa...  1.27 us
  transfers between devices with their start and end apart: 10, of which 4 were waited for; matrix products, arithmetic and copies ran while one was open for 0% of the time, Pallas kernels for 17%

profile of v4, /device:TPU:0, one launch (start us, length us, event | category | flops | bytes accessed | tf_op | source)
XLA Modules:
  0.0 44.6 jit_solution(8372372388284998090)
XLA Ops:
  0.0 0.5 %collective-permute-start.3 = (f32[32,2048]{1,0:T(8,128)}, f32[32,2048]{1,0:T(8,128)S(1)}, u32[]{:S(2)}, u32[]{:S(2)}) collective-permute-start(f32[32,2048]{1,0:T(8,128)} %sources_ref.1), channel_id=1, source_target_pairs={{0,1},{1,0},{2,3},{3,2},{4,5},{5,4},{6,7},{7,6},{8,9},{9,8},{10,11... | collective-permute-start | bytes 786440 | tf_op jit(solution)/shard_map/ppermute | solution.py:445
  1.1 1.5 %lists.1 = (s32[4,52]{1,0:T(4,128)S(4)}, s32[4]{0:T(128)S(4)}, f32[24,256]{1,0:T(8,128)S(1)}, f32[32,256]{1,0:T(8,128)S(1)}) custom-call(s32[1]{0:T(128)} %bitcast.2.place_ref, s32[48]{0:T(128)} %bitcast.14, s32[48]{0:T(128)} %bitcast.15, s32[1]{0:T(128)} %bitcast.12.count_ref), custom_call_target="tpu_custom_call" | custom-call | bytes 1048576 | tf_op jit(solution)/shard_map/lists/pallas_call | solution.py:496
  2.6 0.0 collective-permute-done.3.other_ref
  2.6 1.4 %front.1 = (bf16[512,256]{1,0:T(8,128)(2,1)S(1)}, f32[8,256]{1,0:T(8,128)S(1)}) custom-call(s32[1]{0:T(128)} %bitcast.2.place_ref, f32[32,2048]{1,0:T(8,128)} %sources_ref.1, f32[32,2048]{1,0:T(8,128)S(1)} %collective-permute-done.3.other_ref, f32[32,256]{1,0:T(8,128)S(1)} %get-tuple-element.329._), custom_call_target="tpu_custom_call" | custom-call | bytes 1048576 | tf_op jit(solution)/shard_map/front/pallas_call | solution.py:510
  4.1 2.6 %collective-permute-start.4 = (bf16[512,256]{1,0:T(8,128)(2,1)S(1)}, bf16[512,256]{1,0:T(8,128)(2,1)}, u32[]{:S(2)}, u32[]{:S(2)}) collective-permute-start(bf16[512,256]{1,0:T(8,128)(2,1)S(1)} %get-tuple-element.141), channel_id=1, source_target_pairs={{0,8},{1,24},{2,0},{3,16},{4,12},{5,28},{6,4},{7,20},{8,9},{9,25},... | collective-permute-start | bytes 786440 | tf_op jit(solution)/shard_map/ppermute | solution.py:445
  6.7 1.3 %collective-permute-start.5 = (bf16[512,256]{1,0:T(8,128)(2,1)S(1)}, bf16[512,256]{1,0:T(8,128)(2,1)}, u32[]{:S(2)}, u32[]{:S(2)}) collective-permute-start(bf16[512,256]{1,0:T(8,128)(2,1)S(1)} %get-tuple-element.141), channel_id=1, source_target_pairs={{0,0},{1,16},{2,8},{3,24},{4,4},{5,20},{6,12},{7,28},{8,1},{9,17},... | collective-permute-start | bytes 786440 | tf_op jit(solution)/shard_map/ppermute | solution.py:445
  8.0 6.1 %while.26 = (s32[]{:T(128)}, f32[24,256]{1,0:T(8,128)S(1)}, f32[32,256]{1,0:T(8,128)S(1)}, s32[]{:T(128)}, s32[1]{0:T(128)}, /*index=5*/s32[4,52]{1,0:T(4,128)S(...) while((s32[]{:T(128)}, f32[24,256]{1,0:T(8,128)S(1)}, ...), condition=%wide.region_1.2_spmd, body=%wide.region_0.1_spmd.sunk | while | flops 2 | bytes 2195597 | solution.py:489
  8.0 2.2 %edges.1 = (f32[16,256]{1,0:T(8,128)S(1)}, f32[24,256]{1,0:T(8,128)S(1)}) custom-call(s32[1]{0:T(128)} %get-tuple-element.351.place_ref, s32[1]{0:T(128)} %bitcast.10._, s32[4,52]{1,0:T(4,128)S(4)} %get-tuple-element.352.order_ref, s32[4]{0:T(128)S(4)} %get-tuple-element.353.sizes_ref, bf16[48,256,256]{2,1,0:T(8,128)(2,1)} %get-tuple-element.354.tiles_ref, ...), custom_call_target="tpu_custom_call" | custom-call | bytes 1048576 | tf_op jit(solution)/shard_map/while/body/edges/pallas_call | solution.py:527
  10.3 1.2 %collective-permute-start = (f32[24,256]{1,0:T(8,128)S(1)}, f32[24,256]{1,0:T(8,128)S(1)}, u32[]{:S(2)}, u32[]{:S(2)}) collective-permute-start(f32[24,256]{1,0:T(8,128)S(1)} %get-tuple-element.313.refs_0_), channel_id=1, source_target_pairs={{0,4},{1,5},{2,6},{3,7},{4,0},{5,1},{6,2},{7,3},{8,12},{9,13},{10,... | collective-permute-start | bytes 73736 | tf_op jit(solution)/shard_map/while/body/ppermute | solution.py:445
  11.4 2.7 %collective-permute-done.refs_1_ = f32[24,256]{1,0:T(8,128)S(1)} collective-permute-done((f32[24,256]{1,0:T(8,128)S(1)}, f32[24,256]{1,0:T(8,128)S(1)}, u32[]{:S(2)}, u32[]{:S(2)}) %collective-permute-start) | collective-permute-done | bytes 24608 | tf_op jit(solution)/shard_map/while/body/ppermute | solution.py:445
  14.2 1.2 %collective-permute-start.6 = (bf16[512,256]{1,0:T(8,128)(2,1)}, bf16[512,256]{1,0:T(8,128)(2,1)}, u32[]{:S(2)}, u32[]{:S(2)}) collective-permute-start(bf16[512,256]{1,0:T(8,128)(2,1)} %collective-permute-done.4.refs_0_), channel_id=1, source_target_pairs={{0,4},{1,5},{2,6},{3,7},{4,0},{5,1},{6,2},{7,3},{8,12},{9,13},{10,... | collective-permute-start | bytes 786440 | tf_op jit(solution)/shard_map/ppermute | solution.py:445
  15.4 0.9 %collective-permute-start.7 = (bf16[512,256]{1,0:T(8,128)(2,1)}, bf16[512,256]{1,0:T(8,128)(2,1)}, u32[]{:S(2)}, u32[]{:S(2)}) collective-permute-start(bf16[512,256]{1,0:T(8,128)(2,1)} %collective-permute-done.5.refs_1_), channel_id=1, source_target_pairs={{0,4},{1,5},{2,6},{3,7},{4,0},{5,1},{6,2},{7,3},{8,12},{9,13},{10,... | collective-permute-start | bytes 786440 | tf_op jit(solution)/shard_map/ppermute | solution.py:445
  16.3 14.8 %while.27 = (s32[]{:T(128)}, f32[24,256]{1,0:T(8,128)S(1)}, f32[9,128,256]{2,1,0:T(8,128)S(1)}, bf16[16,256,256]{2,1,0:T(8,128)(2,1)S(1)}, s32[]{:T(128)}, /*ind...) while((s32[]{:T(128)}, f32[24,256]{1,0:T(8,128)S(1)}, ...), condition=%wide.region_3.4_spmd, body=%wide.region_2.3_spmd.sunk | while | flops 2 | bytes 3342533 | solution.py:489
  16.3 6.9 %collective-permute-start.1 = (f32[24,256]{1,0:T(8,128)S(1)}, f32[24,256]{1,0:T(8,128)S(1)}, u32[]{:S(2)}, u32[]{:S(2)}) collective-permute-start(f32[24,256]{1,0:T(8,128)S(1)} %get-tuple-element.370.walk_ref), channel_id=1, source_target_pairs={{0,16},{1,17},{2,18},{3,19},{4,20},{5,21},{6,22},{7,23},{8,24},{9,... | collective-permute-start | bytes 73736 | tf_op jit(solution)/shard_map/while/body/ppermute | solution.py:445
  23.2 3.9 %near.1 = (f32[9,128,256]{2,1,0:T(8,128)S(1)}, bf16[16,256,256]{2,1,0:T(8,128)(2,1)S(1)}) custom-call(s32[1]{0:T(128)} %get-tuple-element.386.place_ref, s32[1]{0:T(128)} %bitcast.11._, s32[4,52]{1,0:T(4,128)S(4)} %get-tuple-element.387.order_ref, s32[4]{0:T(128)S(4)} %get-tuple-element.388.sizes_ref, bf16[48,256,256]{2,1,0:T(8,128)(2,1)} %get-tuple-element.389.tiles_ref, ...), custom_call_target="tpu_custom_call" | custom-call | bytes 1048576 | tf_op jit(solution)/shard_map/while/body/near/pallas_call | solution.py:565
  27.1 0.6 %collective-permute-start.2 = (f32[24,256]{1,0:T(8,128)S(1)}, f32[24,256]{1,0:T(8,128)S(1)}, u32[]{:S(2)}, u32[]{:S(2)}) collective-permute-start(f32[24,256]{1,0:T(8,128)S(1)} %z_level.2.walk_ref), channel_id=1, source_target_pairs={{0,8},{1,9},{2,10},{3,11},{4,12},{5,13},{6,14},{7,15},{8,0},{9,1},... | collective-permute-start | bytes 73736 | tf_op jit(solution)/shard_map/while/body/ppermute | solution.py:445
  27.7 3.4 %collective-permute-done.2.partner_ref = f32[24,256]{1,0:T(8,128)S(1)} collective-permute-done((f32[24,256]{1,0:T(8,128)S(1)}, f32[24,256]{1,0:T(8,128)S(1)}, u32[]{:S(2)}, u32[]{:S(2)}) %collective-permute-start.2) | collective-permute-done | bytes 24608 | tf_op jit(solution)/shard_map/while/body/ppermute | solution.py:445
  31.2 3.1 %far.1 = (f32[512,256]{1,0:T(8,128)S(1)}, f32[528,256]{1,0:T(8,128)S(1)}) custom-call(s32[1]{0:T(128)} %bitcast.2.place_ref, s32[4,52]{1,0:T(4,128)S(4)} %get-tuple-element.363.order_ref, s32[4]{0:T(128)S(4)} %get-tuple-element.364.sizes_ref, bf16[48,256,256]{2,1,0:T(8,128)(2,1)} %get-tuple-element.407, f32[9,128,256]{2,1,0:T(8,128)S(1)} %get-tuple-element.145.near_ref, ...), custom_call_target="tpu_custom_call" | custom-call | bytes 1048576 | tf_op jit(solution)/shard_map/far/pallas_call | solution.py:594
  34.3 0.2 collective-permute-start.8
  34.5 1.8 %collective-permute-done.8.arrived_ref = f32[528,256]{1,0:T(8,128)S(1)} collective-permute-done((f32[528,256]{1,0:T(8,128)S(1)}, f32[528,256]{1,0:T(8,128)S(1)}, u32[]{:S(2)}, u32[]{:S(2)}) %collective-permute-start.8) | collective-permute-done | bytes 540704 | tf_op jit(solution)/shard_map/ppermute | solution.py:445
  36.3 0.1 combine.1
  36.4 2.8 %collective-permute-start.9 = (bf16[288,256]{1,0:T(8,128)(2,1)S(1)}, bf16[288,256]{1,0:T(8,128)(2,1)S(1)}, u32[]{:S(2)}, u32[]{:S(2)}) collective-permute-start(bf16[288,256]{1,0:T(8,128)(2,1)S(1)} %get-tuple-element.158), channel_id=1, source_target_pairs={{0,2},{1,3},{2,0},{3,1},{4,6},{5,7},{6,4},{7,5},{8,10},{9,11},{10,... | collective-permute-start | bytes 442376 | tf_op jit(solution)/shard_map/ppermute | solution.py:445
  39.2 4.1 %collective-permute-done.9.refs_0_ = bf16[288,256]{1,0:T(8,128)(2,1)S(1)} collective-permute-done((bf16[288,256]{1,0:T(8,128)(2,1)S(1)}, bf16[288,256]{1,0:T(8,128)(2,1)S(1)}, u32[]{:S(2)}, u32[]{:S(2)}) %collective-permute-start.9) | collective-permute-done | bytes 147488 | tf_op jit(solution)/shard_map/ppermute | solution.py:445
  43.3 1.3 %back.1 = f32[32,2048]{1,0:T(8,128)} custom-call(s32[1]{0:T(128)} %bitcast.2.place_ref, f32[256,256]{1,0:T(8,128)S(1)} %get-tuple-element.155.own_ref, f32[32,256]{1,0:T(8,128)S(1)} %get-tuple-element.156.both_ref, f32[8,256]{1,0:T(8,128)S(1)} %get-tuple-element.157.firsts_ref, bf16[288,256]{1,0:T(8,128)(2,1)S(1)} %collective-permute-done.9.refs_0_), custom_call_target="tpu_custom_call" | custom-call | bytes 1048576 | tf_op jit(solution)/shard_map/back/pallas_call | solution.py:620
  (10 shorter events, 0.1 us)
Async XLA Ops:
  0.0 2.6 %collective-permute-start.3 = (f32[32,2048]{1,0:T(8,128)}, f32[32,2048]{1,0:T(8,128)S(1)}, u32[]{:S(2)}, u32[]{:S(2)}) collective-permute-start(f32[32,2048]{1,0:T(8,128)} %sources_ref.1), channel_id=1, source_target_pairs={{0,1},{1,0},{2,3},{3,2},{4,5},{5,4},{6,7},{7,6},{8,9},{9,8},{10,11... | collective-permute-start | bytes 786440 | tf_op jit(solution)/shard_map/ppermute | solution.py:445
  4.1 10.1 %collective-permute-start.4 = (bf16[512,256]{1,0:T(8,128)(2,1)S(1)}, bf16[512,256]{1,0:T(8,128)(2,1)}, u32[]{:S(2)}, u32[]{:S(2)}) collective-permute-start(bf16[512,256]{1,0:T(8,128)(2,1)S(1)} %get-tuple-element.141), channel_id=1, source_target_pairs={{0,8},{1,24},{2,0},{3,16},{4,12},{5,28},{6,4},{7,20},{8,9},{9,25},... | collective-permute-start | bytes 786440 | tf_op jit(solution)/shard_map/ppermute | solution.py:445
  6.7 8.7 %collective-permute-start.5 = (bf16[512,256]{1,0:T(8,128)(2,1)S(1)}, bf16[512,256]{1,0:T(8,128)(2,1)}, u32[]{:S(2)}, u32[]{:S(2)}) collective-permute-start(bf16[512,256]{1,0:T(8,128)(2,1)S(1)} %get-tuple-element.141), channel_id=1, source_target_pairs={{0,0},{1,16},{2,8},{3,24},{4,4},{5,20},{6,12},{7,28},{8,1},{9,17},... | collective-permute-start | bytes 786440 | tf_op jit(solution)/shard_map/ppermute | solution.py:445
  10.3 3.9 %collective-permute-start = (f32[24,256]{1,0:T(8,128)S(1)}, f32[24,256]{1,0:T(8,128)S(1)}, u32[]{:S(2)}, u32[]{:S(2)}) collective-permute-start(f32[24,256]{1,0:T(8,128)S(1)} %get-tuple-element.313.refs_0_), channel_id=1, source_target_pairs={{0,4},{1,5},{2,6},{3,7},{4,0},{5,1},{6,2},{7,3},{8,12},{9,13},{10,... | collective-permute-start | bytes 73736 | tf_op jit(solution)/shard_map/while/body/ppermute | solution.py:445
  14.2 17.0 %collective-permute-start.6 = (bf16[512,256]{1,0:T(8,128)(2,1)}, bf16[512,256]{1,0:T(8,128)(2,1)}, u32[]{:S(2)}, u32[]{:S(2)}) collective-permute-start(bf16[512,256]{1,0:T(8,128)(2,1)} %collective-permute-done.4.refs_0_), channel_id=1, source_target_pairs={{0,4},{1,5},{2,6},{3,7},{4,0},{5,1},{6,2},{7,3},{8,12},{9,13},{10,... | collective-permute-start | bytes 786440 | tf_op jit(solution)/shard_map/ppermute | solution.py:445
  15.4 15.8 %collective-permute-start.7 = (bf16[512,256]{1,0:T(8,128)(2,1)}, bf16[512,256]{1,0:T(8,128)(2,1)}, u32[]{:S(2)}, u32[]{:S(2)}) collective-permute-start(bf16[512,256]{1,0:T(8,128)(2,1)} %collective-permute-done.5.refs_1_), channel_id=1, source_target_pairs={{0,4},{1,5},{2,6},{3,7},{4,0},{5,1},{6,2},{7,3},{8,12},{9,13},{10,... | collective-permute-start | bytes 786440 | tf_op jit(solution)/shard_map/ppermute | solution.py:445
  16.3 10.8 %collective-permute-start.1 = (f32[24,256]{1,0:T(8,128)S(1)}, f32[24,256]{1,0:T(8,128)S(1)}, u32[]{:S(2)}, u32[]{:S(2)}) collective-permute-start(f32[24,256]{1,0:T(8,128)S(1)} %get-tuple-element.370.walk_ref), channel_id=1, source_target_pairs={{0,16},{1,17},{2,18},{3,19},{4,20},{5,21},{6,22},{7,23},{8,24},{9,... | collective-permute-start | bytes 73736 | tf_op jit(solution)/shard_map/while/body/ppermute | solution.py:445
  27.1 4.0 %collective-permute-start.2 = (f32[24,256]{1,0:T(8,128)S(1)}, f32[24,256]{1,0:T(8,128)S(1)}, u32[]{:S(2)}, u32[]{:S(2)}) collective-permute-start(f32[24,256]{1,0:T(8,128)S(1)} %z_level.2.walk_ref), channel_id=1, source_target_pairs={{0,8},{1,9},{2,10},{3,11},{4,12},{5,13},{6,14},{7,15},{8,0},{9,1},... | collective-permute-start | bytes 73736 | tf_op jit(solution)/shard_map/while/body/ppermute | solution.py:445
  34.3 2.0 %collective-permute-start.8 = (f32[528,256]{1,0:T(8,128)S(1)}, f32[528,256]{1,0:T(8,128)S(1)}, u32[]{:S(2)}, u32[]{:S(2)}) collective-permute-start(f32[528,256]{1,0:T(8,128)S(1)} %get-tuple-element.154), channel_id=1, source_target_pairs={{0,1},{1,0},{2,3},{3,2},{4,5},{5,4},{6,7},{7,6},{8,9},{9,8},{10,11... | collective-permute-start | bytes 1622024 | tf_op jit(solution)/shard_map/ppermute | solution.py:445
  36.4 7.0 %collective-permute-start.9 = (bf16[288,256]{1,0:T(8,128)(2,1)S(1)}, bf16[288,256]{1,0:T(8,128)(2,1)S(1)}, u32[]{:S(2)}, u32[]{:S(2)}) collective-permute-start(bf16[288,256]{1,0:T(8,128)(2,1)S(1)} %get-tuple-element.158), channel_id=1, source_target_pairs={{0,2},{1,3},{2,0},{3,1},{4,6},{5,7},{6,4},{7,5},{8,10},{9,11},{10,... | collective-permute-start | bytes 442376 | tf_op jit(solution)/shard_map/ppermute | solution.py:445

commit v5 on v4

--- a/solution.py
+++ b/solution.py
@@ -88,13 +88,18 @@
     return (z_of(place_ref) ^ m ^ (spans - 1)) & (spans - 1)
 
 
-def front_kernel(place_ref, sources_ref, other_ref, _, out_ref, first_ref, mine_ref, sem, *, blocks, extent):
+def prepare_kernel(sources_ref, mine_ref, walk_ref, rest_ref, sem):
     copy = pltpu.make_async_copy(sources_ref, mine_ref, sem)
     copy.start()
+    walk_ref[...] = jnp.zeros_like(walk_ref)
+    rest_ref[...] = jnp.zeros_like(rest_ref)
+    copy.wait()
+
+
+def front_kernel(place_ref, mine_ref, other_ref, out_ref, first_ref, *, blocks, extent):
     height = mine_ref.shape[0]
     pair = 2 * height
     signs, scale = haar_parts(extent, False)
-    copy.wait()
     mine, other = mine_ref[...], other_ref[...]
     first_core = core_of(place_ref) == 0
     both = jnp.concatenate([jnp.where(first_core, mine, other), jnp.where(first_core, other, mine)], axis=0)
@@ -116,11 +121,7 @@
     first_ref[:, 0:pair] = first[0:8, :] * (1.0 / math.sqrt(blocks * extent))
 
 
-def list_kernel(
-    place_ref, rows_ref, cols_ref, count_ref, order_ref, sizes_ref, walk_ref, rest_ref, *, blocks, owners
-):
-    walk_ref[...] = jnp.zeros_like(walk_ref)
-    rest_ref[...] = jnp.zeros_like(rest_ref)
+def list_kernel(place_ref, rows_ref, cols_ref, count_ref, order_ref, sizes_ref, *, blocks, owners):
     x = x_of(place_ref)
 
     def visit(slot, sizes):
@@ -315,7 +316,12 @@
     place_ref, order_ref, sizes_ref, tiles_ref, near_ref, ahead_ref, row_ref, cols_ref, *refs, blocks, owners, spans
 ):
     messages = refs[: owners * spans]
-    keep_ref, send_ref, sides, acc, held, sems = refs[owners * spans :]
+    keep_ref, send_ref, sides, acc, held, sems, near_sides, near_sems = refs[owners * spans :]
+    copies = [
+        pltpu.make_async_copy(messages[m], near_sides.at[m], near_sems.at[m]) for m in range(spans)
+    ]
+    for copy in copies:
+        copy.start()
     groups = groups_of(sizes_ref, 1)
     ahead = jnp.minimum(groups, AHEAD // UNROLL)
 
@@ -343,6 +349,9 @@
     lax.fori_loop(0, ahead, ready, 0)
     lax.fori_loop(ahead, groups, group, 0)
 
+    for copy in copies:
+        copy.wait()
+    messages = (*(near_sides.at[m] for m in range(spans)), *messages[spans:])
     lane = lax.broadcasted_iota(jnp.int32, (pair, extent), 1)
     for m in range(spans):
         rows = pl.ds(pl.multiple_of(source_span(place_ref, m, spans) * pair, pair), pair)
@@ -493,30 +502,32 @@
     from_core = other_core(sources)
     gathered = -(-n_row // 8) * 8
     every = (spans * pair, extent)
-    order, sizes, blank_walk, blank_rest = call(
-        list_kernel,
-        "lists",
-        [
-            pltpu.SMEM((4, slots + UNROLL), jnp.int32),
-            pltpu.SMEM((4,), jnp.int32),
-            kept(length + gathered, extent),
-            kept(owners * length, extent),
-        ],
-        [smem] * 4,
-        [smem] * 2 + [vmem] * 2,
-        blocks=blocks,
-        owners=owners,
-    )(place, in_hbm(tile_row.reshape(-1)), in_hbm(tile_col.reshape(-1)), tile_count.reshape(1))
+    mine, blank_walk, blank_rest = call(
+        prepare_kernel,
+        "prepare",
+        [kept(*sources.shape), kept(length + gathered, extent), kept(owners * length, extent)],
+        [hbm],
+        [vmem] * 3,
+        scratch=[pltpu.SemaphoreType.DMA],
+    )(in_hbm(sources))
     message, first = call(
         front_kernel,
         "front",
         [bf16(blocks * pair, extent), f32(8, extent)],
-        [smem, hbm, vmem, unread],
+        [smem, vmem, vmem],
         [vmem] * 2,
-        scratch=[pltpu.VMEM(sources.shape, jnp.float32), pltpu.SemaphoreType.DMA],
         blocks=blocks,
         extent=extent,
-    )(place, in_hbm(sources), from_core, blank_rest)
+    )(place, mine, from_core)
+    order, sizes = call(
+        list_kernel,
+        "lists",
+        [pltpu.SMEM((4, slots + UNROLL), jnp.int32), pltpu.SMEM((4,), jnp.int32)],
+        [smem] * 4,
+        [smem] * 2,
+        blocks=blocks,
+        owners=owners,
+    )(place, in_hbm(tile_row.reshape(-1)), in_hbm(tile_col.reshape(-1)), tile_count.reshape(1))
 
     direct = [
         moved(message, lambda zz, xx, yy, cc, m=m: (cc * spans + (yy ^ m ^ (spans - 1)), xx, zz // 2, zz % 2))
@@ -595,12 +606,14 @@
         far_kernel,
         "far",
         [f32(spans * part, extent), f32(spans * part + length, extent)],
-        [smem] * 3 + [hbm] + [vmem] * (4 + len(direct) + len(swapped)),
+        [smem] * 3 + [hbm] + [vmem] * 4 + [unread] * len(direct) + [vmem] * len(swapped),
         [vmem] * 2,
         scratch=[
             pltpu.VMEM(((owners - 1) * blocks, *every), jnp.bfloat16),
             pltpu.VMEM((blocks + 1, *every), jnp.float32),
             *held_tiles,
+            pltpu.VMEM((spans, blocks * pair, extent), jnp.bfloat16),
+            pltpu.SemaphoreType.DMA((spans,)),
         ],
         blocks=blocks,
         owners=owners,

time: 44.5 us -> 43.8 us (0.984)
  starting transfers between devices: 18.1 us -> 17 us
    ppermute x10, starting transfers between devices: 18.1 us -> 17 us  [moved(): return lax.ppermute(value, ('row', 'col'), pairs)]
    pallas_call x0 -> x1, Pallas kernels: none -> 0.96 us  [local(): call(prepare_kernel, 'prepare', [kept(*sources.shape), kept(length + gath...]
    pallas_call x1, Pallas kernels: 1.45 us -> 0.52 us  [local(): call(front_kernel, 'front', [bf16(blocks * pair, extent), f32(8, extent)]...]
  transfers between devices with their start and end apart: 10 -> 10, of which waited for: 4 -> 6; matrix products, arithmetic and copies ran while one was open for 0% -> 0% of each run, Pallas kernels for 17% -> 20%
where the time goes in v5:
time: 43.8 us; the launch traced here: 44.1 us
  starting transfers between devices  17 us (39%)
  Pallas kernels  14 us (32%)
  waiting for transfers between devices  12.3 us (28%)
  between operations  0.78 us (2%)
    ppermute x10, starting transfers between devices, moved(): return lax.ppermute(value, ('row', 'col'), pairs)  17 us
    ppermute x10, waiting for transfers between devices, moved(): return lax.ppermute(value, ('row', 'col'), pairs)  12.3 us
    pallas_call x1, Pallas kernels, late(): call(near_kernel, 'near', later, [smem] * 4 + [hbm] + [vmem] * len(direct...  3.94 us
    pallas_call x1, Pallas kernels, local(): call(far_kernel, 'far', [f32(spans * part, extent), f32(spans * part + le...  3.25 us
    pallas_call x1, Pallas kernels, early(): call(edge_kernel, 'edges', [f32(length, extent), f32(length + gathered, e...  2.39 us
    pallas_call x1, Pallas kernels, local(): call(list_kernel, 'lists', [pltpu.SMEM((4, slots + UNROLL), jnp.int32), p...  1.54 us
    pallas_call x1, Pallas kernels, local(): call(back_kernel, 'back', f32(*sources.shape), [smem] + [vmem] * (2 + spa...  1.27 us
    pallas_call x1, Pallas kernels, local(): call(prepare_kernel, 'prepare', [kept(*sources.shape), kept(length + gath...  0.96 us
  transfers between devices with their start and end apart: 10, of which 6 were waited for; matrix products, arithmetic and copies ran while one was open for 0% of the time, Pallas kernels for 20%

profile of v5, /device:TPU:0, one launch (start us, length us, event | category | flops | bytes accessed | tf_op | source)
XLA Modules:
  0.0 44.1 jit_solution(5893075895857665881)
XLA Ops:
  0.0 0.5 %collective-permute-start.3 = (f32[32,2048]{1,0:T(8,128)}, f32[32,2048]{1,0:T(8,128)S(1)}, u32[]{:S(2)}, u32[]{:S(2)}) collective-permute-start(f32[32,2048]{1,0:T(8,128)} %sources_ref.1), channel_id=1, source_target_pairs={{0,1},{1,0},{2,3},{3,2},{4,5},{5,4},{6,7},{7,6},{8,9},{9,8},{10,11... | collective-permute-start | bytes 786440 | tf_op jit(solution)/shard_map/ppermute | solution.py:454
  0.5 1.0 %prepare.1 = (f32[32,2048]{1,0:T(8,128)S(1)}, f32[24,256]{1,0:T(8,128)S(1)}, f32[32,256]{1,0:T(8,128)S(1)}) custom-call(f32[32,2048]{1,0:T(8,128)} %sources_ref.1), custom_call_target="tpu_custom_call" | custom-call | bytes 1048576 | tf_op jit(solution)/shard_map/prepare/pallas_call | solution.py:505
  1.5 0.4 collective-permute-done.3.other_ref
  1.8 0.5 %front.1 = (bf16[512,256]{1,0:T(8,128)(2,1)S(1)}, f32[8,256]{1,0:T(8,128)S(1)}) custom-call(s32[1]{0:T(128)} %bitcast.2.place_ref, f32[32,2048]{1,0:T(8,128)S(1)} %get-tuple-element.140.mine_ref, f32[32,2048]{1,0:T(8,128)S(1)} %collective-permute-done.3.other_ref), custom_call_target="tpu_custom_call" | custom-call | bytes 1048576 | tf_op jit(solution)/shard_map/front/pallas_call | solution.py:513
  2.4 3.0 %collective-permute-start.4 = (bf16[512,256]{1,0:T(8,128)(2,1)S(1)}, bf16[512,256]{1,0:T(8,128)(2,1)}, u32[]{:S(2)}, u32[]{:S(2)}) collective-permute-start(bf16[512,256]{1,0:T(8,128)(2,1)S(1)} %get-tuple-element.143), channel_id=1, source_target_pairs={{0,8},{1,24},{2,0},{3,16},{4,12},{5,28},{6,4},{7,20},{8,9},{9,25},... | collective-permute-start | bytes 786440 | tf_op jit(solution)/shard_map/ppermute | solution.py:454
  5.4 1.3 %collective-permute-start.5 = (bf16[512,256]{1,0:T(8,128)(2,1)S(1)}, bf16[512,256]{1,0:T(8,128)(2,1)}, u32[]{:S(2)}, u32[]{:S(2)}) collective-permute-start(bf16[512,256]{1,0:T(8,128)(2,1)S(1)} %get-tuple-element.143), channel_id=1, source_target_pairs={{0,0},{1,16},{2,8},{3,24},{4,4},{5,20},{6,12},{7,28},{8,1},{9,17},... | collective-permute-start | bytes 786440 | tf_op jit(solution)/shard_map/ppermute | solution.py:454
  7.3 1.5 %lists.1 = (s32[4,52]{1,0:T(4,128)S(4)}, s32[4]{0:T(128)S(4)}) custom-call(s32[1]{0:T(128)} %bitcast.2.place_ref, s32[48]{0:T(128)} %bitcast.14, s32[48]{0:T(128)} %bitcast.15, s32[1]{0:T(128)} %bitcast.12.count_ref), custom_call_target="tpu_custom_call" | custom-call | bytes 1048576 | tf_op jit(solution)/shard_map/lists/pallas_call | solution.py:522
  8.9 6.3 %while.26 = (s32[]{:T(128)}, f32[24,256]{1,0:T(8,128)S(1)}, f32[32,256]{1,0:T(8,128)S(1)}, s32[]{:T(128)}, s32[1]{0:T(128)}, /*index=5*/s32[4,52]{1,0:T(4,128)S(...) while((s32[]{:T(128)}, f32[24,256]{1,0:T(8,128)S(1)}, ...), condition=%wide.region_1.2_spmd, body=%wide.region_0.1_spmd.sunk | while | flops 2 | bytes 2195597 | solution.py:498
  8.9 2.4 %edges.1 = (f32[16,256]{1,0:T(8,128)S(1)}, f32[24,256]{1,0:T(8,128)S(1)}) custom-call(s32[1]{0:T(128)} %get-tuple-element.353.place_ref, s32[1]{0:T(128)} %bitcast.10._, s32[4,52]{1,0:T(4,128)S(4)} %get-tuple-element.354.order_ref, s32[4]{0:T(128)S(4)} %get-tuple-element.355.sizes_ref, bf16[48,256,256]{2,1,0:T(8,128)(2,1)} %get-tuple-element.356.tiles_ref, ...), custom_call_target="tpu_custom_call" | custom-call | bytes 1048576 | tf_op jit(solution)/shard_map/while/body/edges/pallas_call | solution.py:538
  11.3 0.6 %collective-permute-start = (f32[24,256]{1,0:T(8,128)S(1)}, f32[24,256]{1,0:T(8,128)S(1)}, u32[]{:S(2)}, u32[]{:S(2)}) collective-permute-start(f32[24,256]{1,0:T(8,128)S(1)} %get-tuple-element.315.refs_0_), channel_id=1, source_target_pairs={{0,4},{1,5},{2,6},{3,7},{4,0},{5,1},{6,2},{7,3},{8,12},{9,13},{10,... | collective-permute-start | bytes 73736 | tf_op jit(solution)/shard_map/while/body/ppermute | solution.py:454
  12.0 3.2 %collective-permute-done.refs_1_ = f32[24,256]{1,0:T(8,128)S(1)} collective-permute-done((f32[24,256]{1,0:T(8,128)S(1)}, f32[24,256]{1,0:T(8,128)S(1)}, u32[]{:S(2)}, u32[]{:S(2)}) %collective-permute-start) | collective-permute-done | bytes 24608 | tf_op jit(solution)/shard_map/while/body/ppermute | solution.py:454
  15.2 0.6 %collective-permute-start.6 = (bf16[512,256]{1,0:T(8,128)(2,1)}, bf16[512,256]{1,0:T(8,128)(2,1)}, u32[]{:S(2)}, u32[]{:S(2)}) collective-permute-start(bf16[512,256]{1,0:T(8,128)(2,1)} %collective-permute-done.4.refs_0_), channel_id=1, source_target_pairs={{0,4},{1,5},{2,6},{3,7},{4,0},{5,1},{6,2},{7,3},{8,12},{9,13},{10,... | collective-permute-start | bytes 786440 | tf_op jit(solution)/shard_map/ppermute | solution.py:454
  15.9 1.4 %collective-permute-start.7 = (bf16[512,256]{1,0:T(8,128)(2,1)}, bf16[512,256]{1,0:T(8,128)(2,1)}, u32[]{:S(2)}, u32[]{:S(2)}) collective-permute-start(bf16[512,256]{1,0:T(8,128)(2,1)} %collective-permute-done.5.refs_1_), channel_id=1, source_target_pairs={{0,4},{1,5},{2,6},{3,7},{4,0},{5,1},{6,2},{7,3},{8,12},{9,13},{10,... | collective-permute-start | bytes 786440 | tf_op jit(solution)/shard_map/ppermute | solution.py:454
  17.4 12.3 %while.27 = (s32[]{:T(128)}, f32[24,256]{1,0:T(8,128)S(1)}, f32[9,128,256]{2,1,0:T(8,128)S(1)}, bf16[16,256,256]{2,1,0:T(8,128)(2,1)S(1)}, s32[]{:T(128)}, /*ind...) while((s32[]{:T(128)}, f32[24,256]{1,0:T(8,128)S(1)}, ...), condition=%wide.region_3.4_spmd, body=%wide.region_2.3_spmd.sunk | while | flops 2 | bytes 3342533 | solution.py:498
  17.4 4.4 %collective-permute-start.1 = (f32[24,256]{1,0:T(8,128)S(1)}, f32[24,256]{1,0:T(8,128)S(1)}, u32[]{:S(2)}, u32[]{:S(2)}) collective-permute-start(f32[24,256]{1,0:T(8,128)S(1)} %get-tuple-element.372.walk_ref), channel_id=1, source_target_pairs={{0,16},{1,17},{2,18},{3,19},{4,20},{5,21},{6,22},{7,23},{8,24},{9,... | collective-permute-start | bytes 73736 | tf_op jit(solution)/shard_map/while/body/ppermute | solution.py:454
  21.7 3.9 %near.1 = (f32[9,128,256]{2,1,0:T(8,128)S(1)}, bf16[16,256,256]{2,1,0:T(8,128)(2,1)S(1)}) custom-call(s32[1]{0:T(128)} %get-tuple-element.388.place_ref, s32[1]{0:T(128)} %bitcast.11._, s32[4,52]{1,0:T(4,128)S(4)} %get-tuple-element.389.order_ref, s32[4]{0:T(128)S(4)} %get-tuple-element.390.sizes_ref, bf16[48,256,256]{2,1,0:T(8,128)(2,1)} %get-tuple-element.391.tiles_ref, ...), custom_call_target="tpu_custom_call" | custom-call | bytes 1048576 | tf_op jit(solution)/shard_map/while/body/near/pallas_call | solution.py:576
  25.7 1.8 %collective-permute-start.2 = (f32[24,256]{1,0:T(8,128)S(1)}, f32[24,256]{1,0:T(8,128)S(1)}, u32[]{:S(2)}, u32[]{:S(2)}) collective-permute-start(f32[24,256]{1,0:T(8,128)S(1)} %z_level.2.walk_ref), channel_id=1, source_target_pairs={{0,8},{1,9},{2,10},{3,11},{4,12},{5,13},{6,14},{7,15},{8,0},{9,1},... | collective-permute-start | bytes 73736 | tf_op jit(solution)/shard_map/while/body/ppermute | solution.py:454
  27.5 2.1 %collective-permute-done.2.partner_ref = f32[24,256]{1,0:T(8,128)S(1)} collective-permute-done((f32[24,256]{1,0:T(8,128)S(1)}, f32[24,256]{1,0:T(8,128)S(1)}, u32[]{:S(2)}, u32[]{:S(2)}) %collective-permute-start.2) | collective-permute-done | bytes 24608 | tf_op jit(solution)/shard_map/while/body/ppermute | solution.py:454
  29.6 0.5 %collective-permute-done.7.refs_3_ = bf16[512,256]{1,0:T(8,128)(2,1)} collective-permute-done((bf16[512,256]{1,0:T(8,128)(2,1)}, bf16[512,256]{1,0:T(8,128)(2,1)}, u32[]{:S(2)}, u32[]{:S(2)}) %collective-permute-start.7) | collective-permute-done | bytes 262176 | tf_op jit(solution)/shard_map/ppermute | solution.py:454
  30.1 3.2 %far.1 = (f32[512,256]{1,0:T(8,128)S(1)}, f32[528,256]{1,0:T(8,128)S(1)}) custom-call(s32[1]{0:T(128)} %bitcast.2.place_ref, s32[4,52]{1,0:T(4,128)S(4)} %get-tuple-element.365.order_ref, s32[4]{0:T(128)S(4)} %get-tuple-element.366.sizes_ref, bf16[48,256,256]{2,1,0:T(8,128)(2,1)} %get-tuple-element.409, f32[9,128,256]{2,1,0:T(8,128)S(1)} %get-tuple-element.147.near_ref, ...), custom_call_target="tpu_custom_call" | custom-call | bytes 1048576 | tf_op jit(solution)/shard_map/far/pallas_call | solution.py:605
  33.5 1.9 %collective-permute-done.8.arrived_ref = f32[528,256]{1,0:T(8,128)S(1)} collective-permute-done((f32[528,256]{1,0:T(8,128)S(1)}, f32[528,256]{1,0:T(8,128)S(1)}, u32[]{:S(2)}, u32[]{:S(2)}) %collective-permute-start.8) | collective-permute-done | bytes 540704 | tf_op jit(solution)/shard_map/ppermute | solution.py:454
  35.4 3.2 %collective-permute-start.9 = (bf16[288,256]{1,0:T(8,128)(2,1)S(1)}, bf16[288,256]{1,0:T(8,128)(2,1)S(1)}, u32[]{:S(2)}, u32[]{:S(2)}) collective-permute-start(bf16[288,256]{1,0:T(8,128)(2,1)S(1)} %get-tuple-element.160), channel_id=1, source_target_pairs={{0,2},{1,3},{2,0},{3,1},{4,6},{5,7},{6,4},{7,5},{8,10},{9,11},{10,... | collective-permute-start | bytes 442376 | tf_op jit(solution)/shard_map/ppermute | solution.py:454
  38.7 4.1 %collective-permute-done.9.refs_0_ = bf16[288,256]{1,0:T(8,128)(2,1)S(1)} collective-permute-done((bf16[288,256]{1,0:T(8,128)(2,1)S(1)}, bf16[288,256]{1,0:T(8,128)(2,1)S(1)}, u32[]{:S(2)}, u32[]{:S(2)}) %collective-permute-start.9) | collective-permute-done | bytes 147488 | tf_op jit(solution)/shard_map/ppermute | solution.py:454
  42.8 1.3 %back.1 = f32[32,2048]{1,0:T(8,128)} custom-call(s32[1]{0:T(128)} %bitcast.2.place_ref, f32[256,256]{1,0:T(8,128)S(1)} %get-tuple-element.157.own_ref, f32[32,256]{1,0:T(8,128)S(1)} %get-tuple-element.158.both_ref, f32[8,256]{1,0:T(8,128)S(1)} %get-tuple-element.159.firsts_ref, bf16[288,256]{1,0:T(8,128)(2,1)S(1)} %collective-permute-done.9.refs_0_), custom_call_target="tpu_custom_call" | custom-call | bytes 1048576 | tf_op jit(solution)/shard_map/back/pallas_call | solution.py:633
  (11 shorter events, 0.2 us)
Async XLA Ops:
  0.0 1.8 %collective-permute-start.3 = (f32[32,2048]{1,0:T(8,128)}, f32[32,2048]{1,0:T(8,128)S(1)}, u32[]{:S(2)}, u32[]{:S(2)}) collective-permute-start(f32[32,2048]{1,0:T(8,128)} %sources_ref.1), channel_id=1, source_target_pairs={{0,1},{1,0},{2,3},{3,2},{4,5},{5,4},{6,7},{7,6},{8,9},{9,8},{10,11... | collective-permute-start | bytes 786440 | tf_op jit(solution)/shard_map/ppermute | solution.py:454
  2.4 12.9 %collective-permute-start.4 = (bf16[512,256]{1,0:T(8,128)(2,1)S(1)}, bf16[512,256]{1,0:T(8,128)(2,1)}, u32[]{:S(2)}, u32[]{:S(2)}) collective-permute-start(bf16[512,256]{1,0:T(8,128)(2,1)S(1)} %get-tuple-element.143), channel_id=1, source_target_pairs={{0,8},{1,24},{2,0},{3,16},{4,12},{5,28},{6,4},{7,20},{8,9},{9,25},... | collective-permute-start | bytes 786440 | tf_op jit(solution)/shard_map/ppermute | solution.py:454
  5.4 10.5 %collective-permute-start.5 = (bf16[512,256]{1,0:T(8,128)(2,1)S(1)}, bf16[512,256]{1,0:T(8,128)(2,1)}, u32[]{:S(2)}, u32[]{:S(2)}) collective-permute-start(bf16[512,256]{1,0:T(8,128)(2,1)S(1)} %get-tuple-element.143), channel_id=1, source_target_pairs={{0,0},{1,16},{2,8},{3,24},{4,4},{5,20},{6,12},{7,28},{8,1},{9,17},... | collective-permute-start | bytes 786440 | tf_op jit(solution)/shard_map/ppermute | solution.py:454
  11.3 3.9 %collective-permute-start = (f32[24,256]{1,0:T(8,128)S(1)}, f32[24,256]{1,0:T(8,128)S(1)}, u32[]{:S(2)}, u32[]{:S(2)}) collective-permute-start(f32[24,256]{1,0:T(8,128)S(1)} %get-tuple-element.315.refs_0_), channel_id=1, source_target_pairs={{0,4},{1,5},{2,6},{3,7},{4,0},{5,1},{6,2},{7,3},{8,12},{9,13},{10,... | collective-permute-start | bytes 73736 | tf_op jit(solution)/shard_map/while/body/ppermute | solution.py:454
  15.2 14.4 %collective-permute-start.6 = (bf16[512,256]{1,0:T(8,128)(2,1)}, bf16[512,256]{1,0:T(8,128)(2,1)}, u32[]{:S(2)}, u32[]{:S(2)}) collective-permute-start(bf16[512,256]{1,0:T(8,128)(2,1)} %collective-permute-done.4.refs_0_), channel_id=1, source_target_pairs={{0,4},{1,5},{2,6},{3,7},{4,0},{5,1},{6,2},{7,3},{8,12},{9,13},{10,... | collective-permute-start | bytes 786440 | tf_op jit(solution)/shard_map/ppermute | solution.py:454
  15.9 14.2 %collective-permute-start.7 = (bf16[512,256]{1,0:T(8,128)(2,1)}, bf16[512,256]{1,0:T(8,128)(2,1)}, u32[]{:S(2)}, u32[]{:S(2)}) collective-permute-start(bf16[512,256]{1,0:T(8,128)(2,1)} %collective-permute-done.5.refs_1_), channel_id=1, source_target_pairs={{0,4},{1,5},{2,6},{3,7},{4,0},{5,1},{6,2},{7,3},{8,12},{9,13},{10,... | collective-permute-start | bytes 786440 | tf_op jit(solution)/shard_map/ppermute | solution.py:454
  17.4 8.3 %collective-permute-start.1 = (f32[24,256]{1,0:T(8,128)S(1)}, f32[24,256]{1,0:T(8,128)S(1)}, u32[]{:S(2)}, u32[]{:S(2)}) collective-permute-start(f32[24,256]{1,0:T(8,128)S(1)} %get-tuple-element.372.walk_ref), channel_id=1, source_target_pairs={{0,16},{1,17},{2,18},{3,19},{4,20},{5,21},{6,22},{7,23},{8,24},{9,... | collective-permute-start | bytes 73736 | tf_op jit(solution)/shard_map/while/body/ppermute | solution.py:454
  25.7 3.9 %collective-permute-start.2 = (f32[24,256]{1,0:T(8,128)S(1)}, f32[24,256]{1,0:T(8,128)S(1)}, u32[]{:S(2)}, u32[]{:S(2)}) collective-permute-start(f32[24,256]{1,0:T(8,128)S(1)} %z_level.2.walk_ref), channel_id=1, source_target_pairs={{0,8},{1,9},{2,10},{3,11},{4,12},{5,13},{6,14},{7,15},{8,0},{9,1},... | collective-permute-start | bytes 73736 | tf_op jit(solution)/shard_map/while/body/ppermute | solution.py:454
  33.4 2.0 %collective-permute-start.8 = (f32[528,256]{1,0:T(8,128)S(1)}, f32[528,256]{1,0:T(8,128)S(1)}, u32[]{:S(2)}, u32[]{:S(2)}) collective-permute-start(f32[528,256]{1,0:T(8,128)S(1)} %get-tuple-element.156), channel_id=1, source_target_pairs={{0,1},{1,0},{2,3},{3,2},{4,5},{5,4},{6,7},{7,6},{8,9},{9,8},{10,11... | collective-permute-start | bytes 1622024 | tf_op jit(solution)/shard_map/ppermute | solution.py:454
  35.4 7.3 %collective-permute-start.9 = (bf16[288,256]{1,0:T(8,128)(2,1)S(1)}, bf16[288,256]{1,0:T(8,128)(2,1)S(1)}, u32[]{:S(2)}, u32[]{:S(2)}) collective-permute-start(bf16[288,256]{1,0:T(8,128)(2,1)S(1)} %get-tuple-element.160), channel_id=1, source_target_pairs={{0,2},{1,3},{2,0},{3,1},{4,6},{5,7},{6,4},{7,5},{8,10},{9,11},{10,... | collective-permute-start | bytes 442376 | tf_op jit(solution)/shard_map/ppermute | solution.py:454

commit v6 on v5

--- a/solution.py
+++ b/solution.py
@@ -313,10 +313,10 @@
 
 
 def far_kernel(
-    place_ref, order_ref, sizes_ref, tiles_ref, near_ref, ahead_ref, row_ref, cols_ref, *refs, blocks, owners, spans
+    place_ref, order_ref, sizes_ref, tiles_ref, _, ahead_ref, row_ref, cols_ref, *refs, blocks, owners, spans
 ):
     messages = refs[: owners * spans]
-    keep_ref, send_ref, sides, acc, held, sems, near_sides, near_sems = refs[owners * spans :]
+    keep_ref, send_ref, acc, sides, held, sems, near_sides, near_sems = refs[owners * spans :]
     copies = [
         pltpu.make_async_copy(messages[m], near_sides.at[m], near_sems.at[m]) for m in range(spans)
     ]
@@ -334,7 +334,6 @@
     height = pair // 2
     x = x_of(place_ref)
     fill_sides(sides, messages[spans:], place_ref, blocks, spans)
-    acc[...] = near_ref[...]
 
     def ready(index, _):
         add_group(order_ref, 1, index, ahead_ref, sides, acc)
@@ -372,8 +371,8 @@
             two = value[y * pair + height : (y + 1) * pair, :]
             at = (y * blocks + i) * height
             keep_ref[at : at + height, :] = jnp.where(first_core, one, two)
-            send_ref[at : at + height, :] = jnp.where(first_core, two, one)
-    send_ref[spans * blocks * height :, :] = cols_ref[...]
+            send_ref[at : at + height, :] = jnp.where(first_core, two, one).astype(jnp.bfloat16)
+    send_ref[spans * blocks * height :, :] = cols_ref[...].astype(jnp.bfloat16)
 
 
 def combine_kernel(place_ref, keep_ref, arrived_ref, cols_ref, own_ref, both_ref, *out_refs):
@@ -382,15 +381,15 @@
     rows = own_ref.shape[0]
     length = cols_ref.shape[0]
     first_core = core_of(place_ref) == 0
-    mine, other = cols_ref[...], arrived_ref[spans * rows :, :]
+    mine, other = cols_ref[...], arrived_ref[spans * rows :, :].astype(jnp.float32)
     both_ref[0:length, :] = jnp.where(first_core, mine, other)
     both_ref[length:, :] = jnp.where(first_core, other, mine)
     at = pl.ds(pl.multiple_of(span * rows, rows), rows)
-    own_ref[...] = keep_ref[at, :] + arrived_ref[at, :]
+    own_ref[...] = keep_ref[at, :] + arrived_ref[at, :].astype(jnp.float32)
     both = both_ref[...].astype(jnp.bfloat16)
     for j, out_ref in enumerate(out_refs, 1):
         at = pl.ds(pl.multiple_of(lax.rem(span + j, spans) * rows, rows), rows)
-        out_ref[0:rows, :] = (keep_ref[at, :] + arrived_ref[at, :]).astype(jnp.bfloat16)
+        out_ref[0:rows, :] = (keep_ref[at, :] + arrived_ref[at, :].astype(jnp.float32)).astype(jnp.bfloat16)
         out_ref[rows:, :] = both
 
 
@@ -602,15 +601,15 @@
     )(place, walk, rest)
 
     part = blocks * height
-    keep, send = call(
+    keep, send, _ = call(
         far_kernel,
         "far",
-        [f32(spans * part, extent), f32(spans * part + length, extent)],
+        [f32(spans * part, extent), bf16(spans * part + length, extent), kept(*sum_shape)],
         [smem] * 3 + [hbm] + [vmem] * 4 + [unread] * len(direct) + [vmem] * len(swapped),
-        [vmem] * 2,
+        [vmem] * 3,
+        aliases={4: 2},
         scratch=[
             pltpu.VMEM(((owners - 1) * blocks, *every), jnp.bfloat16),
-            pltpu.VMEM((blocks + 1, *every), jnp.float32),
             *held_tiles,
             pltpu.VMEM((spans, blocks * pair, extent), jnp.bfloat16),
             pltpu.SemaphoreType.DMA((spans,)),

time: 43.8 us -> 43.1 us (0.984); the launches traced: 44.1 us -> 42.6 us
  starting transfers between devices: 17 us -> 20.1 us
  waiting for transfers between devices: 12.3 us -> 9.89 us
  Pallas kernels: 14 us -> 11.7 us
    ppermute x10, starting transfers between devices: 17 us -> 20.1 us  [moved(): return lax.ppermute(value, ('row', 'col'), pairs)]
    ppermute x10, waiting for transfers between devices: 12.3 us -> 9.89 us  [moved(): return lax.ppermute(value, ('row', 'col'), pairs)]
    pallas_call x1, Pallas kernels: 3.94 us -> 3.07 us  [late(): call(near_kernel, 'near', later, [smem] * 4 + [hbm] + [vmem] * len(direct...]
    pallas_call x1, Pallas kernels: 1.54 us -> 0.95 us  [local(): call(list_kernel, 'lists', [pltpu.SMEM((4, slots + UNROLL), jnp.int32), p...]
  transfers between devices with their start and end apart: 10 -> 10, of which waited for: 6 -> 5; matrix products, arithmetic and copies ran while one was open for 0% -> 0% of each run, Pallas kernels for 20% -> 16%
where the time goes in v6:
time: 43.1 us; the launch traced here: 42.6 us
  starting transfers between devices  20.1 us (47%)
  Pallas kernels  11.7 us (27%)
  waiting for transfers between devices  9.89 us (23%)
  between operations  0.78 us (2%)
    ppermute x10, starting transfers between devices, moved(): return lax.ppermute(value, ('row', 'col'), pairs)  20.1 us
    ppermute x10, waiting for transfers between devices, moved(): return lax.ppermute(value, ('row', 'col'), pairs)  9.89 us
    pallas_call x1, Pallas kernels, late(): call(near_kernel, 'near', later, [smem] * 4 + [hbm] + [vmem] * len(direct...  3.07 us
    pallas_call x1, Pallas kernels, local(): call(far_kernel, 'far', [f32(spans * part, extent), bf16(spans * part + l...  2.85 us
    pallas_call x1, Pallas kernels, early(): call(edge_kernel, 'edges', [f32(length, extent), f32(length + gathered, e...  1.96 us
    pallas_call x1, Pallas kernels, local(): call(back_kernel, 'back', f32(*sources.shape), [smem] + [vmem] * (2 + spa...  1.28 us
    pallas_call x1, Pallas kernels, local(): call(prepare_kernel, 'prepare', [kept(*sources.shape), kept(length + gath...  0.96 us
    pallas_call x1, Pallas kernels, local(): call(list_kernel, 'lists', [pltpu.SMEM((4, slots + UNROLL), jnp.int32), p...  0.95 us
  transfers between devices with their start and end apart: 10, of which 5 were waited for; matrix products, arithmetic and copies ran while one was open for 0% of the time, Pallas kernels for 16%

profile of v6, /device:TPU:0, one launch (start us, length us, event | category | flops | bytes accessed | tf_op | source)
XLA Modules:
  0.0 42.6 jit_solution(14062541419110476795)
XLA Ops:
  0.0 0.5 %collective-permute-start.3 = (f32[32,2048]{1,0:T(8,128)}, f32[32,2048]{1,0:T(8,128)S(1)}, u32[]{:S(2)}, u32[]{:S(2)}) collective-permute-start(f32[32,2048]{1,0:T(8,128)} %sources_ref.1), channel_id=1, source_target_pairs={{0,1},{1,0},{2,3},{3,2},{4,5},{5,4},{6,7},{7,6},{8,9},{9,8},{10,11... | collective-permute-start | bytes 786440 | tf_op jit(solution)/shard_map/ppermute | solution.py:453
  0.5 1.0 %prepare.1 = (f32[32,2048]{1,0:T(8,128)S(1)}, f32[24,256]{1,0:T(8,128)S(1)}, f32[32,256]{1,0:T(8,128)S(1)}) custom-call(f32[32,2048]{1,0:T(8,128)} %sources_ref.1), custom_call_target="tpu_custom_call" | custom-call | bytes 1048576 | tf_op jit(solution)/shard_map/prepare/pallas_call | solution.py:504
  1.5 0.4 collective-permute-done.3.other_ref
  1.8 0.5 %front.1 = (bf16[512,256]{1,0:T(8,128)(2,1)S(1)}, f32[8,256]{1,0:T(8,128)S(1)}) custom-call(s32[1]{0:T(128)} %bitcast.2.place_ref, f32[32,2048]{1,0:T(8,128)S(1)} %get-tuple-element.140.mine_ref, f32[32,2048]{1,0:T(8,128)S(1)} %collective-permute-done.3.other_ref), custom_call_target="tpu_custom_call" | custom-call | bytes 1048576 | tf_op jit(solution)/shard_map/front/pallas_call | solution.py:512
  2.4 3.0 %collective-permute-start.4 = (bf16[512,256]{1,0:T(8,128)(2,1)S(1)}, bf16[512,256]{1,0:T(8,128)(2,1)}, u32[]{:S(2)}, u32[]{:S(2)}) collective-permute-start(bf16[512,256]{1,0:T(8,128)(2,1)S(1)} %get-tuple-element.143), channel_id=1, source_target_pairs={{0,8},{1,24},{2,0},{3,16},{4,12},{5,28},{6,4},{7,20},{8,9},{9,25},... | collective-permute-start | bytes 786440 | tf_op jit(solution)/shard_map/ppermute | solution.py:453
  5.4 1.3 %collective-permute-start.5 = (bf16[512,256]{1,0:T(8,128)(2,1)S(1)}, bf16[512,256]{1,0:T(8,128)(2,1)}, u32[]{:S(2)}, u32[]{:S(2)}) collective-permute-start(bf16[512,256]{1,0:T(8,128)(2,1)S(1)} %get-tuple-element.143), channel_id=1, source_target_pairs={{0,0},{1,16},{2,8},{3,24},{4,4},{5,20},{6,12},{7,28},{8,1},{9,17},... | collective-permute-start | bytes 786440 | tf_op jit(solution)/shard_map/ppermute | solution.py:453
  7.3 0.9 %lists.1 = (s32[4,52]{1,0:T(4,128)S(4)}, s32[4]{0:T(128)S(4)}) custom-call(s32[1]{0:T(128)} %bitcast.2.place_ref, s32[48]{0:T(128)} %bitcast.14, s32[48]{0:T(128)} %bitcast.15, s32[1]{0:T(128)} %bitcast.12.count_ref), custom_call_target="tpu_custom_call" | custom-call | bytes 1048576 | tf_op jit(solution)/shard_map/lists/pallas_call | solution.py:521
  8.3 5.9 %while.26 = (s32[]{:T(128)}, f32[24,256]{1,0:T(8,128)S(1)}, f32[32,256]{1,0:T(8,128)S(1)}, s32[]{:T(128)}, s32[1]{0:T(128)}, /*index=5*/s32[4,52]{1,0:T(4,128)S(...) while((s32[]{:T(128)}, f32[24,256]{1,0:T(8,128)S(1)}, ...), condition=%wide.region_1.2_spmd, body=%wide.region_0.1_spmd.sunk | while | flops 2 | bytes 2195597 | solution.py:497
  8.3 2.0 %edges.1 = (f32[16,256]{1,0:T(8,128)S(1)}, f32[24,256]{1,0:T(8,128)S(1)}) custom-call(s32[1]{0:T(128)} %get-tuple-element.353.place_ref, s32[1]{0:T(128)} %bitcast.10._, s32[4,52]{1,0:T(4,128)S(4)} %get-tuple-element.354.order_ref, s32[4]{0:T(128)S(4)} %get-tuple-element.355.sizes_ref, bf16[48,256,256]{2,1,0:T(8,128)(2,1)} %get-tuple-element.356.tiles_ref, ...), custom_call_target="tpu_custom_call" | custom-call | bytes 1048576 | tf_op jit(solution)/shard_map/while/body/edges/pallas_call | solution.py:537
  10.3 1.7 %collective-permute-start = (f32[24,256]{1,0:T(8,128)S(1)}, f32[24,256]{1,0:T(8,128)S(1)}, u32[]{:S(2)}, u32[]{:S(2)}) collective-permute-start(f32[24,256]{1,0:T(8,128)S(1)} %get-tuple-element.315.refs_0_), channel_id=1, source_target_pairs={{0,4},{1,5},{2,6},{3,7},{4,0},{5,1},{6,2},{7,3},{8,12},{9,13},{10,... | collective-permute-start | bytes 73736 | tf_op jit(solution)/shard_map/while/body/ppermute | solution.py:453
  11.9 2.2 %collective-permute-done.refs_1_ = f32[24,256]{1,0:T(8,128)S(1)} collective-permute-done((f32[24,256]{1,0:T(8,128)S(1)}, f32[24,256]{1,0:T(8,128)S(1)}, u32[]{:S(2)}, u32[]{:S(2)}) %collective-permute-start) | collective-permute-done | bytes 24608 | tf_op jit(solution)/shard_map/while/body/ppermute | solution.py:453
  14.2 1.7 %collective-permute-start.6 = (bf16[512,256]{1,0:T(8,128)(2,1)}, bf16[512,256]{1,0:T(8,128)(2,1)}, u32[]{:S(2)}, u32[]{:S(2)}) collective-permute-start(bf16[512,256]{1,0:T(8,128)(2,1)} %collective-permute-done.4.refs_0_), channel_id=1, source_target_pairs={{0,4},{1,5},{2,6},{3,7},{4,0},{5,1},{6,2},{7,3},{8,12},{9,13},{10,... | collective-permute-start | bytes 786440 | tf_op jit(solution)/shard_map/ppermute | solution.py:453
  15.9 0.4 %collective-permute-start.7 = (bf16[512,256]{1,0:T(8,128)(2,1)}, bf16[512,256]{1,0:T(8,128)(2,1)}, u32[]{:S(2)}, u32[]{:S(2)}) collective-permute-start(bf16[512,256]{1,0:T(8,128)(2,1)} %collective-permute-done.5.refs_1_), channel_id=1, source_target_pairs={{0,4},{1,5},{2,6},{3,7},{4,0},{5,1},{6,2},{7,3},{8,12},{9,13},{10,... | collective-permute-start | bytes 786440 | tf_op jit(solution)/shard_map/ppermute | solution.py:453
  16.3 12.6 %while.27 = (s32[]{:T(128)}, f32[24,256]{1,0:T(8,128)S(1)}, f32[9,128,256]{2,1,0:T(8,128)S(1)}, bf16[16,256,256]{2,1,0:T(8,128)(2,1)S(1)}, s32[]{:T(128)}, /*ind...) while((s32[]{:T(128)}, f32[24,256]{1,0:T(8,128)S(1)}, ...), condition=%wide.region_3.4_spmd, body=%wide.region_2.3_spmd.sunk | while | flops 2 | bytes 3342533 | solution.py:497
  16.4 5.4 %collective-permute-start.1 = (f32[24,256]{1,0:T(8,128)S(1)}, f32[24,256]{1,0:T(8,128)S(1)}, u32[]{:S(2)}, u32[]{:S(2)}) collective-permute-start(f32[24,256]{1,0:T(8,128)S(1)} %get-tuple-element.372.walk_ref), channel_id=1, source_target_pairs={{0,16},{1,17},{2,18},{3,19},{4,20},{5,21},{6,22},{7,23},{8,24},{9,... | collective-permute-start | bytes 73736 | tf_op jit(solution)/shard_map/while/body/ppermute | solution.py:453
  21.7 3.1 %near.1 = (f32[9,128,256]{2,1,0:T(8,128)S(1)}, bf16[16,256,256]{2,1,0:T(8,128)(2,1)S(1)}) custom-call(s32[1]{0:T(128)} %get-tuple-element.388.place_ref, s32[1]{0:T(128)} %bitcast.11._, s32[4,52]{1,0:T(4,128)S(4)} %get-tuple-element.389.order_ref, s32[4]{0:T(128)S(4)} %get-tuple-element.390.sizes_ref, bf16[48,256,256]{2,1,0:T(8,128)(2,1)} %get-tuple-element.391.tiles_ref, ...), custom_call_target="tpu_custom_call" | custom-call | bytes 1048576 | tf_op jit(solution)/shard_map/while/body/near/pallas_call | solution.py:575
  24.8 2.3 %collective-permute-start.2 = (f32[24,256]{1,0:T(8,128)S(1)}, f32[24,256]{1,0:T(8,128)S(1)}, u32[]{:S(2)}, u32[]{:S(2)}) collective-permute-start(f32[24,256]{1,0:T(8,128)S(1)} %z_level.2.walk_ref), channel_id=1, source_target_pairs={{0,8},{1,9},{2,10},{3,11},{4,12},{5,13},{6,14},{7,15},{8,0},{9,1},... | collective-permute-start | bytes 73736 | tf_op jit(solution)/shard_map/while/body/ppermute | solution.py:453
  27.1 1.8 %collective-permute-done.2.partner_ref = f32[24,256]{1,0:T(8,128)S(1)} collective-permute-done((f32[24,256]{1,0:T(8,128)S(1)}, f32[24,256]{1,0:T(8,128)S(1)}, u32[]{:S(2)}, u32[]{:S(2)}) %collective-permute-start.2) | collective-permute-done | bytes 24608 | tf_op jit(solution)/shard_map/while/body/ppermute | solution.py:453
  29.0 2.9 %far.1 = (f32[512,256]{1,0:T(8,128)S(1)}, bf16[528,256]{1,0:T(8,128)(2,1)S(1)}, f32[9,128,256]{2,1,0:T(8,128)S(1)}) custom-call(s32[1]{0:T(128)} %bitcast.2.place_ref, s32[4,52]{1,0:T(4,128)S(4)} %get-tuple-element.365.order_ref, s32[4]{0:T(128)S(4)} %get-tuple-element.366.sizes_ref, ...), custom_call_target="tpu_custom_call", output_to_operand_aliasing={{2}: (4, {})} | custom-call | bytes 1048576 | tf_op jit(solution)/shard_map/far/pallas_call | solution.py:604
  31.8 0.3 collective-permute-start.8
  32.1 1.3 %collective-permute-done.8.arrived_ref = bf16[528,256]{1,0:T(8,128)(2,1)S(1)} collective-permute-done((bf16[528,256]{1,0:T(8,128)(2,1)S(1)}, bf16[528,256]{1,0:T(8,128)(2,1)S(1)}, u32[]{:S(2)}, u32[]{:S(2)}) %collective-permute-start.8) | collective-permute-done | bytes 270368 | tf_op jit(solution)/shard_map/ppermute | solution.py:453
  33.5 3.6 %collective-permute-start.9 = (bf16[288,256]{1,0:T(8,128)(2,1)S(1)}, bf16[288,256]{1,0:T(8,128)(2,1)S(1)}, u32[]{:S(2)}, u32[]{:S(2)}) collective-permute-start(bf16[288,256]{1,0:T(8,128)(2,1)S(1)} %get-tuple-element.160), channel_id=1, source_target_pairs={{0,2},{1,3},{2,0},{3,1},{4,6},{5,7},{6,4},{7,5},{8,10},{9,11},{10,... | collective-permute-start | bytes 442376 | tf_op jit(solution)/shard_map/ppermute | solution.py:453
  37.1 4.1 %collective-permute-done.9.refs_0_ = bf16[288,256]{1,0:T(8,128)(2,1)S(1)} collective-permute-done((bf16[288,256]{1,0:T(8,128)(2,1)S(1)}, bf16[288,256]{1,0:T(8,128)(2,1)S(1)}, u32[]{:S(2)}, u32[]{:S(2)}) %collective-permute-start.9) | collective-permute-done | bytes 147488 | tf_op jit(solution)/shard_map/ppermute | solution.py:453
  41.3 1.3 %back.1 = f32[32,2048]{1,0:T(8,128)} custom-call(s32[1]{0:T(128)} %bitcast.2.place_ref, f32[256,256]{1,0:T(8,128)S(1)} %get-tuple-element.157.own_ref, f32[32,256]{1,0:T(8,128)S(1)} %get-tuple-element.158.both_ref, f32[8,256]{1,0:T(8,128)S(1)} %get-tuple-element.159.firsts_ref, bf16[288,256]{1,0:T(8,128)(2,1)S(1)} %collective-permute-done.9.refs_0_), custom_call_target="tpu_custom_call" | custom-call | bytes 1048576 | tf_op jit(solution)/shard_map/back/pallas_call | solution.py:632
  (11 shorter events, 0.1 us)
Async XLA Ops:
  0.0 1.8 %collective-permute-start.3 = (f32[32,2048]{1,0:T(8,128)}, f32[32,2048]{1,0:T(8,128)S(1)}, u32[]{:S(2)}, u32[]{:S(2)}) collective-permute-start(f32[32,2048]{1,0:T(8,128)} %sources_ref.1), channel_id=1, source_target_pairs={{0,1},{1,0},{2,3},{3,2},{4,5},{5,4},{6,7},{7,6},{8,9},{9,8},{10,11... | collective-permute-start | bytes 786440 | tf_op jit(solution)/shard_map/ppermute | solution.py:453
  2.4 11.9 %collective-permute-start.4 = (bf16[512,256]{1,0:T(8,128)(2,1)S(1)}, bf16[512,256]{1,0:T(8,128)(2,1)}, u32[]{:S(2)}, u32[]{:S(2)}) collective-permute-start(bf16[512,256]{1,0:T(8,128)(2,1)S(1)} %get-tuple-element.143), channel_id=1, source_target_pairs={{0,8},{1,24},{2,0},{3,16},{4,12},{5,28},{6,4},{7,20},{8,9},{9,25},... | collective-permute-start | bytes 786440 | tf_op jit(solution)/shard_map/ppermute | solution.py:453
  5.4 10.5 %collective-permute-start.5 = (bf16[512,256]{1,0:T(8,128)(2,1)S(1)}, bf16[512,256]{1,0:T(8,128)(2,1)}, u32[]{:S(2)}, u32[]{:S(2)}) collective-permute-start(bf16[512,256]{1,0:T(8,128)(2,1)S(1)} %get-tuple-element.143), channel_id=1, source_target_pairs={{0,0},{1,16},{2,8},{3,24},{4,4},{5,20},{6,12},{7,28},{8,1},{9,17},... | collective-permute-start | bytes 786440 | tf_op jit(solution)/shard_map/ppermute | solution.py:453
  10.3 3.9 %collective-permute-start = (f32[24,256]{1,0:T(8,128)S(1)}, f32[24,256]{1,0:T(8,128)S(1)}, u32[]{:S(2)}, u32[]{:S(2)}) collective-permute-start(f32[24,256]{1,0:T(8,128)S(1)} %get-tuple-element.315.refs_0_), channel_id=1, source_target_pairs={{0,4},{1,5},{2,6},{3,7},{4,0},{5,1},{6,2},{7,3},{8,12},{9,13},{10,... | collective-permute-start | bytes 73736 | tf_op jit(solution)/shard_map/while/body/ppermute | solution.py:453
  14.2 14.8 %collective-permute-start.6 = (bf16[512,256]{1,0:T(8,128)(2,1)}, bf16[512,256]{1,0:T(8,128)(2,1)}, u32[]{:S(2)}, u32[]{:S(2)}) collective-permute-start(bf16[512,256]{1,0:T(8,128)(2,1)} %collective-permute-done.4.refs_0_), channel_id=1, source_target_pairs={{0,4},{1,5},{2,6},{3,7},{4,0},{5,1},{6,2},{7,3},{8,12},{9,13},{10,... | collective-permute-start | bytes 786440 | tf_op jit(solution)/shard_map/ppermute | solution.py:453
  15.9 13.1 %collective-permute-start.7 = (bf16[512,256]{1,0:T(8,128)(2,1)}, bf16[512,256]{1,0:T(8,128)(2,1)}, u32[]{:S(2)}, u32[]{:S(2)}) collective-permute-start(bf16[512,256]{1,0:T(8,128)(2,1)} %collective-permute-done.5.refs_1_), channel_id=1, source_target_pairs={{0,4},{1,5},{2,6},{3,7},{4,0},{5,1},{6,2},{7,3},{8,12},{9,13},{10,... | collective-permute-start | bytes 786440 | tf_op jit(solution)/shard_map/ppermute | solution.py:453
  16.4 8.5 %collective-permute-start.1 = (f32[24,256]{1,0:T(8,128)S(1)}, f32[24,256]{1,0:T(8,128)S(1)}, u32[]{:S(2)}, u32[]{:S(2)}) collective-permute-start(f32[24,256]{1,0:T(8,128)S(1)} %get-tuple-element.372.walk_ref), channel_id=1, source_target_pairs={{0,16},{1,17},{2,18},{3,19},{4,20},{5,21},{6,22},{7,23},{8,24},{9,... | collective-permute-start | bytes 73736 | tf_op jit(solution)/shard_map/while/body/ppermute | solution.py:453
  24.8 4.1 %collective-permute-start.2 = (f32[24,256]{1,0:T(8,128)S(1)}, f32[24,256]{1,0:T(8,128)S(1)}, u32[]{:S(2)}, u32[]{:S(2)}) collective-permute-start(f32[24,256]{1,0:T(8,128)S(1)} %z_level.2.walk_ref), channel_id=1, source_target_pairs={{0,8},{1,9},{2,10},{3,11},{4,12},{5,13},{6,14},{7,15},{8,0},{9,1},... | collective-permute-start | bytes 73736 | tf_op jit(solution)/shard_map/while/body/ppermute | solution.py:453
  31.8 1.6 %collective-permute-start.8 = (bf16[528,256]{1,0:T(8,128)(2,1)S(1)}, bf16[528,256]{1,0:T(8,128)(2,1)S(1)}, u32[]{:S(2)}, u32[]{:S(2)}) collective-permute-start(bf16[528,256]{1,0:T(8,128)(2,1)S(1)} %get-tuple-element.156), channel_id=1, source_target_pairs={{0,1},{1,0},{2,3},{3,2},{4,5},{5,4},{6,7},{7,6},{8,9},{9,8},{10,11... | collective-permute-start | bytes 811016 | tf_op jit(solution)/shard_map/ppermute | solution.py:453
  33.5 7.8 %collective-permute-start.9 = (bf16[288,256]{1,0:T(8,128)(2,1)S(1)}, bf16[288,256]{1,0:T(8,128)(2,1)S(1)}, u32[]{:S(2)}, u32[]{:S(2)}) collective-permute-start(bf16[288,256]{1,0:T(8,128)(2,1)S(1)} %get-tuple-element.160), channel_id=1, source_target_pairs={{0,2},{1,3},{2,0},{3,1},{4,6},{5,7},{6,4},{7,5},{8,10},{9,11},{10,... | collective-permute-start | bytes 442376 | tf_op jit(solution)/shard_map/ppermute | solution.py:453

commit v7 on v6

--- a/solution.py
+++ b/solution.py
@@ -11,7 +11,7 @@
 ROOT_HALF = 1.0 / math.sqrt(2.0)
 SIDE_ROWS = 16
 UNROLL = 4
-AHEAD = 16
+AHEAD = 12
 LANES = 128
 MIB = 2**20
 

time: 43.1 us -> 42.2 us (0.979)
  Pallas kernels: 11.7 us -> 11.2 us
    pallas_call x1, Pallas kernels: 2.85 us -> 1.82 us  [local(): call(far_kernel, 'far', [f32(spans * part, extent), bf16(spans * part + l...]
  transfers between devices with their start and end apart: 10 -> 10, of which waited for: 5 -> 6; matrix products, arithmetic and copies ran while one was open for 0% -> 0% of each run, Pallas kernels for 16% -> 18%
where the time goes in v7:
time: 42.2 us; the launch traced here: 41.5 us
  starting transfers between devices  19.9 us (47%)
  Pallas kernels  11.2 us (27%)
  waiting for transfers between devices  9.53 us (23%)
  between operations  0.78 us (2%)
    ppermute x10, starting transfers between devices, moved(): return lax.ppermute(value, ('row', 'col'), pairs)  19.9 us
    ppermute x10, waiting for transfers between devices, moved(): return lax.ppermute(value, ('row', 'col'), pairs)  9.53 us
    pallas_call x1, Pallas kernels, late(): call(near_kernel, 'near', later, [smem] * 4 + [hbm] + [vmem] * len(direct...  3.49 us
    pallas_call x1, Pallas kernels, early(): call(edge_kernel, 'edges', [f32(length, extent), f32(length + gathered, e...  1.96 us
    pallas_call x1, Pallas kernels, local(): call(far_kernel, 'far', [f32(spans * part, extent), bf16(spans * part + l...  1.82 us
    pallas_call x1, Pallas kernels, local(): call(back_kernel, 'back', f32(*sources.shape), [smem] + [vmem] * (2 + spa...  1.28 us
    pallas_call x1, Pallas kernels, local(): call(list_kernel, 'lists', [pltpu.SMEM((4, slots + UNROLL), jnp.int32), p...  1.1 us
    pallas_call x1, Pallas kernels, local(): call(prepare_kernel, 'prepare', [kept(*sources.shape), kept(length + gath...  0.96 us
  transfers between devices with their start and end apart: 10, of which 6 were waited for; matrix products, arithmetic and copies ran while one was open for 0% of the time, Pallas kernels for 18%

profile of v7, /device:TPU:0, one launch (start us, length us, event | category | flops | bytes accessed | tf_op | source)
XLA Modules:
  0.0 41.5 jit_solution(2207837793256622798)
XLA Ops:
  0.0 0.5 %collective-permute-start.3 = (f32[32,2048]{1,0:T(8,128)}, f32[32,2048]{1,0:T(8,128)S(1)}, u32[]{:S(2)}, u32[]{:S(2)}) collective-permute-start(f32[32,2048]{1,0:T(8,128)} %sources_ref.1), channel_id=1, source_target_pairs={{0,1},{1,0},{2,3},{3,2},{4,5},{5,4},{6,7},{7,6},{8,9},{9,8},{10,11... | collective-permute-start | bytes 786440 | tf_op jit(solution)/shard_map/ppermute | solution.py:453
  0.5 1.0 %prepare.1 = (f32[32,2048]{1,0:T(8,128)S(1)}, f32[24,256]{1,0:T(8,128)S(1)}, f32[32,256]{1,0:T(8,128)S(1)}) custom-call(f32[32,2048]{1,0:T(8,128)} %sources_ref.1), custom_call_target="tpu_custom_call" | custom-call | bytes 1048576 | tf_op jit(solution)/shard_map/prepare/pallas_call | solution.py:504
  1.5 0.4 collective-permute-done.3.other_ref
  1.8 0.5 %front.1 = (bf16[512,256]{1,0:T(8,128)(2,1)S(1)}, f32[8,256]{1,0:T(8,128)S(1)}) custom-call(s32[1]{0:T(128)} %bitcast.2.place_ref, f32[32,2048]{1,0:T(8,128)S(1)} %get-tuple-element.140.mine_ref, f32[32,2048]{1,0:T(8,128)S(1)} %collective-permute-done.3.other_ref), custom_call_target="tpu_custom_call" | custom-call | bytes 1048576 | tf_op jit(solution)/shard_map/front/pallas_call | solution.py:512
  2.4 3.0 %collective-permute-start.4 = (bf16[512,256]{1,0:T(8,128)(2,1)S(1)}, bf16[512,256]{1,0:T(8,128)(2,1)}, u32[]{:S(2)}, u32[]{:S(2)}) collective-permute-start(bf16[512,256]{1,0:T(8,128)(2,1)S(1)} %get-tuple-element.143), channel_id=1, source_target_pairs={{0,8},{1,24},{2,0},{3,16},{4,12},{5,28},{6,4},{7,20},{8,9},{9,25},... | collective-permute-start | bytes 786440 | tf_op jit(solution)/shard_map/ppermute | solution.py:453
  5.4 1.3 %collective-permute-start.5 = (bf16[512,256]{1,0:T(8,128)(2,1)S(1)}, bf16[512,256]{1,0:T(8,128)(2,1)}, u32[]{:S(2)}, u32[]{:S(2)}) collective-permute-start(bf16[512,256]{1,0:T(8,128)(2,1)S(1)} %get-tuple-element.143), channel_id=1, source_target_pairs={{0,0},{1,16},{2,8},{3,24},{4,4},{5,20},{6,12},{7,28},{8,1},{9,17},... | collective-permute-start | bytes 786440 | tf_op jit(solution)/shard_map/ppermute | solution.py:453
  7.3 1.1 %lists.1 = (s32[4,52]{1,0:T(4,128)S(4)}, s32[4]{0:T(128)S(4)}) custom-call(s32[1]{0:T(128)} %bitcast.2.place_ref, s32[48]{0:T(128)} %bitcast.14, s32[48]{0:T(128)} %bitcast.15, s32[1]{0:T(128)} %bitcast.12.count_ref), custom_call_target="tpu_custom_call" | custom-call | bytes 1048576 | tf_op jit(solution)/shard_map/lists/pallas_call | solution.py:521
  8.5 6.5 %while.26 = (s32[]{:T(128)}, f32[24,256]{1,0:T(8,128)S(1)}, f32[32,256]{1,0:T(8,128)S(1)}, s32[]{:T(128)}, s32[1]{0:T(128)}, /*index=5*/s32[4,52]{1,0:T(4,128)S(...) while((s32[]{:T(128)}, f32[24,256]{1,0:T(8,128)S(1)}, ...), condition=%wide.region_1.2_spmd, body=%wide.region_0.1_spmd.sunk | while | flops 2 | bytes 2195597 | solution.py:497
  8.5 2.0 %edges.1 = (f32[16,256]{1,0:T(8,128)S(1)}, f32[24,256]{1,0:T(8,128)S(1)}) custom-call(s32[1]{0:T(128)} %get-tuple-element.353.place_ref, s32[1]{0:T(128)} %bitcast.10._, s32[4,52]{1,0:T(4,128)S(4)} %get-tuple-element.354.order_ref, s32[4]{0:T(128)S(4)} %get-tuple-element.355.sizes_ref, bf16[48,256,256]{2,1,0:T(8,128)(2,1)} %get-tuple-element.356.tiles_ref, ...), custom_call_target="tpu_custom_call" | custom-call | bytes 1048576 | tf_op jit(solution)/shard_map/while/body/edges/pallas_call | solution.py:537
  10.4 2.7 %collective-permute-start = (f32[24,256]{1,0:T(8,128)S(1)}, f32[24,256]{1,0:T(8,128)S(1)}, u32[]{:S(2)}, u32[]{:S(2)}) collective-permute-start(f32[24,256]{1,0:T(8,128)S(1)} %get-tuple-element.315.refs_0_), channel_id=1, source_target_pairs={{0,4},{1,5},{2,6},{3,7},{4,0},{5,1},{6,2},{7,3},{8,12},{9,13},{10,... | collective-permute-start | bytes 73736 | tf_op jit(solution)/shard_map/while/body/ppermute | solution.py:453
  13.1 1.8 %collective-permute-done.refs_1_ = f32[24,256]{1,0:T(8,128)S(1)} collective-permute-done((f32[24,256]{1,0:T(8,128)S(1)}, f32[24,256]{1,0:T(8,128)S(1)}, u32[]{:S(2)}, u32[]{:S(2)}) %collective-permute-start) | collective-permute-done | bytes 24608 | tf_op jit(solution)/shard_map/while/body/ppermute | solution.py:453
  15.0 2.1 %collective-permute-start.6 = (bf16[512,256]{1,0:T(8,128)(2,1)}, bf16[512,256]{1,0:T(8,128)(2,1)S(1)}, u32[]{:S(2)}, u32[]{:S(2)}) collective-permute-start(bf16[512,256]{1,0:T(8,128)(2,1)} %collective-permute-done.4.refs_0_), channel_id=1, source_target_pairs={{0,4},{1,5},{2,6},{3,7},{4,0},{5,1},{6,2},{7,3},{8,12},{9,13},{10,... | collective-permute-start | bytes 786440 | tf_op jit(solution)/shard_map/ppermute | solution.py:453
  17.2 12.3 %while.27 = (s32[]{:T(128)}, f32[24,256]{1,0:T(8,128)S(1)}, f32[9,128,256]{2,1,0:T(8,128)S(1)}, bf16[12,256,256]{2,1,0:T(8,128)(2,1)S(1)}, s32[]{:T(128)}, /*ind...) while((s32[]{:T(128)}, f32[24,256]{1,0:T(8,128)S(1)}, ...), condition=%wide.region_3.4_spmd, body=%wide.region_2.3_spmd.sunk | while | flops 2 | bytes 3342533 | solution.py:497
  17.2 4.6 %collective-permute-start.1 = (f32[24,256]{1,0:T(8,128)S(1)}, f32[24,256]{1,0:T(8,128)S(1)}, u32[]{:S(2)}, u32[]{:S(2)}) collective-permute-start(f32[24,256]{1,0:T(8,128)S(1)} %get-tuple-element.372.walk_ref), channel_id=1, source_target_pairs={{0,16},{1,17},{2,18},{3,19},{4,20},{5,21},{6,22},{7,23},{8,24},{9,... | collective-permute-start | bytes 73736 | tf_op jit(solution)/shard_map/while/body/ppermute | solution.py:453
  21.7 3.5 %near.1 = (f32[9,128,256]{2,1,0:T(8,128)S(1)}, bf16[12,256,256]{2,1,0:T(8,128)(2,1)S(1)}) custom-call(s32[1]{0:T(128)} %get-tuple-element.388.place_ref, s32[1]{0:T(128)} %bitcast.11._, s32[4,52]{1,0:T(4,128)S(4)} %get-tuple-element.389.order_ref, s32[4]{0:T(128)S(4)} %get-tuple-element.390.sizes_ref, bf16[48,256,256]{2,1,0:T(8,128)(2,1)} %get-tuple-element.391.tiles_ref, ...), custom_call_target="tpu_custom_call" | custom-call | bytes 1048576 | tf_op jit(solution)/shard_map/while/body/near/pallas_call | solution.py:575
  25.3 2.4 %collective-permute-start.2 = (f32[24,256]{1,0:T(8,128)S(1)}, f32[24,256]{1,0:T(8,128)S(1)}, u32[]{:S(2)}, u32[]{:S(2)}) collective-permute-start(f32[24,256]{1,0:T(8,128)S(1)} %z_level.2.walk_ref), channel_id=1, source_target_pairs={{0,8},{1,9},{2,10},{3,11},{4,12},{5,13},{6,14},{7,15},{8,0},{9,1},... | collective-permute-start | bytes 73736 | tf_op jit(solution)/shard_map/while/body/ppermute | solution.py:453
  27.7 1.8 %collective-permute-done.2.partner_ref = f32[24,256]{1,0:T(8,128)S(1)} collective-permute-done((f32[24,256]{1,0:T(8,128)S(1)}, f32[24,256]{1,0:T(8,128)S(1)}, u32[]{:S(2)}, u32[]{:S(2)}) %collective-permute-start.2) | collective-permute-done | bytes 24608 | tf_op jit(solution)/shard_map/while/body/ppermute | solution.py:453
  29.5 0.1 collective-permute-done.7.refs_3_
  29.6 1.8 %far.1 = (f32[512,256]{1,0:T(8,128)S(1)}, bf16[528,256]{1,0:T(8,128)(2,1)S(1)}, f32[9,128,256]{2,1,0:T(8,128)S(1)}) custom-call(s32[1]{0:T(128)} %bitcast.2.place_ref, s32[4,52]{1,0:T(4,128)S(4)} %get-tuple-element.365.order_ref, s32[4]{0:T(128)S(4)} %get-tuple-element.366.sizes_ref, ...), custom_call_target="tpu_custom_call", output_to_operand_aliasing={{2}: (4, {})} | custom-call | bytes 1048576 | tf_op jit(solution)/shard_map/far/pallas_call | solution.py:604
  31.4 0.3 collective-permute-start.8
  31.8 1.3 %collective-permute-done.8.arrived_ref = bf16[528,256]{1,0:T(8,128)(2,1)S(1)} collective-permute-done((bf16[528,256]{1,0:T(8,128)(2,1)S(1)}, bf16[528,256]{1,0:T(8,128)(2,1)S(1)}, u32[]{:S(2)}, u32[]{:S(2)}) %collective-permute-start.8) | collective-permute-done | bytes 270368 | tf_op jit(solution)/shard_map/ppermute | solution.py:453
  33.1 3.0 %collective-permute-start.9 = (bf16[288,256]{1,0:T(8,128)(2,1)S(1)}, bf16[288,256]{1,0:T(8,128)(2,1)S(1)}, u32[]{:S(2)}, u32[]{:S(2)}) collective-permute-start(bf16[288,256]{1,0:T(8,128)(2,1)S(1)} %get-tuple-element.160), channel_id=1, source_target_pairs={{0,2},{1,3},{2,0},{3,1},{4,6},{5,7},{6,4},{7,5},{8,10},{9,11},{10,... | collective-permute-start | bytes 442376 | tf_op jit(solution)/shard_map/ppermute | solution.py:453
  36.1 4.1 %collective-permute-done.9.refs_0_ = bf16[288,256]{1,0:T(8,128)(2,1)S(1)} collective-permute-done((bf16[288,256]{1,0:T(8,128)(2,1)S(1)}, bf16[288,256]{1,0:T(8,128)(2,1)S(1)}, u32[]{:S(2)}, u32[]{:S(2)}) %collective-permute-start.9) | collective-permute-done | bytes 147488 | tf_op jit(solution)/shard_map/ppermute | solution.py:453
  40.2 1.3 %back.1 = f32[32,2048]{1,0:T(8,128)} custom-call(s32[1]{0:T(128)} %bitcast.2.place_ref, f32[256,256]{1,0:T(8,128)S(1)} %get-tuple-element.157.own_ref, f32[32,256]{1,0:T(8,128)S(1)} %get-tuple-element.158.both_ref, f32[8,256]{1,0:T(8,128)S(1)} %get-tuple-element.159.firsts_ref, bf16[288,256]{1,0:T(8,128)(2,1)S(1)} %collective-permute-done.9.refs_0_), custom_call_target="tpu_custom_call" | custom-call | bytes 1048576 | tf_op jit(solution)/shard_map/back/pallas_call | solution.py:632
  (11 shorter events, 0.2 us)
Async XLA Ops:
  0.0 1.8 %collective-permute-start.3 = (f32[32,2048]{1,0:T(8,128)}, f32[32,2048]{1,0:T(8,128)S(1)}, u32[]{:S(2)}, u32[]{:S(2)}) collective-permute-start(f32[32,2048]{1,0:T(8,128)} %sources_ref.1), channel_id=1, source_target_pairs={{0,1},{1,0},{2,3},{3,2},{4,5},{5,4},{6,7},{7,6},{8,9},{9,8},{10,11... | collective-permute-start | bytes 786440 | tf_op jit(solution)/shard_map/ppermute | solution.py:453
  2.4 12.6 %collective-permute-start.4 = (bf16[512,256]{1,0:T(8,128)(2,1)S(1)}, bf16[512,256]{1,0:T(8,128)(2,1)}, u32[]{:S(2)}, u32[]{:S(2)}) collective-permute-start(bf16[512,256]{1,0:T(8,128)(2,1)S(1)} %get-tuple-element.143), channel_id=1, source_target_pairs={{0,8},{1,24},{2,0},{3,16},{4,12},{5,28},{6,4},{7,20},{8,9},{9,25},... | collective-permute-start | bytes 786440 | tf_op jit(solution)/shard_map/ppermute | solution.py:453
  5.4 11.7 %collective-permute-start.5 = (bf16[512,256]{1,0:T(8,128)(2,1)S(1)}, bf16[512,256]{1,0:T(8,128)(2,1)}, u32[]{:S(2)}, u32[]{:S(2)}) collective-permute-start(bf16[512,256]{1,0:T(8,128)(2,1)S(1)} %get-tuple-element.143), channel_id=1, source_target_pairs={{0,0},{1,16},{2,8},{3,24},{4,4},{5,20},{6,12},{7,28},{8,1},{9,17},... | collective-permute-start | bytes 786440 | tf_op jit(solution)/shard_map/ppermute | solution.py:453
  10.4 4.5 %collective-permute-start = (f32[24,256]{1,0:T(8,128)S(1)}, f32[24,256]{1,0:T(8,128)S(1)}, u32[]{:S(2)}, u32[]{:S(2)}) collective-permute-start(f32[24,256]{1,0:T(8,128)S(1)} %get-tuple-element.315.refs_0_), channel_id=1, source_target_pairs={{0,4},{1,5},{2,6},{3,7},{4,0},{5,1},{6,2},{7,3},{8,12},{9,13},{10,... | collective-permute-start | bytes 73736 | tf_op jit(solution)/shard_map/while/body/ppermute | solution.py:453
  15.0 14.5 %collective-permute-start.6 = (bf16[512,256]{1,0:T(8,128)(2,1)}, bf16[512,256]{1,0:T(8,128)(2,1)S(1)}, u32[]{:S(2)}, u32[]{:S(2)}) collective-permute-start(bf16[512,256]{1,0:T(8,128)(2,1)} %collective-permute-done.4.refs_0_), channel_id=1, source_target_pairs={{0,4},{1,5},{2,6},{3,7},{4,0},{5,1},{6,2},{7,3},{8,12},{9,13},{10,... | collective-permute-start | bytes 786440 | tf_op jit(solution)/shard_map/ppermute | solution.py:453
  17.1 12.6 %collective-permute-start.7 = (bf16[512,256]{1,0:T(8,128)(2,1)}, bf16[512,256]{1,0:T(8,128)(2,1)S(1)}, u32[]{:S(2)}, u32[]{:S(2)}) collective-permute-start(bf16[512,256]{1,0:T(8,128)(2,1)} %collective-permute-done.5.refs_1_), channel_id=1, source_target_pairs={{0,4},{1,5},{2,6},{3,7},{4,0},{5,1},{6,2},{7,3},{8,12},{9,13},{10,... | collective-permute-start | bytes 786440 | tf_op jit(solution)/shard_map/ppermute | solution.py:453
  17.2 8.0 %collective-permute-start.1 = (f32[24,256]{1,0:T(8,128)S(1)}, f32[24,256]{1,0:T(8,128)S(1)}, u32[]{:S(2)}, u32[]{:S(2)}) collective-permute-start(f32[24,256]{1,0:T(8,128)S(1)} %get-tuple-element.372.walk_ref), channel_id=1, source_target_pairs={{0,16},{1,17},{2,18},{3,19},{4,20},{5,21},{6,22},{7,23},{8,24},{9,... | collective-permute-start | bytes 73736 | tf_op jit(solution)/shard_map/while/body/ppermute | solution.py:453
  25.3 4.2 %collective-permute-start.2 = (f32[24,256]{1,0:T(8,128)S(1)}, f32[24,256]{1,0:T(8,128)S(1)}, u32[]{:S(2)}, u32[]{:S(2)}) collective-permute-start(f32[24,256]{1,0:T(8,128)S(1)} %z_level.2.walk_ref), channel_id=1, source_target_pairs={{0,8},{1,9},{2,10},{3,11},{4,12},{5,13},{6,14},{7,15},{8,0},{9,1},... | collective-permute-start | bytes 73736 | tf_op jit(solution)/shard_map/while/body/ppermute | solution.py:453
  31.4 1.6 %collective-permute-start.8 = (bf16[528,256]{1,0:T(8,128)(2,1)S(1)}, bf16[528,256]{1,0:T(8,128)(2,1)S(1)}, u32[]{:S(2)}, u32[]{:S(2)}) collective-permute-start(bf16[528,256]{1,0:T(8,128)(2,1)S(1)} %get-tuple-element.156), channel_id=1, source_target_pairs={{0,1},{1,0},{2,3},{3,2},{4,5},{5,4},{6,7},{7,6},{8,9},{9,8},{10,11... | collective-permute-start | bytes 811016 | tf_op jit(solution)/shard_map/ppermute | solution.py:453
  33.1 7.1 %collective-permute-start.9 = (bf16[288,256]{1,0:T(8,128)(2,1)S(1)}, bf16[288,256]{1,0:T(8,128)(2,1)S(1)}, u32[]{:S(2)}, u32[]{:S(2)}) collective-permute-start(bf16[288,256]{1,0:T(8,128)(2,1)S(1)} %get-tuple-element.160), channel_id=1, source_target_pairs={{0,2},{1,3},{2,0},{3,1},{4,6},{5,7},{6,4},{7,5},{8,10},{9,11},{10,... | collective-permute-start | bytes 442376 | tf_op jit(solution)/shard_map/ppermute | solution.py:453
